TPU v7x, 512 devices: a whole 4x4x16 slice. The times are simulated.
512 devices in a mesh: gx: 4 (over y), gy: 8 (over x, core), gz: 16 (over z).
Axes of the slice: x: 4, y: 4, z: 16, core: 2. Of those that a mesh axis runs over, the one named last changes fastest.
Arguments:
- resid: bfloat16 [2, 64, 18432], P(None, None, ('gx', 'gy', 'gz')), may hold values from -6 to 6
- query: bfloat16 [2, 64, 12288], P(None, None, 'gz'), may hold values from -6 to 6
- new_kv: bfloat16 [2, 64, 512], P(None, 'gz'), may hold values from -6 to 6
- key_cache: bfloat16 [64, 4096, 256], P('gz', ('gx', 'gy')), may hold values from -4 to 4
- value_cache: bfloat16 [64, 4096, 256], P('gz', ('gx', 'gy')), may hold values from -6 to 6
- lengths: int32 [64], P('gz'), may hold values from 1024 to 4096, as said below
- out_weight: bfloat16 [12288, 18432], P(('gy', 'gz'), 'gx'), may hold values from -0.21875 to 0.21875
- hidden: bfloat16 [2, 64, 36864], P(None, 'gx', ('gy', 'gz')), may hold values from -6 to 6
- down_weight: bfloat16 [36864, 18432], P(('gy', 'gz'), 'gx'), may hold values from -0.125 to 0.125
Outputs:
- layer_out: bfloat16 [2, 64, 18432], P(None, None, ('gx', 'gy', 'gz'))
Inputs may be any that keep to these rules, and one draw needn't show every extreme that they name: Transcript b attends to cache positions below lengths[b]; some transcript's length is 4096 in every draw.
All inputs are finite; a program needn't handle non-finite values.
Results may differ from a plain program's by a relative error of at most 0.0034.
Values may be sent and summed in bfloat16 or wider, within the bound.
No kernel may reach another device: no remote copies, remote signals or barrier semaphores. Data moves between devices by JAX's collectives and lax.ppermute only.
A program may use at most 64 MiB of HBM per device.

v0:
```python
import jax
import jax.numpy as jnp
from jax import lax
from jax.sharding import PartitionSpec as P

HEADS = 48
HD = 256


def per_device(
    resid, query, new_kv, key_cache, value_cache, lengths, out_weight, hidden, down_weight
):
    local_q = lax.all_to_all(query, "gz", split_axis=1, concat_axis=2, tiled=True)
    groups = local_q.shape[1]
    qf = local_q.reshape(2, groups, HEADS, HD)
    scale = HD ** (-0.5)
    span = key_cache.shape[1]
    positions = lax.axis_index(("gx", "gy")) * span + jnp.arange(span, dtype=jnp.int32)
    position_is_present = positions[None, :] < lengths[:, None]
    present_position_mask = position_is_present[None, :, None, :]
    cached_score_rows = (
        jnp.einsum("tbhd,bpd->tbhp", qf, key_cache, preferred_element_type=jnp.float32) * scale
    )
    cached_score_rows = jnp.where(present_position_mask, cached_score_rows, -1e30)
    fresh_k = new_kv[..., :HD]
    incoming_value = new_kv[..., HD:]
    allowed = jnp.arange(2)[None, :] <= jnp.arange(2)[:, None]
    amask = allowed[:, None, None, :]
    new_scores = (
        jnp.einsum("tbhd,ubd->tbhu", qf, fresh_k, preferred_element_type=jnp.float32) * scale
    )
    new_scores = jnp.where(amask, new_scores, -1e30)
    device_score_maximum = jnp.maximum(jnp.max(cached_score_rows, -1), jnp.max(new_scores, -1))
    global_score_maximum = lax.pmax(device_score_maximum, ("gx", "gy"))
    cached_attention_weight = jnp.where(
        present_position_mask, jnp.exp(cached_score_rows - global_score_maximum[..., None]), 0.0
    ).astype(jnp.bfloat16)
    part_total = jnp.sum(cached_attention_weight.astype(jnp.float32), -1)
    part_acc = jnp.einsum(
        "tbhp,bpd->tbhd", cached_attention_weight, value_cache, preferred_element_type=jnp.float32
    )
    total, acc = lax.psum((part_total, part_acc), ("gx", "gy"))
    new_w = jnp.where(amask, jnp.exp(new_scores - global_score_maximum[..., None]), 0.0).astype(
        jnp.bfloat16
    )
    total = total + jnp.sum(new_w.astype(jnp.float32), -1)
    acc = acc + jnp.einsum(
        "tbhu,ubd->tbhd", new_w, incoming_value, preferred_element_type=jnp.float32
    )
    attn = (acc / total[..., None]).astype(jnp.bfloat16).reshape(2, groups, HEADS * HD)
    width = out_weight.shape[0]
    every = lax.all_gather(attn, "gz", axis=1, tiled=True)
    block = lax.axis_index(("gy", "gz"))
    mine = lax.dynamic_slice_in_dim(every, block * width, width, 2)
    projected = jnp.einsum("tbr,rc->tbc", mine, out_weight, preferred_element_type=jnp.float32)
    feed = jnp.einsum(
        "tbf,fc->tbc",
        lax.all_gather(hidden, "gx", axis=1, tiled=True),
        down_weight,
        preferred_element_type=jnp.float32,
    )
    partial_sum = projected + feed
    summed = lax.psum_scatter(partial_sum, ("gy", "gz"), scatter_dimension=2, tiled=True)
    return (summed + resid.astype(jnp.float32)).astype(jnp.bfloat16)


def solution(mesh):
    in_specs = (
        P(None, None, ("gx", "gy", "gz")),
        P(None, None, "gz"),
        P(None, "gz", None),
        P("gz", ("gx", "gy"), None),
        P("gz", ("gx", "gy"), None),
        P("gz"),
        P(("gy", "gz"), "gx"),
        P(None, "gx", ("gy", "gz")),
        P(("gy", "gz"), "gx"),
    )
    out_specs = P(None, None, ("gx", "gy", "gz"))
    return jax.shard_map(
        per_device, mesh=mesh, in_specs=in_specs, out_specs=out_specs, check_vma=False
    )
```

profile of v0, /device:TPU:24, one launch (start us, length us, event | category | flops | bytes accessed | tf_op | source)
XLA Modules:
  0.0 763.2 jit_solution(16574520534614404974)
XLA Ops:
  6.5 2.0 copy.16
  8.5 15.2 %all-to-all-start = ((bf16[2,64,768]{2,0,1:T(2,128)(2,1)}), bf16[2,64,768]{2,0,1:T(2,128)(2,1)S(1)}, u32[]{:S(2)}, u32[]{:S(2)}) async-start(bf16[2,64,768]{2,0,1:T(2,128)(2,1)} %copy.16), calls=%async_computation | async-start | bytes 393216 | tf_op jit(solution)/shard_map/all_to_all | solution.py:13
  23.7 0.0 all-reduce.4.cloned.1.call-start
  23.8 0.7 broadcast_compare_fusion
  24.5 0.7 fusion.15
  25.2 14.9 %all-to-all-done = bf16[2,64,768]{2,0,1:T(2,128)(2,1)S(1)} async-done(((bf16[2,64,768]{2,0,1:T(2,128)(2,1)}), bf16[2,64,768]{2,0,1:T(2,128)(2,1)S(1)}, u32[]{:S(2)}, u32[]{:S(2)}) %all-to-all-start) | async-done | bytes 196640 | tf_op jit(solution)/shard_map/all_to_all | solution.py:13
  40.2 0.1 reshape.50
  40.3 1.3 fusion.16
  41.5 0.2 fusion.17
  41.8 53.0 %pmax.7 = f32[2,4,48]{2,0,1:T(2,128)S(1)} all-reduce(f32[2,4,48]{2,0,1:T(2,128)S(1)} %max.5), channel_id=1, replica_groups=mesh['gx'=4,'gy'=8,'gz'=16] {'gx','gy'}, use_global_device_ids=true, to_apply=%region_2.3 | all-reduce | flops 384 | bytes 3072 | tf_op jit(solution)/shard_map/pmax | solution.py:34
  94.8 0.2 convert_reduce_fusion
  95.0 54.6 %psum.15 = f32[2,4,48]{2,0,1:T(2,128)S(1)} all-reduce(f32[2,4,48]{2,0,1:T(2,128)S(1)} %convert_reduce_fusion), channel_id=1, replica_groups=mesh['gx'=4,'gy'=8,'gz'=16] {'gx','gy'}, use_global_device_ids=true, to_apply=%region_5.6 | all-reduce | flops 384 | bytes 3072 | tf_op jit(solution)/shard_map/psum | solution.py:42
  149.7 2.0 convolution_bitcast_fusion.1
  151.6 0.0 all-reduce.4.cloned.1.call-update
  151.7 0.0 all-gather.2.cloned.1.call-start
  151.7 0.1 convert_reduce_fusion.1
  151.8 144.7 %all-reduce.4.cloned.1.call-done = f32[2,4,48,256]{3,2,0,1:T(8,128)} async-done(((f32[2,4,48,256]{3,2,0,1:T(8,128)}), f32[2,4,48,256]{3,2,0,1:T(8,128)}) %all-reduce.4.cloned.1.call-update) | async-done | bytes 393232 | tf_op jit(solution)/shard_map/psum | solution.py:42
  296.5 1.2 fusion.3
  297.8 0.7 reshape.51
  298.5 0.0 all-gather.2.cloned.1.call-update
  298.5 0.0 all-reduce.6.cloned.1.call-start
  298.6 12.0 %all_gather.7 = bf16[2,64,288]{2,1,0:T(8,128)(2,1)S(1)} all-gather(bf16[2,16,288]{2,1,0:T(8,128)(2,1)S(1)} %copy-done.1), channel_id=1, replica_groups=mesh['gx'=4,'gy'=8,'gz'=16] {'gx'}, dimensions={1}, use_global_device_ids=true | all-gather | bytes 92160 | tf_op jit(solution)/shard_map/all_gather | solution.py:58
  310.5 63.8 %all-gather.2.cloned.1.call-done = bf16[2,64,12288]{2,0,1:T(2,128)(2,1)} async-done(((bf16[2,4,12288]{2,0,1:T(2,128)(2,1)}), bf16[2,64,12288]{2,0,1:T(2,128)(2,1)}) %all-gather.2.cloned.1.call-update) | async-done | bytes 3145744 | tf_op jit(solution)/shard_map/all_gather | solution.py:52
  374.3 0.9 constant_dynamic-slice_fusion
  375.2 2.0 fusion.8
  377.2 1.7 convolution_add_fusion
  379.0 18.1 %copy.21 = f32[2,64,4608]{1,0,2:T(2,128)} copy(f32[2,64,4608]{1,2,0:T(8,128)S(1)} %convolution_add_fusion) | data formatting | bytes 4718592 | tf_op jit(solution)/shard_map/add | solution.py:62
  397.1 0.0 all-reduce.6.cloned.1.call-update
  397.1 1.3 dynamic-slice
  399.0 356.2 %all-reduce.6.cloned.1.call-done = f32[2,64,4608]{1,0,2:T(2,128)} async-done(((f32[2,64,4608]{1,0,2:T(2,128)}), f32[2,64,4608]{1,0,2:T(2,128)}) %all-reduce.6.cloned.1.call-update) | async-done | bytes 2359312
  755.3 0.0 copy-done.2
  755.3 1.4 fusion.12
  (10 shorter events, 0.1 us)
Async XLA Ops:
  6.5 370.7 %copy-start = (bf16[288,4608]{1,0:T(8,128)(2,1)S(1)}, bf16[288,4608]{1,0:T(8,128)(2,1)}, u32[]{:S(2)}) copy-start(bf16[288,4608]{1,0:T(8,128)(2,1)} %param.17) | copy-start | bytes 7962628
  6.5 292.0 %copy-start.1 = (bf16[2,16,288]{2,1,0:T(8,128)(2,1)S(1)}, bf16[2,16,288]{2,1,0:T(8,128)(2,1)}, u32[]{:S(2)}) copy-start(bf16[2,16,288]{2,1,0:T(8,128)(2,1)} %param.16) | copy-start | bytes 55300
  8.5 31.6 %all-to-all-start = ((bf16[2,64,768]{2,0,1:T(2,128)(2,1)}), bf16[2,64,768]{2,0,1:T(2,128)(2,1)S(1)}, u32[]{:S(2)}, u32[]{:S(2)}) async-start(bf16[2,64,768]{2,0,1:T(2,128)(2,1)} %copy.16), calls=%async_computation | async-start | bytes 393216 | tf_op jit(solution)/shard_map/all_to_all | solution.py:13
  23.7 272.8 %all-reduce.4.cloned.1.call-start = ((), (), s32[]{:S(2)}) async-start(), calls=%async_computation.1 | async-start | bytes 786432 | tf_op jit(solution)/shard_map/psum | solution.py:42
  151.7 222.6 %all-gather.2.cloned.1.call-start = ((), (), s32[]{:S(2)}) async-start(), calls=%async_computation.2 | async-start | bytes 3342336 | tf_op jit(solution)/shard_map/all_gather | solution.py:52
  298.5 456.8 %all-reduce.6.cloned.1.call-start = ((), (), s32[]{:S(2)}) async-start(), calls=%async_computation.3 | async-start | bytes 9437184
  397.1 358.2 %copy-start.2 = (bf16[2,64,36]{1,0,2:T(2,128)(2,1)S(1)}, bf16[2,64,36]{1,0,2:T(2,128)(2,1)}, u32[]{:S(2)}) copy-start(bf16[2,64,36]{1,0,2:T(2,128)(2,1)} %param.9) | copy-start | bytes 27652
Sparse Core Ops, SparseCore 0:
  151.8 144.6 all-reduce.3
  298.6 75.6 all-gather.1
  397.2 357.9 all-reduce.5
where the time goes:
time: 764 us; the launch traced here: 763 us
  waiting for transfers between devices  580 us (76%)
  blocking collectives  120 us (16%)
  local copies, waits for them, and re-layouts  23.8 us (3%)
  starting transfers between devices  15.3 us (2%)
  between operations  13.9 us (2%)
  matrix products  8.43 us (1%)
    unnamed x4, waiting for transfers between devices  356 us
    psum x1, waiting for transfers between devices, per_device(): total, acc = lax.psum((part_total, part_acc), ('gx', 'gy'))  145 us
    all_gather x1, waiting for transfers between devices, per_device(): every = lax.all_gather(attn, 'gz', axis=1, tiled=True)  63.8 us
    psum x1, blocking collectives, per_device(): total, acc = lax.psum((part_total, part_acc), ('gx', 'gy'))  54.6 us
    pmax x1, blocking collectives, per_device(): global_score_maximum = lax.pmax(device_score_maximum, ('gx', 'gy'))  53 us
    add x1, local copies, waits for them, and re-layouts, per_device(): partial_sum = projected + feed  18.1 us
  transfers between devices with their start and end apart: 4, of which 4 were waited for; matrix products, arithmetic and copies ran while one was open for 0% of the time, Pallas kernels for 0%

commit v1 on v0

v1 whole, which is shorter than its diff:
```python
import jax
import jax.numpy as jnp
from jax import lax
from jax.sharding import Mesh
from jax.sharding import PartitionSpec as P

HEADS = 48
HD = 256
F32 = jnp.float32
BF16 = jnp.bfloat16
GY = ("gyx", "core")
NEG = -1e30


def per_device(
    resid, query, new_kv, key_cache, value_cache, lengths, out_weight, hidden, down_weight
):
    q = query.reshape(2, 16, 4, 768).transpose(1, 2, 0, 3)
    q = lax.all_to_all(q, "gz", split_axis=0, concat_axis=0, tiled=True)
    qf = q.reshape(16, 4, 2, 3, HD).transpose(1, 0, 2, 3, 4).reshape(4, 96, HD)

    every_hidden = lax.all_gather(hidden, "gx", axis=1, tiled=True)
    feed = jnp.einsum("tbf,fc->ctb", every_hidden, down_weight, preferred_element_type=F32)

    place = lax.axis_index(("gx",) + GY)
    positions = place * 128 + jnp.arange(128, dtype=jnp.int32)
    present = (positions[None, :] < lengths[:, None])[:, None, :]
    scale = HD**-0.5
    s = jnp.einsum("bqd,bpd->bqp", qf, key_cache, preferred_element_type=F32) * scale
    s = jnp.where(present, s, NEG)
    step = (jnp.arange(96) // 3) % 2
    allowed = (jnp.arange(2)[None, :] <= step[:, None]) & (place == 0)
    sn = jnp.einsum("bqd,ubd->bqu", qf, new_kv[..., :HD], preferred_element_type=F32) * scale
    sn = jnp.where(allowed[None], sn, NEG)
    peak = jnp.maximum(jnp.max(s, -1), jnp.max(sn, -1)).astype(BF16)
    pf = peak.astype(F32)[..., None]
    w = jnp.where(present, jnp.exp(s - pf), 0.0).astype(BF16)
    wn = jnp.where(allowed[None], jnp.exp(sn - pf), 0.0).astype(BF16)
    total = jnp.sum(w.astype(F32), -1) + jnp.sum(wn.astype(F32), -1)
    acc = jnp.einsum("bqp,bpd->bqd", w, value_cache, preferred_element_type=F32)
    acc = acc + jnp.einsum("bqu,ubd->bqd", wn, new_kv[..., HD:], preferred_element_type=F32)
    total_hi = total.astype(BF16)
    total_lo = (total - total_hi.astype(F32)).astype(BF16)
    stats = jnp.stack([peak, total_hi, total_lo, jnp.zeros_like(peak)], 1)
    stats = stats.reshape(4, 4, 8, 12).transpose(0, 2, 1, 3).reshape(32, 4, 12)
    stats = jnp.pad(stats, ((0, 0), (0, 0), (0, HD - 12)))
    message = jnp.concatenate([acc.astype(BF16).reshape(32, 12, HD), stats], 1)

    message = lax.all_to_all(message, ("gx",) + GY, split_axis=0, concat_axis=0, tiled=True)
    peaks = message[:, 12, :12].astype(F32)
    totals = message[:, 13, :12].astype(F32) + message[:, 14, :12].astype(F32)
    share = jnp.exp(peaks - jnp.max(peaks, 0))
    share = share / jnp.sum(share * totals, 0)
    attn = jnp.sum(message[:, :12].astype(F32) * share[..., None], 0).astype(BF16)
    attn = attn.reshape(2, 2, 3, HD).transpose(1, 0, 2, 3).reshape(2, 16, 96).transpose(1, 0, 2)
    attn = jnp.broadcast_to(attn[:, None], (16, 4, 2, 96)).reshape(64, 2, 96)

    mine = lax.all_to_all(attn, ("gz", "gx"), split_axis=0, concat_axis=0, tiled=True)
    projected = jnp.einsum("btf,fc->ctb", mine, out_weight, preferred_element_type=F32)

    part = (projected + feed).reshape(4, 2, 576, 128)
    core = lax.axis_index("core")
    theirs = lax.dynamic_index_in_dim(part, 1 - core, 1, keepdims=False).astype(BF16)
    ours = lax.dynamic_index_in_dim(part, core, 1, keepdims=False)
    theirs = lax.ppermute(theirs, "core", [(0, 1), (1, 0)])
    pair = (ours + theirs.astype(F32)).astype(BF16)
    row = lax.all_to_all(pair, "gyx", split_axis=0, concat_axis=0, tiled=True)
    row = jnp.sum(row.astype(F32), 0).astype(BF16).reshape(16, 36, 128)
    column = lax.all_to_all(row, "gz", split_axis=0, concat_axis=0, tiled=True)
    summed = jnp.sum(column.astype(F32), 0).reshape(36, 2, 64).transpose(1, 2, 0)
    return (summed + resid.astype(F32)).astype(BF16)


def solution(mesh):
    mesh = Mesh(mesh.devices.reshape(4, 4, 2, 16), ("gx", "gyx", "core", "gz"))
    rows = GY + ("gz",)
    width = P(None, None, ("gx",) + rows)
    in_specs = (
        width,
        P(None, None, "gz"),
        P(None, "gz", None),
        P("gz", ("gx",) + GY, None),
        P("gz", ("gx",) + GY, None),
        P("gz"),
        P(rows, "gx"),
        P(None, "gx", rows),
        P(rows, "gx"),
    )
    return jax.shard_map(
        per_device, mesh=mesh, in_specs=in_specs, out_specs=width, check_vma=False
    )
```

time: 764 us -> 140 us (0.18)
  the two profiles are of different devices: /device:TPU:24 before, /device:TPU:8 now
where the time goes in v1:
time: 140 us; the launch traced here: 139 us
  blocking collectives  65.2 us (47%)
  starting transfers between devices  24.7 us (18%)
  local copies, waits for them, and re-layouts  22.9 us (16%)
  waiting for transfers between devices  16.7 us (12%)
  matrix products  5.78 us (4%)
  other arithmetic  3.8 us (3%)
    all_to_all x1, blocking collectives, per_device(): column = lax.all_to_all(row, 'gz', split_axis=0, concat_axis=0, tiled=True)  25 us
    all_to_all x1, starting transfers between devices, per_device(): q = lax.all_to_all(q, 'gz', split_axis=0, concat_axis=0, tiled=True)  15.2 us
    all_to_all x1, waiting for transfers between devices, per_device(): q = lax.all_to_all(q, 'gz', split_axis=0, concat_axis=0, tiled=True)  14.9 us
    all_to_all x1, blocking collectives, per_device(): lax.all_to_all(message, ('gx',) + GY, split_axis=0, concat_axis=0, tiled=...  14.8 us
    all_to_all x1, blocking collectives, per_device(): row = lax.all_to_all(pair, 'gyx', split_axis=0, concat_axis=0, tiled=True)  13.5 us
    all_gather x1, blocking collectives, per_device(): every_hidden = lax.all_gather(hidden, 'gx', axis=1, tiled=True)  11.9 us
    dynamic_slice x2, local copies, waits for them, and re-layouts, per_device(): ours = lax.dynamic_index_in_dim(part, core, 1, keepdims=False)  7.63 us
    all_to_all x1, starting transfers between devices, per_device(): lax.all_to_all(attn, ('gz', 'gx'), split_axis=0, concat_axis=0, tiled=True)  7.55 us
  transfers between devices with their start and end apart: 3, of which 2 were waited for; matrix products, arithmetic and copies ran while one was open for 7% of the time, Pallas kernels for 0%

profile of v1, /device:TPU:8, one launch (start us, length us, event | category | flops | bytes accessed | tf_op | source)
XLA Modules:
  0.0 139.3 jit_solution(1321324279399925947)
XLA Ops:
  0.0 2.0 %copy.40 = bf16[2,64,768]{2,0,1:T(2,128)(2,1)} copy(bf16[2,64,768]{2,1,0:T(8,128)(2,1)} %param.10) | data formatting | bytes 393216 | tf_op args[1]
  2.0 15.2 %all-to-all-start = ((bf16[16,4,2,768]{3,2,1,0:T(2,128)(2,1)}), bf16[16,4,2,768]{3,2,1,0:T(2,128)(2,1)S(1)}, u32[]{:S(2)}, u32[]{:S(2)}) async-start(bf16[16,4,2,768]{3,2,1,0:T(2,128)(2,1)} %bitcast.1), calls=%async_computation | async-start | bytes 393216 | tf_op jit(solution)/shard_map/all_to_all | solution.py:19
  17.3 0.7 broadcast_compare_fusion
  18.0 0.7 fusion.25
  18.7 14.9 %all-to-all-done = bf16[16,4,2,768]{3,2,1,0:T(2,128)(2,1)S(1)} async-done(((bf16[16,4,2,768]{3,2,1,0:T(2,128)(2,1)}), bf16[16,4,2,768]{3,2,1,0:T(2,128)(2,1)S(1)}, u32[]{:S(2)}, u32[]{:S(2)}) %all-to-all-start) | async-done | bytes 196640 | tf_op jit(solution)/shard_map/all_to_all | solution.py:19
  33.7 0.2 copy.42
  33.9 1.3 fusion.26
  35.2 0.2 fusion.27
  35.4 0.2 convert_reduce_fusion.1
  35.7 0.2 fusion.17
  35.9 0.3 fusion.2
  36.3 0.1 add.85
  36.5 0.1 maximum_maximum_fusion
  36.7 14.8 %all_to_all.25 = bf16[32,16,256]{2,1,0:T(8,128)(2,1)S(1)} all-to-all(bf16[32,16,256]{2,1,0:T(8,128)(2,1)S(1)} %fusion.7), channel_id=1, replica_groups=mesh['gx'=4,'gyx'=4,'core'=2,'gz'=16] {'gx','gyx','core'}, dimensions={0} | all-to-all | bytes 524288 | tf_op jit(solution)/shard_map/all_to_all | solution.py:49
  51.6 0.1 multiply_reduce_fusion
  51.9 0.6 broadcast_in_dim.59
  52.5 7.6 %all-to-all-start.2 = ((bf16[64,2,96]{2,1,0:T(2,128)(2,1)}), bf16[64,2,96]{2,1,0:T(2,128)(2,1)S(1)}, u32[]{:S(2)}, u32[]{:S(2)}) async-start(bf16[64,2,96]{2,1,0:T(2,128)(2,1)} %bitcast.10), calls=%async_computation.2 | async-start | bytes 65536 | tf_op jit(solution)/shard_map/all_to_all | solution.py:58
  60.1 11.9 %all_gather.3 = bf16[2,64,288]{2,1,0:T(8,128)(2,1)S(1)} all-gather(bf16[2,16,288]{2,1,0:T(8,128)(2,1)S(1)} %copy-done.2), channel_id=1, replica_groups=mesh['gx'=4,'gyx'=4,'core'=2,'gz'=16] {'gx'}, dimensions={1}, use_global_device_ids=true | all-gather | bytes 92160 | tf_op jit(solution)/shard_map/all_gather | solution.py:22
  72.0 1.8 %all-to-all-done.2 = bf16[64,2,96]{2,1,0:T(2,128)(2,1)S(1)} async-done(((bf16[64,2,96]{2,1,0:T(2,128)(2,1)}), bf16[64,2,96]{2,1,0:T(2,128)(2,1)S(1)}, u32[]{:S(2)}, u32[]{:S(2)}) %all-to-all-start.2) | async-done | bytes 24608 | tf_op jit(solution)/shard_map/all_to_all | solution.py:58
  73.8 1.6 %convolution_bitcast_fusion = f32[4608,2,64]{0,2,1:T(8,128)S(1)} fusion(bf16[96,4608]{1,0:T(8,128)(2,1)} %param.15, bf16[64,2,96]{2,1,0:T(2,128)(2,1)S(1)} %all-to-all-done.2), kind=kOutput, calls=%fused_computation.1 | convolution fusion | flops 113246208 | bytes 3268608 | tf_op jit(solution)/shard_map/btf,fc->ctb/dot_general | solution.py:59
  75.5 2.2 %convolution_add_fusion = f32[4608,2,64]{0,2,1:T(8,128)} fusion(f32[4608,2,64]{0,2,1:T(8,128)S(1)} %convolution_bitcast_fusion, bf16[2,64,288]{2,1,0:T(8,128)(2,1)S(1)} %all_gather.3, bf16[288,4608]{1,0:T(8,128)(2,1)S(1)} %copy-done), kind=kOutput, calls=%fused_computation | convolution fusion | flops 340328448 | bytes 7446528 | tf_op jit(solution)/shard_map/tbf,fc->ctb/dot_general | solution.py:23
  77.7 4.7 %reshape.230 = f32[4,2,576,128]{2,1,0,3:T(2,128)} reshape(f32[4608,2,64]{0,2,1:T(8,128)} %convolution_add_fusion) | data formatting | bytes 4718592 | tf_op jit(solution)/shard_map/reshape | solution.py:61
  82.3 4.0 %constant_dynamic-slice_fusion = bf16[4,1,576,128]{2,1,0,3:T(2,128)(2,1)} fusion(f32[4,2,576,128]{2,1,0,3:T(2,128)} %reshape.230, s32[]{:T(128)S(6)} %select_n.48), kind=kLoop, calls=%fused_computation.52 | loop fusion | bytes 1179652 | tf_op jit(solution)/shard_map/jit(dynamic_index_in_dim)/dynamic_slice | solution.py:63
  86.3 2.5 %copy.57 = bf16[4,1,576,128]{3,2,1,0:T(8,128)(2,1)S(1)} copy(bf16[4,1,576,128]{2,1,0,3:T(2,128)(2,1)} %constant_dynamic-slice_fusion) | data formatting | bytes 1179648
  88.8 1.9 %collective-permute-start = (bf16[4,576,128]{2,1,0:T(8,128)(2,1)S(1)}, bf16[4,576,128]{2,1,0:T(8,128)(2,1)}, u32[]{:S(2)}, u32[]{:S(2)}) collective-permute-start(bf16[4,576,128]{2,1,0:T(8,128)(2,1)S(1)} %bitcast.50), channel_id=1, source_target_pairs={{0,16},{16,0},{1,17},{17,1},{2,18},{18,2},{3,19},{19,3},{4,20},{20... | collective-permute-start | bytes 1769480 | tf_op jit(solution)/shard_map/ppermute | solution.py:65
  90.8 4.0 %constant_dynamic-slice_fusion.1 = f32[4,1,576,128]{2,1,0,3:T(1,128)} fusion(f32[4,2,576,128]{2,1,0,3:T(2,128)} %reshape.230, s32[]{:T(128)S(6)} %select_n.47), kind=kLoop, calls=%fused_computation.53 | loop fusion | bytes 2359300 | tf_op jit(solution)/shard_map/jit(dynamic_index_in_dim)/dynamic_slice | solution.py:64
  94.7 3.7 %copy.52 = f32[4,1,576,128]{3,2,0,1:T(8,128)} copy(f32[4,1,576,128]{2,1,0,3:T(1,128)} %constant_dynamic-slice_fusion.1) | data formatting | bytes 2359296 | tf_op jit(solution)/shard_map/jit(dynamic_index_in_dim)/dynamic_slice | solution.py:64
  98.4 1.5 %fusion.1 = bf16[4,576,128]{2,1,0:T(8,128)(2,1)S(1)} fusion(f32[4,1,576,128]{3,2,0,1:T(8,128)} %copy.52, bf16[4,576,128]{2,1,0:T(8,128)(2,1)} %collective-permute-done), kind=kLoop, calls=%fused_computation.5 | loop fusion | flops 884736 | bytes 2359296 | tf_op jit(solution)/shard_map/convert_element_type | solution.py:66
  99.9 13.5 %all_to_all.26 = bf16[4,576,128]{2,1,0:T(8,128)(2,1)S(1)} all-to-all(bf16[4,576,128]{2,1,0:T(8,128)(2,1)S(1)} %fusion.1), channel_id=1, replica_groups=mesh['gx'=4,'gyx'=4,'core'=2,'gz'=16] {'gyx'}, dimensions={0} | all-to-all | bytes 1179648 | tf_op jit(solution)/shard_map/all_to_all | solution.py:67
  113.4 0.1 reduce_sum.61
  113.6 25.0 %all_to_all.27 = bf16[16,36,128]{2,1,0:T(8,128)(2,1)S(1)} all-to-all(bf16[16,36,128]{2,1,0:T(8,128)(2,1)S(1)} %reshape.231), channel_id=1, replica_groups=mesh['gx'=4,'gyx'=4,'core'=2,'gz'=16] {'gz'}, dimensions={0} | all-to-all | bytes 294912 | tf_op jit(solution)/shard_map/all_to_all | solution.py:69
  138.7 0.6 fusion.10
  (34 shorter events, 0.9 us)
Async XLA Ops:
  0.0 75.4 %copy-start = (bf16[288,4608]{1,0:T(8,128)(2,1)S(1)}, bf16[288,4608]{1,0:T(8,128)(2,1)}, u32[]{:S(2)}) copy-start(bf16[288,4608]{1,0:T(8,128)(2,1)} %param.17) | copy-start | bytes 7962628
  0.0 35.9 %copy-start.1 = (bf16[4,128,256]{2,1,0:T(8,128)(2,1)S(1)}, bf16[4,128,256]{2,1,0:T(8,128)(2,1)}, u32[]{:S(2)}) copy-start(bf16[4,128,256]{2,1,0:T(8,128)(2,1)} %param.13) | copy-start | bytes 786436
  2.0 31.6 %all-to-all-start = ((bf16[16,4,2,768]{3,2,1,0:T(2,128)(2,1)}), bf16[16,4,2,768]{3,2,1,0:T(2,128)(2,1)S(1)}, u32[]{:S(2)}, u32[]{:S(2)}) async-start(bf16[16,4,2,768]{3,2,1,0:T(2,128)(2,1)} %bitcast.1), calls=%async_computation | async-start | bytes 393216 | tf_op jit(solution)/shard_map/all_to_all | solution.py:19
  33.9 26.1 %copy-start.2 = (bf16[2,16,288]{2,1,0:T(8,128)(2,1)S(1)}, bf16[2,16,288]{2,1,0:T(8,128)(2,1)}, u32[]{:S(2)}) copy-start(bf16[2,16,288]{2,1,0:T(8,128)(2,1)} %param.16) | copy-start | bytes 55300
  52.5 21.3 %all-to-all-start.2 = ((bf16[64,2,96]{2,1,0:T(2,128)(2,1)}), bf16[64,2,96]{2,1,0:T(2,128)(2,1)S(1)}, u32[]{:S(2)}, u32[]{:S(2)}) async-start(bf16[64,2,96]{2,1,0:T(2,128)(2,1)} %bitcast.10), calls=%async_computation.2 | async-start | bytes 65536 | tf_op jit(solution)/shard_map/all_to_all | solution.py:58
  88.8 9.6 %collective-permute-start = (bf16[4,576,128]{2,1,0:T(8,128)(2,1)S(1)}, bf16[4,576,128]{2,1,0:T(8,128)(2,1)}, u32[]{:S(2)}, u32[]{:S(2)}) collective-permute-start(bf16[4,576,128]{2,1,0:T(8,128)(2,1)S(1)} %bitcast.50), channel_id=1, source_target_pairs={{0,16},{16,0},{1,17},{17,1},{2,18},{18,2},{3,19},{19,3},{4,20},{20... | collective-permute-start | bytes 1769480 | tf_op jit(solution)/shard_map/ppermute | solution.py:65
  98.4 40.3 %copy-start.3 = (bf16[2,64,36]{1,0,2:T(2,128)(2,1)S(1)}, bf16[2,64,36]{1,0,2:T(2,128)(2,1)}, u32[]{:S(2)}) copy-start(bf16[2,64,36]{1,0,2:T(2,128)(2,1)} %param.9) | copy-start | bytes 27652

commit v2 on v1

v2 whole, which is shorter than its diff:
```python
import jax
import jax.numpy as jnp
from jax import lax
from jax.experimental import pallas as pl
from jax.experimental.pallas import tpu as pltpu
from jax.sharding import Mesh
from jax.sharding import PartitionSpec as P

HEADS = 48
HD = 256
F32 = jnp.float32
BF16 = jnp.bfloat16
GY = ("gyx", "core")
NEG = -1e30
TILE = 1152


def turned_product(x, w, dtype, more=None):
    rows, depth = x.shape
    columns = w.shape[1]

    def kernel(x_ref, w_ref, *refs):
        y = jnp.dot(x_ref[...], w_ref[...], preferred_element_type=F32).T
        if more is not None:
            y = y + refs[0][...]
        refs[-1][...] = y.astype(dtype)

    out_block = pl.BlockSpec((TILE, rows), lambda i: (i, 0))
    in_specs = [
        pl.BlockSpec((rows, depth), lambda i: (0, 0)),
        pl.BlockSpec((depth, TILE), lambda i: (0, i)),
    ]
    operands = [x, w]
    if more is not None:
        in_specs.append(out_block)
        operands.append(more)
    return pl.pallas_call(
        kernel,
        grid=(columns // TILE,),
        in_specs=in_specs,
        out_specs=out_block,
        out_shape=jax.ShapeDtypeStruct((columns, rows), dtype),
        compiler_params=pltpu.CompilerParams(vmem_limit_bytes=16 * 2**20),
        cost_estimate=pl.CostEstimate(
            flops=2 * rows * depth * columns,
            bytes_accessed=2 * depth * columns + 4 * rows * columns,
            transcendentals=0,
        ),
    )(*operands)


def exchange(x, axes):
    return lax.all_to_all(x, axes, split_axis=0, concat_axis=0, tiled=True)


def per_device(
    resid, query, new_kv, key_cache, value_cache, lengths, out_weight, hidden, down_weight
):
    gx = lax.axis_index("gx")
    gy = lax.axis_index(GY)
    blocks = []
    for hop in range(4):
        owner = (gx + hop) & 3
        block = jnp.concatenate(
            [lax.dynamic_index_in_dim(c, owner, 0, False) for c in (key_cache, value_cache)], -1
        )
        if hop:
            block = lax.ppermute(block, "gx", [(i, (i + hop) % 4) for i in range(4)])
        blocks.append(block)
    cache = jnp.concatenate(blocks, 0)
    keys, values = cache[:, :HD], cache[:, HD:]

    pick = jnp.arange(32)
    pick = (pick % 2) * 64 + (pick // 2) * 4 + gx
    pick = (pick[:, None] == jnp.arange(128)[None, :]).astype(BF16)
    q = jnp.dot(pick, query.reshape(128, 768), preferred_element_type=F32).astype(BF16)
    q = exchange(q.reshape(16, 2, 768), "gz")
    qf = q.reshape(16, 2, 3, HD).reshape(96, HD)

    at = jnp.arange(512, dtype=jnp.int32)
    positions = (((gx - at // 128) & 3) * 8 + gy) * 128 + at % 128
    length = lax.dynamic_index_in_dim(lengths, gx, 0, keepdims=False)
    present = (positions < length)[None]
    scale = HD**-0.5
    s = jnp.einsum("qd,pd->qp", qf, keys, preferred_element_type=F32) * scale
    s = jnp.where(present, s, NEG)
    fresh = lax.dynamic_index_in_dim(new_kv, gx, 1, keepdims=False)
    step = (jnp.arange(96) // 3) % 2
    allowed = (jnp.arange(2)[None, :] <= step[:, None]) & (gy == 0)
    sn = jnp.einsum("qd,ud->qu", qf, fresh[:, :HD], preferred_element_type=F32) * scale
    sn = jnp.where(allowed, sn, NEG)
    peak = jnp.maximum(jnp.max(s, -1), jnp.max(sn, -1)).astype(BF16)
    pf = peak.astype(F32)[:, None]
    w = jnp.where(present, jnp.exp(s - pf), 0.0).astype(BF16)
    wn = jnp.where(allowed, jnp.exp(sn - pf), 0.0).astype(BF16)
    total = jnp.sum(w.astype(F32), -1) + jnp.sum(wn.astype(F32), -1)
    acc = jnp.einsum("qp,pd->qd", w, values, preferred_element_type=F32)
    acc = acc + jnp.einsum("qu,ud->qd", wn, fresh[:, HD:], preferred_element_type=F32)
    total_hi = total.astype(BF16)
    total_lo = (total - total_hi.astype(F32)).astype(BF16)
    stats = jnp.stack([peak, total_hi, total_lo, jnp.zeros_like(peak)], 0)
    stats = stats.reshape(4, 8, 12).transpose(1, 0, 2)
    stats = jnp.pad(stats, ((0, 0), (0, 0), (0, HD - 12)))
    message = jnp.concatenate([acc.astype(BF16).reshape(8, 12, HD), stats], 1)

    message = exchange(message, GY)
    peaks = message[:, 12, :12].astype(F32)
    totals = message[:, 13, :12].astype(F32) + message[:, 14, :12].astype(F32)
    share = jnp.exp(peaks - jnp.max(peaks, 0))
    share = share / jnp.sum(share * totals, 0)
    attn = jnp.sum(message[:, :12].astype(F32) * share[..., None], 0).astype(BF16)
    attn = attn.reshape(2, 2, 3, HD).transpose(1, 0, 2, 3).reshape(2, 16, 96).transpose(1, 0, 2)
    attn = jnp.broadcast_to(attn[:, None], (16, 4, 2, 96)).reshape(64, 2, 96)

    spread = lax.all_gather(hidden, "gx", axis=1, tiled=True).reshape(128, 288)
    feed = turned_product(spread, down_weight, F32)

    mine = exchange(attn, ("gz", "gx")).transpose(1, 0, 2).reshape(128, 96)
    part = turned_product(mine, out_weight, BF16, feed)

    row = exchange(part.reshape(8, 576, 128), GY)
    row = jnp.sum(row.astype(F32), 0).astype(BF16).reshape(16, 36, 128)
    column = exchange(row, "gz")
    summed = jnp.sum(column.astype(F32), 0).reshape(36, 2, 64).transpose(1, 2, 0)
    return (summed + resid.astype(F32)).astype(BF16)


def solution(mesh):
    mesh = Mesh(mesh.devices.reshape(4, 4, 2, 16), ("gx", "gyx", "core", "gz"))
    rows = GY + ("gz",)
    width = P(None, None, ("gx",) + rows)
    in_specs = (
        width,
        P(None, None, "gz"),
        P(None, "gz", None),
        P("gz", ("gx",) + GY, None),
        P("gz", ("gx",) + GY, None),
        P("gz"),
        P(rows, "gx"),
        P(None, "gx", rows),
        P(rows, "gx"),
    )
    return jax.shard_map(
        per_device, mesh=mesh, in_specs=in_specs, out_specs=width, check_vma=False
    )
```

time: 140 us -> 125 us (0.89)
  local copies, waits for them, and re-layouts: 22.9 us -> 6.92 us
  starting transfers between devices: 24.7 us -> 40 us
  waiting for transfers between devices: 16.7 us -> 2.18 us
  matrix products: 5.78 us -> 1.08 us
  Pallas kernels: 0 us -> 3.51 us
  blocking collectives: 65.2 us -> 68.6 us
  other arithmetic: 3.8 us -> 2.11 us
    all_to_all x2, waiting for transfers between devices: 16.7 us -> 0.01 us  [exchange(): return lax.all_to_all(x, axes, split_axis=0, concat_axis=0, tiled=True)]
    dynamic_slice x3 -> x2, local copies, waits for them, and re-layouts: 11.6 us -> 1.3 us  [the longest x1 0.71 us: per_device(): fresh = lax.dynamic_index_in_dim(new_kv, gx, 1, keepdims=False)]
    ppermute x1 -> x3, starting transfers between devices: 1.92 us -> 10 us  [per_device(): block = lax.ppermute(block, 'gx', [(i, (i + hop) % 4) for i in range(4)])]
    all_to_all x2, starting transfers between devices: 22.7 us -> 29.9 us  [exchange(): return lax.all_to_all(x, axes, split_axis=0, concat_axis=0, tiled=True)]
    dot_general x6 -> x5, matrix products: 5.78 us -> 1.08 us  [the longest x1 0.31 us: per_device(): s = jnp.einsum('qd,pd->qp', qf, keys, preferred_element_type=F32) * scale]
    reshape x3 -> x2, local copies, waits for them, and re-layouts: 4.79 us -> 0.68 us  [the longest x1 0.66 us: per_device(): q = exchange(q.reshape(16, 2, 768), 'gz')]
    pallas_call x0 -> x2, Pallas kernels: none -> 3.51 us  [turned_product(): pl.pallas_call(kernel, grid=(columns // TILE,), in_specs=in_specs, out_sp...]
    all_to_all x3, blocking collectives: 53.3 us -> 56.5 us  [exchange(): return lax.all_to_all(x, axes, split_axis=0, concat_axis=0, tiled=True)]
  transfers between devices with their start and end apart: 3 -> 5, of which waited for: 2 -> 1; matrix products, arithmetic and copies ran while one was open for 7% -> 3% of each run, Pallas kernels for 0% -> 1%
where the time goes in v2:
time: 125 us
  blocking collectives  68.6 us (55%)
  starting transfers between devices  40 us (32%)
  local copies, waits for them, and re-layouts  6.92 us (6%)
  Pallas kernels  3.51 us (3%)
  waiting for transfers between devices  2.18 us (2%)
  other arithmetic  2.11 us (2%)
    all_to_all x3, blocking collectives, exchange(): return lax.all_to_all(x, axes, split_axis=0, concat_axis=0, tiled=True)  56.5 us
    all_to_all x2, starting transfers between devices, exchange(): return lax.all_to_all(x, axes, split_axis=0, concat_axis=0, tiled=True)  29.9 us
    all_gather x1, blocking collectives, per_device(): spread = lax.all_gather(hidden, 'gx', axis=1, tiled=True).reshape(128, 288)  12 us
    ppermute x3, starting transfers between devices, per_device(): block = lax.ppermute(block, 'gx', [(i, (i + hop) % 4) for i in range(4)])  10 us
    pallas_call x2, Pallas kernels, turned_product(): pl.pallas_call(kernel, grid=(columns // TILE,), in_specs=in_specs, out_sp...  3.51 us
    unnamed x13, local copies, waits for them, and re-layouts  2.69 us
  transfers between devices with their start and end apart: 5, of which 1 were waited for; matrix products, arithmetic and copies ran while one was open for 3% of the time, Pallas kernels for 1%

profile of v2, /device:TPU:8, one launch (start us, length us, event | category | flops | bytes accessed | tf_op | source)
XLA Modules:
  0.0 124.6 jit_solution(4663223536306117972)
XLA Ops:
  0.0 0.9 copy-done
  0.9 0.2 convolution_convert_fusion
  1.1 0.7 reshape.227
  1.8 15.2 %all-to-all-start = ((bf16[16,2,768]{2,1,0:T(2,128)(2,1)}), bf16[16,2,768]{2,1,0:T(2,128)(2,1)S(1)}, u32[]{:S(2)}, u32[]{:S(2)}) async-start(bf16[16,2,768]{2,1,0:T(2,128)(2,1)} %reshape.227), calls=%async_computation | async-start | bytes 98304 | tf_op jit(solution)/shard_map/all_to_all | solution.py:53
  17.0 1.1 dynamic-slice_bitcast_fusion.6
  18.1 4.2 %collective-permute-start.1 = (bf16[128,512]{1,0:T(8,128)(2,1)S(1)}, bf16[128,512]{1,0:T(8,128)(2,1)S(1)}, u32[]{:S(2)}, u32[]{:S(2)}) collective-permute-start(bf16[128,512]{1,0:T(8,128)(2,1)S(1)} %pad_maximum_fusion.2), channel_id=1, source_target_pairs={{0,256},{128,384},{256,0},{384,128},{1,257},{129,385},{257,1},{385... | collective-permute-start | bytes 393224 | tf_op jit(solution)/shard_map/ppermute | solution.py:68
  22.4 3.3 %collective-permute-start.2 = (bf16[128,512]{1,0:T(8,128)(2,1)S(1)}, bf16[128,512]{1,0:T(8,128)(2,1)S(1)}, u32[]{:S(2)}, u32[]{:S(2)}) collective-permute-start(bf16[128,512]{1,0:T(8,128)(2,1)S(1)} %pad_maximum_fusion.3), channel_id=1, source_target_pairs={{0,384},{128,0},{256,128},{384,256},{1,385},{129,1},{257,129},{385... | collective-permute-start | bytes 393224 | tf_op jit(solution)/shard_map/ppermute | solution.py:68
  25.7 2.6 %collective-permute-start = (bf16[128,512]{1,0:T(8,128)(2,1)S(1)}, bf16[128,512]{1,0:T(8,128)(2,1)S(1)}, u32[]{:S(2)}, u32[]{:S(2)}) collective-permute-start(bf16[128,512]{1,0:T(8,128)(2,1)S(1)} %pad_maximum_fusion.1), channel_id=1, source_target_pairs={{0,128},{128,256},{256,384},{384,0},{1,129},{129,257},{257,385},{3... | collective-permute-start | bytes 393224 | tf_op jit(solution)/shard_map/ppermute | solution.py:68
  28.2 0.7 constant_dynamic-slice_fusion
  29.0 0.6 dynamic_slice.33
  29.7 0.7 fusion.22
  30.3 2.2 %collective-permute-done = bf16[128,512]{1,0:T(8,128)(2,1)S(1)} collective-permute-done((bf16[128,512]{1,0:T(8,128)(2,1)S(1)}, bf16[128,512]{1,0:T(8,128)(2,1)S(1)}, u32[]{:S(2)}, u32[]{:S(2)}) %collective-permute-start) | collective-permute-done | bytes 131104 | tf_op jit(solution)/shard_map/ppermute | solution.py:68
  32.6 0.3 fusion.34
  32.9 0.1 fusion.35
  33.1 0.2 convert_reduce_fusion.1
  33.4 0.1 convert_element_type.146
  33.5 0.2 fusion.25
  33.7 0.2 fusion.1
  34.1 9.7 %all_to_all.25 = bf16[8,16,256]{2,1,0:T(8,128)(2,1)S(1)} all-to-all(bf16[8,16,256]{2,1,0:T(8,128)(2,1)S(1)} %fusion.6), channel_id=1, replica_groups=mesh['gx'=4,'gyx'=4,'core'=2,'gz'=16] {'gyx','core'}, dimensions={0} | all-to-all | bytes 131072 | tf_op jit(solution)/shard_map/all_to_all | solution.py:53
  43.9 0.1 multiply_reduce_fusion
  44.0 0.1 reshape.229
  44.1 0.6 broadcast_in_dim.45
  44.7 14.7 %all-to-all-start.2 = ((bf16[64,2,96]{2,1,0:T(2,128)(2,1)}), bf16[64,2,96]{2,1,0:T(2,128)(2,1)S(1)}, u32[]{:S(2)}, u32[]{:S(2)}) async-start(bf16[64,2,96]{2,1,0:T(2,128)(2,1)} %bitcast.17), calls=%async_computation.2 | async-start | bytes 65536 | tf_op jit(solution)/shard_map/all_to_all | solution.py:53
  59.5 12.0 %all_gather.3 = bf16[2,64,288]{2,1,0:T(8,128)(2,1)S(1)} all-gather(bf16[2,16,288]{2,1,0:T(8,128)(2,1)S(1)} %copy-done.3), channel_id=1, replica_groups=mesh['gx'=4,'gyx'=4,'core'=2,'gz'=16] {'gx'}, dimensions={1}, use_global_device_ids=true | all-gather | bytes 92160 | tf_op jit(solution)/shard_map/all_gather | solution.py:115
  71.5 1.7 %copy-done.1 = bf16[288,4608]{1,0:T(8,128)(2,1)S(1)} copy-done((bf16[288,4608]{1,0:T(8,128)(2,1)S(1)}, bf16[288,4608]{1,0:T(8,128)(2,1)}, u32[]{:S(2)}) %copy-start.1) | copy-done | bytes 2654232
  73.3 1.8 %shard_map.91.refs_0_ = f32[4608,128]{1,0:T(8,128)S(1)} custom-call(bf16[128,288]{1,0:T(8,128)(2,1)S(1)} %bitcast.45, bf16[288,4608]{1,0:T(8,128)(2,1)S(1)} %copy-done.1), custom_call_target="tpu_custom_call" | custom-call | flops 339738624 | bytes 5013504 | tf_op jit(solution)/shard_map/pallas_call | solution.py:37
  75.1 1.7 %shard_map.92 = bf16[4608,128]{1,0:T(8,128)(2,1)S(1)} custom-call(bf16[128,96]{1,0:T(8,128)(2,1)S(1)} %bitcast.46, bf16[96,4608]{1,0:T(8,128)(2,1)S(1)} %copy-done.2, f32[4608,128]{1,0:T(8,128)S(1)} %shard_map.91.refs_0_), custom_call_target="tpu_custom_call" | custom-call | flops 113246208 | bytes 3244032 | tf_op jit(solution)/shard_map/pallas_call | solution.py:37
  76.8 19.9 %all_to_all.26 = bf16[8,576,128]{2,1,0:T(8,128)(2,1)S(1)} all-to-all(bf16[8,576,128]{2,1,0:T(8,128)(2,1)S(1)} %bitcast.44), channel_id=1, replica_groups=mesh['gx'=4,'gyx'=4,'core'=2,'gz'=16] {'gyx','core'}, dimensions={0} | all-to-all | bytes 2359296 | tf_op jit(solution)/shard_map/all_to_all | solution.py:53
  96.7 0.2 reduce_sum.61
  96.9 26.9 %all_to_all.27 = bf16[16,36,128]{2,1,0:T(8,128)(2,1)S(1)} all-to-all(bf16[16,36,128]{2,1,0:T(8,128)(2,1)S(1)} %reshape.234), channel_id=1, replica_groups=mesh['gx'=4,'gyx'=4,'core'=2,'gz'=16] {'gz'}, dimensions={0} | all-to-all | bytes 294912 | tf_op jit(solution)/shard_map/all_to_all | solution.py:53
  123.9 0.1 reshape.235
  124.0 0.6 fusion.7
  (43 shorter events, 0.7 us)
Async XLA Ops:
  0.0 0.9 copy-start
  0.0 29.0 %copy-start.5 = (s32[4]{0:T(128)S(1)}, s32[4]{0:T(128)}, u32[]{:S(2)}) copy-start(s32[4]{0:T(128)} %param.14) | copy-start | bytes 52
  1.8 30.8 %all-to-all-start = ((bf16[16,2,768]{2,1,0:T(2,128)(2,1)}), bf16[16,2,768]{2,1,0:T(2,128)(2,1)S(1)}, u32[]{:S(2)}, u32[]{:S(2)}) async-start(bf16[16,2,768]{2,1,0:T(2,128)(2,1)} %reshape.227), calls=%async_computation | async-start | bytes 98304 | tf_op jit(solution)/shard_map/all_to_all | solution.py:53
  18.1 41.4 %copy-start.3 = (bf16[2,16,288]{2,1,0:T(8,128)(2,1)S(1)}, bf16[2,16,288]{2,1,0:T(8,128)(2,1)}, u32[]{:S(2)}) copy-start(bf16[2,16,288]{2,1,0:T(8,128)(2,1)} %param.16) | copy-start | bytes 55300
  18.1 12.2 %collective-permute-start.1 = (bf16[128,512]{1,0:T(8,128)(2,1)S(1)}, bf16[128,512]{1,0:T(8,128)(2,1)S(1)}, u32[]{:S(2)}, u32[]{:S(2)}) collective-permute-start(bf16[128,512]{1,0:T(8,128)(2,1)S(1)} %pad_maximum_fusion.2), channel_id=1, source_target_pairs={{0,256},{128,384},{256,0},{384,128},{1,257},{129,385},{257,1},{385... | collective-permute-start | bytes 393224 | tf_op jit(solution)/shard_map/ppermute | solution.py:68
  22.4 8.0 %collective-permute-start.2 = (bf16[128,512]{1,0:T(8,128)(2,1)S(1)}, bf16[128,512]{1,0:T(8,128)(2,1)S(1)}, u32[]{:S(2)}, u32[]{:S(2)}) collective-permute-start(bf16[128,512]{1,0:T(8,128)(2,1)S(1)} %pad_maximum_fusion.3), channel_id=1, source_target_pairs={{0,384},{128,0},{256,128},{384,256},{1,385},{129,1},{257,129},{385... | collective-permute-start | bytes 393224 | tf_op jit(solution)/shard_map/ppermute | solution.py:68
  25.7 6.9 %collective-permute-start = (bf16[128,512]{1,0:T(8,128)(2,1)S(1)}, bf16[128,512]{1,0:T(8,128)(2,1)S(1)}, u32[]{:S(2)}, u32[]{:S(2)}) collective-permute-start(bf16[128,512]{1,0:T(8,128)(2,1)S(1)} %pad_maximum_fusion.1), channel_id=1, source_target_pairs={{0,128},{128,256},{256,384},{384,0},{1,129},{129,257},{257,385},{3... | collective-permute-start | bytes 393224 | tf_op jit(solution)/shard_map/ppermute | solution.py:68
  44.7 30.4 %all-to-all-start.2 = ((bf16[64,2,96]{2,1,0:T(2,128)(2,1)}), bf16[64,2,96]{2,1,0:T(2,128)(2,1)S(1)}, u32[]{:S(2)}, u32[]{:S(2)}) async-start(bf16[64,2,96]{2,1,0:T(2,128)(2,1)} %bitcast.17), calls=%async_computation.2 | async-start | bytes 65536 | tf_op jit(solution)/shard_map/all_to_all | solution.py:53
  71.5 1.8 %copy-start.1 = (bf16[288,4608]{1,0:T(8,128)(2,1)S(1)}, bf16[288,4608]{1,0:T(8,128)(2,1)}, u32[]{:S(2)}) copy-start(bf16[288,4608]{1,0:T(8,128)(2,1)} %w_ref.2) | copy-start | bytes 7962628
  73.3 1.9 %copy-start.2 = (bf16[96,4608]{1,0:T(8,128)(2,1)S(1)}, bf16[96,4608]{1,0:T(8,128)(2,1)}, u32[]{:S(2)}) copy-start(bf16[96,4608]{1,0:T(8,128)(2,1)} %w_ref.3) | copy-start | bytes 2654212
  76.8 47.2 %copy-start.4 = (bf16[2,64,36]{1,0,2:T(2,128)(2,1)S(1)}, bf16[2,64,36]{1,0,2:T(2,128)(2,1)}, u32[]{:S(2)}) copy-start(bf16[2,64,36]{1,0,2:T(2,128)(2,1)} %param.9) | copy-start | bytes 27652

commit v3 on v1

v3 whole, which is shorter than its diff:
```python
import jax
import jax.numpy as jnp
from jax import lax
from jax.experimental import pallas as pl
from jax.experimental.pallas import tpu as pltpu
from jax.sharding import Mesh
from jax.sharding import PartitionSpec as P

HEADS = 48
HD = 256
F32 = jnp.float32
BF16 = jnp.bfloat16
GY = ("gyx", "core")
NEG = -1e30
TILE = 1152


def split_product(core, x, out_weight, gathered, down_weight):
    rows, depth = x.shape
    shares, held, width = gathered.shape
    columns = out_weight.shape[1]
    half = TILE // 2

    def kernel(core_ref, x_ref, w_ref, h_ref, d_ref, ours_ref, theirs_ref, full_ref):
        hidden = jnp.concatenate(
            [h_ref[s, 16 * t : 16 * t + 16, :] for t in range(2) for s in range(shares)], 0
        )
        y = jnp.dot(hidden, d_ref[...], preferred_element_type=F32)
        y = y + jnp.dot(x_ref[...], w_ref[...], preferred_element_type=F32)
        full_ref[...] = y.T
        mine = core_ref[0]
        ours_ref[...] = full_ref[pl.ds(pl.multiple_of(mine * half, half), half), :]
        theirs = full_ref[pl.ds(pl.multiple_of((1 - mine) * half, half), half), :]
        theirs_ref[...] = theirs.astype(BF16)

    half_block = pl.BlockSpec((half, rows), lambda i: (i, 0))
    return pl.pallas_call(
        kernel,
        grid=(columns // TILE,),
        in_specs=[
            pl.BlockSpec(memory_space=pltpu.SMEM),
            pl.BlockSpec((rows, depth), lambda i: (0, 0)),
            pl.BlockSpec((depth, TILE), lambda i: (0, i)),
            pl.BlockSpec((shares, held, width), lambda i: (0, 0, 0)),
            pl.BlockSpec((width, TILE), lambda i: (0, i)),
        ],
        out_specs=[half_block, half_block],
        out_shape=[
            jax.ShapeDtypeStruct((columns // 2, rows), F32),
            jax.ShapeDtypeStruct((columns // 2, rows), BF16),
        ],
        scratch_shapes=[pltpu.VMEM((TILE, rows), F32)],
        compiler_params=pltpu.CompilerParams(vmem_limit_bytes=16 * 2**20),
        cost_estimate=pl.CostEstimate(
            flops=2 * rows * (depth + width) * columns,
            bytes_accessed=2 * (depth + width) * columns + 3 * rows * columns,
            transcendentals=0,
        ),
    )(core.reshape(1), x, out_weight, gathered, down_weight)


def exchange(x, axes):
    return lax.all_to_all(x, axes, split_axis=0, concat_axis=0, tiled=True)


def per_device(
    resid, query, new_kv, key_cache, value_cache, lengths, out_weight, hidden, down_weight
):
    gx, gyx, core = lax.axis_index("gx"), lax.axis_index("gyx"), lax.axis_index("core")

    spread = jnp.pad(hidden.reshape(32, 288), ((0, 480), (0, 0)))
    spread = lax.all_gather(spread, "gx", axis=0, tiled=True).reshape(4, 512, 288)[:, :32]

    pair = jnp.concatenate([key_cache, value_cache], -1)
    pair = lax.ppermute(pair, "core", [(0, 1), (1, 0)])
    keys = jnp.concatenate([key_cache, pair[..., :HD]], 1)
    values = jnp.concatenate([value_cache, pair[..., HD:]], 1)
    q = exchange(query.reshape(2, 16, 4, 768).transpose(1, 2, 0, 3), "gz")
    q = lax.dynamic_index_in_dim(q.reshape(4, 2, 2, 4, 2, 768), core, 1, keepdims=False)
    qf = q.reshape(4, 2, 4, 2, 3, HD).transpose(2, 0, 1, 3, 4, 5).reshape(4, 48, HD)

    at = jnp.arange(256, dtype=jnp.int32)
    owner = gx * 8 + gyx * 2 + jnp.where(at < 128, core, 1 - core)
    positions = owner * 128 + at % 128
    present = (positions[None] < lengths[:, None])[:, None]
    scale = HD**-0.5
    s = jnp.einsum("bqd,bpd->bqp", qf, keys, preferred_element_type=F32) * scale
    s = jnp.where(present, s, NEG)
    step = (jnp.arange(48) // 3) % 2
    allowed = (jnp.arange(2)[None, :] <= step[:, None]) & (gx + gyx == 0)
    sn = jnp.einsum("bqd,ubd->bqu", qf, new_kv[..., :HD], preferred_element_type=F32) * scale
    sn = jnp.where(allowed, sn, NEG)
    peak = jnp.maximum(jnp.max(s, -1), jnp.max(sn, -1)).astype(BF16)
    pf = peak.astype(F32)[..., None]
    w = jnp.where(present, jnp.exp(s - pf), 0.0).astype(BF16)
    wn = jnp.where(allowed, jnp.exp(sn - pf), 0.0).astype(BF16)
    total = jnp.sum(w.astype(F32), -1) + jnp.sum(wn.astype(F32), -1)
    acc = jnp.einsum("bqp,bpd->bqd", w, values, preferred_element_type=F32)
    acc = acc + jnp.einsum("bqu,ubd->bqd", wn, new_kv[..., HD:], preferred_element_type=F32)
    total_hi = total.astype(BF16)
    total_lo = (total - total_hi.astype(F32)).astype(BF16)
    stats = jnp.stack([peak, total_hi, total_lo, jnp.zeros_like(peak)], 1)
    stats = stats.reshape(4, 4, 4, 12).transpose(0, 2, 1, 3).reshape(16, 4, 12)
    stats = jnp.pad(stats, ((0, 0), (0, 0), (0, HD - 12)))
    message = jnp.concatenate([acc.astype(BF16).reshape(16, 12, HD), stats], 1)

    message = exchange(message, ("gx", "gyx"))
    peaks = message[:, 12, :12].astype(F32)
    totals = message[:, 13, :12].astype(F32) + message[:, 14, :12].astype(F32)
    share = jnp.exp(peaks - jnp.max(peaks, 0))
    share = share / jnp.sum(share * totals, 0)
    attn = jnp.sum(message[:, :12].astype(F32) * share[..., None], 0).astype(BF16)
    attn = attn.reshape(2, 2, 3, HD).transpose(1, 0, 2, 3).reshape(2, 16, 96).transpose(1, 0, 2)
    attn = jnp.broadcast_to(attn[:, None], (16, 4, 2, 96)).reshape(64, 2, 96)

    attn, spread = lax.optimization_barrier((attn, spread))

    mine = exchange(attn, ("gz", "gx")).transpose(1, 0, 2).reshape(128, 96)
    ours, theirs = split_product(core, mine, out_weight, spread, down_weight)

    theirs = lax.ppermute(theirs, "core", [(0, 1), (1, 0)])
    row = (ours + theirs.astype(F32)).astype(BF16).reshape(4, 576, 128)
    row = exchange(row, "gyx")
    row = jnp.sum(row.astype(F32), 0).astype(BF16).reshape(16, 36, 128)
    column = exchange(row, "gz")
    summed = jnp.sum(column.astype(F32), 0).reshape(36, 2, 64).transpose(1, 2, 0)
    return (summed + resid.astype(F32)).astype(BF16)


def solution(mesh):
    mesh = Mesh(mesh.devices.reshape(4, 4, 2, 16), ("gx", "gyx", "core", "gz"))
    rows = GY + ("gz",)
    width = P(None, None, ("gx",) + rows)
    in_specs = (
        width,
        P(None, None, "gz"),
        P(None, "gz", None),
        P("gz", ("gx",) + GY, None),
        P("gz", ("gx",) + GY, None),
        P("gz"),
        P(rows, "gx"),
        P(None, "gx", rows),
        P(rows, "gx"),
    )
    return jax.shard_map(
        per_device, mesh=mesh, in_specs=in_specs, out_specs=width, check_vma=False
    )
```

time: 140 us -> 140 us (level)
  the two profiles are of different devices: /device:TPU:8 before, /device:TPU:32 now
where the time goes in v3:
time: 140 us; the launch traced here: 139 us
  blocking collectives  75.5 us (54%)
  starting transfers between devices  19.2 us (14%)
  waiting for transfers between devices  14.9 us (11%)
  between operations  13.7 us (10%)
  local copies, waits for them, and re-layouts  7.86 us (6%)
  matrix products  3.12 us (2%)
  other arithmetic  2.5 us (2%)
  Pallas kernels  2.47 us (2%)
    all_to_all x4, blocking collectives, exchange(): return lax.all_to_all(x, axes, split_axis=0, concat_axis=0, tiled=True)  75.5 us
    all_to_all x1, starting transfers between devices, exchange(): return lax.all_to_all(x, axes, split_axis=0, concat_axis=0, tiled=True)  15.3 us
    all_to_all x1, waiting for transfers between devices, exchange(): return lax.all_to_all(x, axes, split_axis=0, concat_axis=0, tiled=True)  9.62 us
  transfers between devices with their start and end apart: 4, of which 4 were waited for; matrix products, arithmetic and copies ran while one was open for 7% of the time, Pallas kernels for 0%

profile of v3, /device:TPU:32, one launch (start us, length us, event | category | flops | bytes accessed | tf_op | source)
XLA Modules:
  0.0 139.2 jit_solution(5892156274073637516)
XLA Ops:
  6.5 1.9 %copy.41 = bf16[2,64,768]{2,0,1:T(2,128)(2,1)} copy(bf16[2,64,768]{2,1,0:T(8,128)(2,1)} %param.10) | data formatting | bytes 393216 | tf_op jit(solution)/shard_map/reshape | solution.py:78
  8.4 15.3 %all-to-all-start = ((bf16[16,4,2,768]{3,2,1,0:T(2,128)(2,1)}), bf16[16,4,2,768]{3,2,1,0:T(2,128)(2,1)S(1)}, u32[]{:S(2)}, u32[]{:S(2)}) async-start(bf16[16,4,2,768]{3,2,1,0:T(2,128)(2,1)} %bitcast.2), calls=%async_computation | async-start | bytes 393216 | tf_op jit(solution)/shard_map/all_to_all | solution.py:63
  23.8 1.5 %pad.9 = bf16[512,288]{1,0:T(8,128)(2,1)} pad(bf16[32,288]{1,0:T(8,128)(2,1)} %bitcast.50, bf16[]{:T(256)} %constant.77.clone.1), padding=0_480x0_0 | pad | bytes 313346 | tf_op jit(solution)/shard_map/jit(_pad)/pad | solution.py:71
  25.4 1.9 %collective-permute-start = (bf16[4,128,512]{2,1,0:T(8,128)(2,1)S(1)}, bf16[4,128,512]{2,1,0:T(8,128)(2,1)S(1)}, u32[]{:S(2)}, u32[]{:S(2)}) collective-permute-start(bf16[4,128,512]{2,1,0:T(8,128)(2,1)S(1)} %pad_maximum_fusion), channel_id=1, source_target_pairs={{0,16},{16,0},{1,17},{17,1},{2,18},{18,2},{3,19},{19,3},{4,20},{20... | collective-permute-start | bytes 1572872 | tf_op jit(solution)/shard_map/ppermute | solution.py:75
  27.6 0.6 fusion.33
  28.1 1.1 collective-permute-done
  29.2 0.7 fusion.31
  29.9 9.6 %all-to-all-done = bf16[16,4,2,768]{3,2,1,0:T(2,128)(2,1)S(1)} async-done(((bf16[16,4,2,768]{3,2,1,0:T(2,128)(2,1)}), bf16[16,4,2,768]{3,2,1,0:T(2,128)(2,1)S(1)}, u32[]{:S(2)}, u32[]{:S(2)}) %all-to-all-start) | async-done | bytes 196640 | tf_op jit(solution)/shard_map/all_to_all | solution.py:63
  39.8 0.1 fusion.36
  40.0 0.4 fusion.35
  40.4 0.2 convert_reduce_fusion.1
  40.6 0.1 maximum_maximum_fusion
  40.7 0.1 fusion.34
  40.8 1.1 fusion.19
  41.9 1.6 %fusion.1 = bf16[4,48,256]{2,1,0:T(8,128)(2,1)} fusion(f32[4,48,256]{2,1,0:T(8,128)S(1)} %fusion.19, bf16[4,128,256]{2,1,0:T(8,128)(2,1)S(1)} %copy-done.5, bf16[4,128,256]{2,1,0:T(8,128)(2,1)S(1)} %copy-done.4, f32[4,48,256]{2,1,0:T(8,128)S(1)} %get-tuple-element.28, f32[4,48]{1,0:T(4,128)S(1)} %get-tuple-element.15, pred[4,256]{1,0:T(4,128)(4,1)} %copy-done.8), kind=kOutput, calls=%fused_computation.4 | convolution fusion | flops 26460160 | bytes 1017600 | tf_op jit(solution)/shard_map/bqp,bpd->bqd/dot_general | solution.py:98
  43.4 1.6 %reshape.212 = bf16[16,12,256]{2,1,0:T(8,128)(2,1)} reshape(bf16[4,48,256]{2,1,0:T(8,128)(2,1)} %fusion.1) | data formatting | bytes 196608 | tf_op jit(solution)/shard_map/reshape | solution.py:105
  45.0 0.9 fusion.10
  45.9 14.8 %all_to_all.25 = bf16[16,16,256]{2,1,0:T(8,128)(2,1)S(1)} all-to-all(bf16[16,16,256]{2,1,0:T(8,128)(2,1)S(1)} %fusion.10), channel_id=1, replica_groups=mesh['gx'=4,'gyx'=4,'core'=2,'gz'=16] {'gx','gyx'}, dimensions={0} | all-to-all | bytes 262144 | tf_op jit(solution)/shard_map/all_to_all | solution.py:63
  60.9 0.1 multiply_reduce_fusion
  61.0 0.1 reshape.214
  61.1 2.2 %all-gather.2.cloned.1.call-done = bf16[2048,288]{1,0:T(8,128)(2,1)} async-done(((bf16[512,288]{1,0:T(8,128)(2,1)}), bf16[2048,288]{1,0:T(8,128)(2,1)}) %all-gather.2.cloned.1.call-update) | async-done | bytes 1179664 | tf_op jit(solution)/shard_map/all_gather | solution.py:72
  63.4 0.9 slice.62.h_ref
  64.3 27.9 %all_to_all.26 = bf16[64,2,96]{2,1,0:T(2,128)(2,1)S(1)} all-to-all(bf16[64,2,96]{2,1,0:T(2,128)(2,1)S(1)} %bitcast.42), channel_id=1, replica_groups=mesh['gx'=4,'gyx'=4,'core'=2,'gz'=16] {'gz','gx'}, dimensions={0} | all-to-all | bytes 49152 | tf_op jit(solution)/shard_map/all_to_all | solution.py:63
  92.2 2.5 %shard_map.91 = (f32[2304,128]{1,0:T(8,128)S(1)}, bf16[2304,128]{1,0:T(8,128)(2,1)S(1)}) custom-call(s32[1]{0:T(128)} %bitcast.core_ref, bf16[128,96]{1,0:T(8,128)(2,1)S(1)} %bitcast.38, bf16[96,4608]{1,0:T(8,128)(2,1)S(1)} %copy-done.1, bf16[4,32,288]{2,1,0:T(8,128)(2,1)S(1)} %slice.62.h_ref, bf16[288,4608]{1,0:T(8,128)(2,1)S(1)} %copy-done), custom_call_target="tpu_custom_call" | custom-call | flops 452984832 | bytes 5308416 | tf_op jit(solution)/shard_map/pallas_call | solution.py:37
  94.6 1.9 %collective-permute-start.1 = (bf16[2304,128]{1,0:T(8,128)(2,1)S(1)}, bf16[2304,128]{1,0:T(8,128)(2,1)S(1)}, u32[]{:S(2)}, u32[]{:S(2)}) collective-permute-start(bf16[2304,128]{1,0:T(8,128)(2,1)S(1)} %get-tuple-element.12), channel_id=1, source_target_pairs={{0,16},{16,0},{1,17},{17,1},{2,18},{18,2},{3,19},{19,3},{4,20},{20... | collective-permute-start | bytes 1769480 | tf_op jit(solution)/shard_map/ppermute | solution.py:121
  96.6 2.0 %collective-permute-done.1 = bf16[2304,128]{1,0:T(8,128)(2,1)S(1)} collective-permute-done((bf16[2304,128]{1,0:T(8,128)(2,1)S(1)}, bf16[2304,128]{1,0:T(8,128)(2,1)S(1)}, u32[]{:S(2)}, u32[]{:S(2)}) %collective-permute-start.1) | collective-permute-done | bytes 589856 | tf_op jit(solution)/shard_map/ppermute | solution.py:121
  98.5 0.1 add_convert_fusion
  98.7 14.1 %all_to_all.27 = bf16[4,576,128]{2,1,0:T(8,128)(2,1)S(1)} all-to-all(bf16[4,576,128]{2,1,0:T(8,128)(2,1)S(1)} %bitcast.39), channel_id=1, replica_groups=mesh['gx'=4,'gyx'=4,'core'=2,'gz'=16] {'gyx'}, dimensions={0} | all-to-all | bytes 1179648 | tf_op jit(solution)/shard_map/all_to_all | solution.py:63
  112.8 0.1 reduce_sum.61
  112.9 18.7 %all_to_all.28 = bf16[16,36,128]{2,1,0:T(8,128)(2,1)S(1)} all-to-all(bf16[16,36,128]{2,1,0:T(8,128)(2,1)S(1)} %reshape.220), channel_id=1, replica_groups=mesh['gx'=4,'gyx'=4,'core'=2,'gz'=16] {'gz'}, dimensions={0} | all-to-all | bytes 294912 | tf_op jit(solution)/shard_map/all_to_all | solution.py:63
  131.6 0.1 reshape.221
  131.7 0.6 fusion.13
  (49 shorter events, 0.8 us)
Async XLA Ops:
  6.5 18.8 %copy-start.3 = (bf16[4,128,256]{2,1,0:T(8,128)(2,1)S(1)}, bf16[4,128,256]{2,1,0:T(8,128)(2,1)}, u32[]{:S(2)}) copy-start(bf16[4,128,256]{2,1,0:T(8,128)(2,1)} %param.13) | copy-start | bytes 786436
  6.5 18.8 %copy-start.2 = (bf16[4,128,256]{2,1,0:T(8,128)(2,1)S(1)}, bf16[4,128,256]{2,1,0:T(8,128)(2,1)}, u32[]{:S(2)}) copy-start(bf16[4,128,256]{2,1,0:T(8,128)(2,1)} %param.12) | copy-start | bytes 786436
  8.4 19.1 %copy-start.9 = (s32[4]{0:T(128)S(1)}, s32[4]{0:T(128)}, u32[]{:S(2)}) copy-start(s32[4]{0:T(128)} %param.14) | copy-start | bytes 52
  8.4 19.1 %copy-start.7 = (bf16[2,4,512]{2,1,0:T(4,128)(2,1)S(1)}, bf16[2,4,512]{2,1,0:T(4,128)(2,1)}, u32[]{:S(2)}) copy-start(bf16[2,4,512]{2,1,0:T(4,128)(2,1)} %param.11) | copy-start | bytes 24580
  8.4 31.2 %all-to-all-start = ((bf16[16,4,2,768]{3,2,1,0:T(2,128)(2,1)}), bf16[16,4,2,768]{3,2,1,0:T(2,128)(2,1)S(1)}, u32[]{:S(2)}, u32[]{:S(2)}) async-start(bf16[16,4,2,768]{3,2,1,0:T(2,128)(2,1)} %bitcast.2), calls=%async_computation | async-start | bytes 393216 | tf_op jit(solution)/shard_map/all_to_all | solution.py:63
  23.8 39.6 %all-gather.2.cloned.1.call-start = ((), (), s32[]{:S(2)}) async-start(), calls=%async_computation.5 | async-start | bytes 1966080 | tf_op jit(solution)/shard_map/all_gather | solution.py:72
  25.4 3.8 %collective-permute-start = (bf16[4,128,512]{2,1,0:T(8,128)(2,1)S(1)}, bf16[4,128,512]{2,1,0:T(8,128)(2,1)S(1)}, u32[]{:S(2)}, u32[]{:S(2)}) collective-permute-start(bf16[4,128,512]{2,1,0:T(8,128)(2,1)S(1)} %pad_maximum_fusion), channel_id=1, source_target_pairs={{0,16},{16,0},{1,17},{17,1},{2,18},{18,2},{3,19},{19,3},{4,20},{20... | collective-permute-start | bytes 1572872 | tf_op jit(solution)/shard_map/ppermute | solution.py:75
  27.5 12.8 %copy-start.8 = (pred[4,256]{1,0:T(4,128)(4,1)}, pred[4,256]{1,0:T(4,128)(4,1)S(1)}, u32[]{:S(2)}) copy-start(pred[4,256]{1,0:T(4,128)(4,1)S(1)} %broadcast_compare_fusion) | copy-start | bytes 3076
  39.7 2.1 %copy-start.4 = (bf16[4,128,256]{2,1,0:T(8,128)(2,1)S(1)}, bf16[4,128,256]{2,1,0:T(8,128)(2,1)}, u32[]{:S(2)}) copy-start(bf16[4,128,256]{2,1,0:T(8,128)(2,1)} %param.13) | copy-start | bytes 786436
  39.7 2.1 %copy-start.5 = (bf16[4,128,256]{2,1,0:T(8,128)(2,1)S(1)}, bf16[4,128,256]{2,1,0:T(8,128)(2,1)}, u32[]{:S(2)}) copy-start(bf16[4,128,256]{2,1,0:T(8,128)(2,1)} %get-tuple-element.17) | copy-start | bytes 786436
  39.9 52.2 %copy-start.1 = (bf16[96,4608]{1,0:T(8,128)(2,1)S(1)}, bf16[96,4608]{1,0:T(8,128)(2,1)}, u32[]{:S(2)}) copy-start(bf16[96,4608]{1,0:T(8,128)(2,1)} %w_ref.1) | copy-start | bytes 2654212
  40.8 51.4 %copy-start = (bf16[288,4608]{1,0:T(8,128)(2,1)S(1)}, bf16[288,4608]{1,0:T(8,128)(2,1)}, u32[]{:S(2)}) copy-start(bf16[288,4608]{1,0:T(8,128)(2,1)} %d_ref.1) | copy-start | bytes 7962628
  94.6 3.9 %collective-permute-start.1 = (bf16[2304,128]{1,0:T(8,128)(2,1)S(1)}, bf16[2304,128]{1,0:T(8,128)(2,1)S(1)}, u32[]{:S(2)}, u32[]{:S(2)}) collective-permute-start(bf16[2304,128]{1,0:T(8,128)(2,1)S(1)} %get-tuple-element.12), channel_id=1, source_target_pairs={{0,16},{16,0},{1,17},{17,1},{2,18},{18,2},{3,19},{19,3},{4,20},{20... | collective-permute-start | bytes 1769480 | tf_op jit(solution)/shard_map/ppermute | solution.py:121
  98.7 33.1 %copy-start.6 = (bf16[2,64,36]{1,0,2:T(2,128)(2,1)S(1)}, bf16[2,64,36]{1,0,2:T(2,128)(2,1)}, u32[]{:S(2)}) copy-start(bf16[2,64,36]{1,0,2:T(2,128)(2,1)} %param.9) | copy-start | bytes 27652
Sparse Core Ops, SparseCore 0:
  26.7 36.6 all-gather.1

commit v4 on v3

--- a/solution.py
+++ b/solution.py
@@ -21,42 +21,58 @@
     columns = out_weight.shape[1]
     half = TILE // 2
 
-    def kernel(core_ref, x_ref, w_ref, h_ref, d_ref, ours_ref, theirs_ref, full_ref):
+    tiles = columns // TILE
+
+    def kernel(core_ref, x_ref, h_ref, w_hbm, d_hbm, ours_ref, theirs_ref, w_buf, d_buf, full, sems):
+        copies = []
+        for i in range(tiles):
+            place = pl.ds(i * TILE, TILE)
+            copies.append(
+                (
+                    pltpu.make_async_copy(d_hbm.at[:, place], d_buf.at[i], sems.at[0, i]),
+                    pltpu.make_async_copy(w_hbm.at[:, place], w_buf.at[i], sems.at[1, i]),
+                )
+            )
+            for copy in copies[-1]:
+                copy.start()
         hidden = jnp.concatenate(
             [h_ref[s, 16 * t : 16 * t + 16, :] for t in range(2) for s in range(shares)], 0
         )
-        y = jnp.dot(hidden, d_ref[...], preferred_element_type=F32)
-        y = y + jnp.dot(x_ref[...], w_ref[...], preferred_element_type=F32)
-        full_ref[...] = y.T
         mine = core_ref[0]
-        ours_ref[...] = full_ref[pl.ds(pl.multiple_of(mine * half, half), half), :]
-        theirs = full_ref[pl.ds(pl.multiple_of((1 - mine) * half, half), half), :]
-        theirs_ref[...] = theirs.astype(BF16)
+        for i in range(tiles):
+            for copy in copies[i]:
+                copy.wait()
+            y = jnp.dot(hidden, d_buf[i], preferred_element_type=F32)
+            y = y + jnp.dot(x_ref[...], w_buf[i], preferred_element_type=F32)
+            full[...] = y.T
+            rows_i = pl.ds(i * half, half)
+            ours_ref[rows_i, :] = full[pl.ds(pl.multiple_of(mine * half, half), half), :]
+            theirs = full[pl.ds(pl.multiple_of((1 - mine) * half, half), half), :]
+            theirs_ref[rows_i, :] = theirs.astype(BF16)
 
-    half_block = pl.BlockSpec((half, rows), lambda i: (i, 0))
+    in_vmem = pl.BlockSpec(memory_space=pltpu.VMEM)
+    in_hbm = pl.BlockSpec(memory_space=pltpu.HBM)
     return pl.pallas_call(
         kernel,
-        grid=(columns // TILE,),
-        in_specs=[
-            pl.BlockSpec(memory_space=pltpu.SMEM),
-            pl.BlockSpec((rows, depth), lambda i: (0, 0)),
-            pl.BlockSpec((depth, TILE), lambda i: (0, i)),
-            pl.BlockSpec((shares, held, width), lambda i: (0, 0, 0)),
-            pl.BlockSpec((width, TILE), lambda i: (0, i)),
-        ],
-        out_specs=[half_block, half_block],
+        in_specs=[pl.BlockSpec(memory_space=pltpu.SMEM), in_vmem, in_vmem, in_hbm, in_hbm],
+        out_specs=[in_vmem, in_vmem],
         out_shape=[
             jax.ShapeDtypeStruct((columns // 2, rows), F32),
             jax.ShapeDtypeStruct((columns // 2, rows), BF16),
         ],
-        scratch_shapes=[pltpu.VMEM((TILE, rows), F32)],
-        compiler_params=pltpu.CompilerParams(vmem_limit_bytes=16 * 2**20),
+        scratch_shapes=[
+            pltpu.VMEM((tiles, depth, TILE), BF16),
+            pltpu.VMEM((tiles, width, TILE), BF16),
+            pltpu.VMEM((TILE, rows), F32),
+            pltpu.SemaphoreType.DMA((2, tiles)),
+        ],
+        compiler_params=pltpu.CompilerParams(vmem_limit_bytes=51 * 2**20),
         cost_estimate=pl.CostEstimate(
             flops=2 * rows * (depth + width) * columns,
             bytes_accessed=2 * (depth + width) * columns + 3 * rows * columns,
             transcendentals=0,
         ),
-    )(core.reshape(1), x, out_weight, gathered, down_weight)
+    )(core.reshape(1), x, gathered, out_weight, down_weight)
 
 
 def exchange(x, axes):
@@ -68,13 +84,15 @@
 ):
     gx, gyx, core = lax.axis_index("gx"), lax.axis_index("gyx"), lax.axis_index("core")
 
-    spread = jnp.pad(hidden.reshape(32, 288), ((0, 480), (0, 0)))
-    spread = lax.all_gather(spread, "gx", axis=0, tiled=True).reshape(4, 512, 288)[:, :32]
-
     pair = jnp.concatenate([key_cache, value_cache], -1)
+    pair, own = lax.optimization_barrier((pair, hidden))
     pair = lax.ppermute(pair, "core", [(0, 1), (1, 0)])
+    near = lax.ppermute(own, "gx", [(i, i ^ 1) for i in range(4)])
     keys = jnp.concatenate([key_cache, pair[..., :HD]], 1)
     values = jnp.concatenate([value_cache, pair[..., HD:]], 1)
+    keys, near = lax.optimization_barrier((keys, near))
+    near = jnp.where(gx % 2 == 0, jnp.stack([hidden, near]), jnp.stack([near, hidden]))
+    far = lax.ppermute(near, "gx", [(i, i ^ 2) for i in range(4)])
     q = exchange(query.reshape(2, 16, 4, 768).transpose(1, 2, 0, 3), "gz")
     q = lax.dynamic_index_in_dim(q.reshape(4, 2, 2, 4, 2, 768), core, 1, keepdims=False)
     qf = q.reshape(4, 2, 4, 2, 3, HD).transpose(2, 0, 1, 3, 4, 5).reshape(4, 48, HD)
@@ -113,7 +131,9 @@
     attn = attn.reshape(2, 2, 3, HD).transpose(1, 0, 2, 3).reshape(2, 16, 96).transpose(1, 0, 2)
     attn = jnp.broadcast_to(attn[:, None], (16, 4, 2, 96)).reshape(64, 2, 96)
 
-    attn, spread = lax.optimization_barrier((attn, spread))
+    attn, far = lax.optimization_barrier((attn, far))
+    spread = jnp.where(gx < 2, jnp.concatenate([near, far]), jnp.concatenate([far, near]))
+    spread = spread.reshape(4, 32, 288)
 
     mine = exchange(attn, ("gz", "gx")).transpose(1, 0, 2).reshape(128, 96)
     ours, theirs = split_product(core, mine, out_weight, spread, down_weight)

time: 140 us -> 115 us (0.82)
  blocking collectives: 75.5 us -> 33.3 us
  starting transfers between devices: 19.2 us -> 43 us
  between operations: 13.7 us -> 0.36 us
  waiting for transfers between devices: 14.9 us -> 27.2 us
  local copies, waits for them, and re-layouts: 7.86 us -> 3.15 us
  matrix products: 3.12 us -> 0.98 us
    all_to_all x4 -> x2, blocking collectives: 75.5 us -> 33.3 us  [exchange(): return lax.all_to_all(x, axes, split_axis=0, concat_axis=0, tiled=True)]
    all_to_all x1 -> x3, starting transfers between devices: 15.3 us -> 30.4 us  [exchange(): return lax.all_to_all(x, axes, split_axis=0, concat_axis=0, tiled=True)]
    all_to_all x1 -> x3, waiting for transfers between devices: 9.62 us -> 23.6 us  [exchange(): return lax.all_to_all(x, axes, split_axis=0, concat_axis=0, tiled=True)]
    ppermute x0 -> x2, starting transfers between devices: none -> 8.82 us  [the longest x1 5.34 us: per_device(): far = lax.ppermute(near, 'gx', [(i, i ^ 2) for i in range(4)])]
    all_gather x1 -> x0, waiting for transfers between devices: 2.22 us -> none  [per_device(): lax.all_gather(spread, 'gx', axis=0, tiled=True).reshape(4, 512, 288)]
    reshape x1, local copies, waits for them, and re-layouts: 1.58 us -> 0.03 us  [per_device(): message = jnp.concatenate([acc.astype(BF16).reshape(16, 12, HD), stats], 1)]
    pad x1 -> x0, local copies, waits for them, and re-layouts: 1.51 us -> none  [per_device(): spread = jnp.pad(hidden.reshape(32, 288), ((0, 480), (0, 0)))]
  transfers between devices with their start and end apart: 4 -> 7, of which waited for: 4 -> 5; matrix products, arithmetic and copies ran while one was open for 7% -> 2% of each run, Pallas kernels for 0% -> 0%
where the time goes in v4:
time: 115 us
  starting transfers between devices  43 us (37%)
  blocking collectives  33.3 us (29%)
  waiting for transfers between devices  27.2 us (24%)
  other arithmetic  3.44 us (3%)
  Pallas kernels  3.3 us (3%)
  local copies, waits for them, and re-layouts  3.15 us (3%)
    all_to_all x2, blocking collectives, exchange(): return lax.all_to_all(x, axes, split_axis=0, concat_axis=0, tiled=True)  33.3 us
    all_to_all x3, starting transfers between devices, exchange(): return lax.all_to_all(x, axes, split_axis=0, concat_axis=0, tiled=True)  30.4 us
    all_to_all x3, waiting for transfers between devices, exchange(): return lax.all_to_all(x, axes, split_axis=0, concat_axis=0, tiled=True)  23.6 us
    ppermute x1, starting transfers between devices, per_device(): far = lax.ppermute(near, 'gx', [(i, i ^ 2) for i in range(4)])  5.34 us
    ppermute x1, starting transfers between devices, per_device(): near = lax.ppermute(own, 'gx', [(i, i ^ 1) for i in range(4)])  3.48 us
    pallas_call x1, Pallas kernels, split_product(): pl.pallas_call(kernel, in_specs=[pl.BlockSpec(memory_space=pltpu.SMEM), i...  3.3 us
  transfers between devices with their start and end apart: 7, of which 5 were waited for; matrix products, arithmetic and copies ran while one was open for 2% of the time, Pallas kernels for 0%

profile of v4, /device:TPU:32, one launch (start us, length us, event | category | flops | bytes accessed | tf_op | source)
XLA Modules:
  0.0 114.7 jit_solution(1210395632400853066)
XLA Ops:
  0.0 1.8 %copy.41 = bf16[2,64,768]{2,0,1:T(2,128)(2,1)} copy(bf16[2,64,768]{2,1,0:T(8,128)(2,1)} %param.10) | data formatting | bytes 393216 | tf_op jit(solution)/shard_map/reshape | solution.py:96
  1.8 15.2 %all-to-all-start = ((bf16[16,4,2,768]{3,2,1,0:T(2,128)(2,1)}), bf16[16,4,2,768]{3,2,1,0:T(2,128)(2,1)S(1)}, u32[]{:S(2)}, u32[]{:S(2)}) async-start(bf16[16,4,2,768]{3,2,1,0:T(2,128)(2,1)} %bitcast.2), calls=%async_computation | async-start | bytes 393216 | tf_op jit(solution)/shard_map/all_to_all | solution.py:79
  17.1 1.1 pad_maximum_fusion
  18.2 3.5 %collective-permute-start.1 = (bf16[2,16,288]{2,1,0:T(8,128)(2,1)S(1)}, bf16[2,16,288]{2,1,0:T(8,128)(2,1)S(1)}, u32[]{:S(2)}, u32[]{:S(2)}) collective-permute-start(bf16[2,16,288]{2,1,0:T(8,128)(2,1)S(1)} %copy-done.3), channel_id=1, source_target_pairs={{0,128},{128,0},{256,384},{384,256},{1,129},{129,1},{257,385},{385... | collective-permute-start | bytes 55304 | tf_op jit(solution)/shard_map/ppermute | solution.py:90
  21.7 1.9 %collective-permute-start = (bf16[4,128,512]{2,1,0:T(8,128)(2,1)S(1)}, bf16[4,128,512]{2,1,0:T(8,128)(2,1)S(1)}, u32[]{:S(2)}, u32[]{:S(2)}) collective-permute-start(bf16[4,128,512]{2,1,0:T(8,128)(2,1)S(1)} %pad_maximum_fusion), channel_id=1, source_target_pairs={{0,16},{16,0},{1,17},{17,1},{2,18},{18,2},{3,19},{19,3},{4,20},{20... | collective-permute-start | bytes 1572872 | tf_op jit(solution)/shard_map/ppermute | solution.py:89
  23.9 1.6 %collective-permute-done = bf16[4,128,512]{2,1,0:T(8,128)(2,1)S(1)} collective-permute-done((bf16[4,128,512]{2,1,0:T(8,128)(2,1)S(1)}, bf16[4,128,512]{2,1,0:T(8,128)(2,1)S(1)}, u32[]{:S(2)}, u32[]{:S(2)}) %collective-permute-start) | collective-permute-done | bytes 524320 | tf_op jit(solution)/shard_map/ppermute | solution.py:89
  25.6 7.3 %all-to-all-done = bf16[16,4,2,768]{3,2,1,0:T(2,128)(2,1)S(1)} async-done(((bf16[16,4,2,768]{3,2,1,0:T(2,128)(2,1)}), bf16[16,4,2,768]{3,2,1,0:T(2,128)(2,1)S(1)}, u32[]{:S(2)}, u32[]{:S(2)}) %all-to-all-start) | async-done | bytes 196640 | tf_op jit(solution)/shard_map/all_to_all | solution.py:79
  33.1 0.1 fusion.32
  33.2 0.4 fusion.31
  33.6 0.2 convert_reduce_fusion.1
  33.8 0.1 maximum_maximum_fusion
  33.9 0.1 fusion.30
  34.0 0.2 fusion.16
  34.3 0.3 fusion.1
  34.6 0.7 fusion.7
  35.2 7.0 %all-to-all-start.1 = ((bf16[16,16,256]{2,1,0:T(8,128)(2,1)}), bf16[16,16,256]{2,1,0:T(8,128)(2,1)S(1)}, u32[]{:S(2)}, u32[]{:S(2)}) async-start(bf16[16,16,256]{2,1,0:T(8,128)(2,1)} %fusion.7), calls=%async_computation.1 | async-start | bytes 262144 | tf_op jit(solution)/shard_map/all_to_all | solution.py:79
  42.3 5.3 %collective-permute-start.2 = (bf16[2,2,16,288]{3,2,1,0:T(8,128)(2,1)S(1)}, bf16[2,2,16,288]{3,2,1,0:T(8,128)(2,1)S(1)}, u32[]{:S(2)}, u32[]{:S(2)}) collective-permute-start(bf16[2,2,16,288]{3,2,1,0:T(8,128)(2,1)S(1)} %maximum_select_fusion.1), channel_id=1, source_target_pairs={{0,256},{128,384},{256,0},{384,128},{1,257},{129,385},{257,1},{385... | collective-permute-start | bytes 110600 | tf_op jit(solution)/shard_map/ppermute | solution.py:95
  47.7 2.6 %all-to-all-done.1 = bf16[16,16,256]{2,1,0:T(8,128)(2,1)S(1)} async-done(((bf16[16,16,256]{2,1,0:T(8,128)(2,1)}), bf16[16,16,256]{2,1,0:T(8,128)(2,1)S(1)}, u32[]{:S(2)}, u32[]{:S(2)}) %all-to-all-start.1) | async-done | bytes 131104 | tf_op jit(solution)/shard_map/all_to_all | solution.py:79
  50.4 0.1 multiply_reduce_fusion
  50.5 0.1 reshape.221
  50.6 0.6 broadcast_in_dim.61
  51.3 8.1 %all-to-all-start.2 = ((bf16[64,2,96]{2,1,0:T(2,128)(2,1)}), bf16[64,2,96]{2,1,0:T(2,128)(2,1)S(1)}, u32[]{:S(2)}, u32[]{:S(2)}) async-start(bf16[64,2,96]{2,1,0:T(2,128)(2,1)} %bitcast.13), calls=%async_computation.2 | async-start | bytes 65536 | tf_op jit(solution)/shard_map/all_to_all | solution.py:79
  59.4 13.7 %all-to-all-done.2 = bf16[64,2,96]{2,1,0:T(2,128)(2,1)S(1)} async-done(((bf16[64,2,96]{2,1,0:T(2,128)(2,1)}), bf16[64,2,96]{2,1,0:T(2,128)(2,1)S(1)}, u32[]{:S(2)}, u32[]{:S(2)}) %all-to-all-start.2) | async-done | bytes 24608 | tf_op jit(solution)/shard_map/all_to_all | solution.py:79
  73.1 3.3 %shard_map.91 = (f32[2304,128]{1,0:T(8,128)S(1)}, bf16[2304,128]{1,0:T(8,128)(2,1)S(1)}) custom-call(s32[1]{0:T(128)} %bitcast.core_ref, bf16[128,96]{1,0:T(8,128)(2,1)S(1)} %bitcast.42, bf16[4,32,288]{2,1,0:T(8,128)(2,1)S(1)} %maximum_select_fusion.h_ref, bf16[96,4608]{1,0:T(8,128)(2,1)S(1)} %copy-done, bf16[288,4608]{1,0:T(8,128)(2,1)} %d_hbm.1), custom_call_target="tpu_custom_call" | custom-call | flops 452984832 | bytes 5308416 | tf_op jit(solution)/shard_map/pallas_call | solution.py:55
  76.5 1.9 %collective-permute-start.3 = (bf16[2304,128]{1,0:T(8,128)(2,1)S(1)}, bf16[2304,128]{1,0:T(8,128)(2,1)S(1)}, u32[]{:S(2)}, u32[]{:S(2)}) collective-permute-start(bf16[2304,128]{1,0:T(8,128)(2,1)S(1)} %get-tuple-element.20), channel_id=1, source_target_pairs={{0,16},{16,0},{1,17},{17,1},{2,18},{18,2},{3,19},{19,3},{4,20},{20... | collective-permute-start | bytes 1769480 | tf_op jit(solution)/shard_map/ppermute | solution.py:141
  78.4 2.0 %collective-permute-done.3 = bf16[2304,128]{1,0:T(8,128)(2,1)S(1)} collective-permute-done((bf16[2304,128]{1,0:T(8,128)(2,1)S(1)}, bf16[2304,128]{1,0:T(8,128)(2,1)S(1)}, u32[]{:S(2)}, u32[]{:S(2)}) %collective-permute-start.3) | collective-permute-done | bytes 589856 | tf_op jit(solution)/shard_map/ppermute | solution.py:141
  80.4 0.2 add_convert_fusion
  80.5 14.5 %all_to_all.25 = bf16[4,576,128]{2,1,0:T(8,128)(2,1)S(1)} all-to-all(bf16[4,576,128]{2,1,0:T(8,128)(2,1)S(1)} %bitcast.43), channel_id=1, replica_groups=mesh['gx'=4,'gyx'=4,'core'=2,'gz'=16] {'gyx'}, dimensions={0} | all-to-all | bytes 1179648 | tf_op jit(solution)/shard_map/all_to_all | solution.py:79
  95.0 0.1 reduce_sum.61
  95.2 18.8 %all_to_all.26 = bf16[16,36,128]{2,1,0:T(8,128)(2,1)S(1)} all-to-all(bf16[16,36,128]{2,1,0:T(8,128)(2,1)S(1)} %reshape.225), channel_id=1, replica_groups=mesh['gx'=4,'gyx'=4,'core'=2,'gz'=16] {'gz'}, dimensions={0} | all-to-all | bytes 294912 | tf_op jit(solution)/shard_map/all_to_all | solution.py:79
  114.0 0.1 reshape.226
  114.1 0.6 fusion.10
  (48 shorter events, 0.9 us)
Async XLA Ops:
  0.0 18.2 %copy-start.3 = (bf16[2,16,288]{2,1,0:T(8,128)(2,1)S(1)}, bf16[2,16,288]{2,1,0:T(8,128)(2,1)}, u32[]{:S(2)}) copy-start(bf16[2,16,288]{2,1,0:T(8,128)(2,1)} %param.16) | copy-start | bytes 55300
  0.0 23.6 %copy-start.6 = (s32[4]{0:T(128)S(1)}, s32[4]{0:T(128)}, u32[]{:S(2)}) copy-start(s32[4]{0:T(128)} %param.14) | copy-start | bytes 52
  0.0 23.8 %copy-start.5 = (bf16[2,4,512]{2,1,0:T(4,128)(2,1)S(1)}, bf16[2,4,512]{2,1,0:T(4,128)(2,1)}, u32[]{:S(2)}) copy-start(bf16[2,4,512]{2,1,0:T(4,128)(2,1)} %param.11) | copy-start | bytes 24580
  1.8 31.0 %all-to-all-start = ((bf16[16,4,2,768]{3,2,1,0:T(2,128)(2,1)}), bf16[16,4,2,768]{3,2,1,0:T(2,128)(2,1)S(1)}, u32[]{:S(2)}, u32[]{:S(2)}) async-start(bf16[16,4,2,768]{3,2,1,0:T(2,128)(2,1)} %bitcast.2), calls=%async_computation | async-start | bytes 393216 | tf_op jit(solution)/shard_map/all_to_all | solution.py:79
  17.1 8.5 %copy-start.1 = (bf16[4,128,256]{2,1,0:T(8,128)(2,1)S(1)}, bf16[4,128,256]{2,1,0:T(8,128)(2,1)}, u32[]{:S(2)}) copy-start(bf16[4,128,256]{2,1,0:T(8,128)(2,1)} %param.12) | copy-start | bytes 786436
  18.2 7.4 %collective-permute-start.1 = (bf16[2,16,288]{2,1,0:T(8,128)(2,1)S(1)}, bf16[2,16,288]{2,1,0:T(8,128)(2,1)S(1)}, u32[]{:S(2)}, u32[]{:S(2)}) collective-permute-start(bf16[2,16,288]{2,1,0:T(8,128)(2,1)S(1)} %copy-done.3), channel_id=1, source_target_pairs={{0,128},{128,0},{256,384},{384,256},{1,129},{129,1},{257,385},{385... | collective-permute-start | bytes 55304 | tf_op jit(solution)/shard_map/ppermute | solution.py:90
  21.7 3.8 %collective-permute-start = (bf16[4,128,512]{2,1,0:T(8,128)(2,1)S(1)}, bf16[4,128,512]{2,1,0:T(8,128)(2,1)S(1)}, u32[]{:S(2)}, u32[]{:S(2)}) collective-permute-start(bf16[4,128,512]{2,1,0:T(8,128)(2,1)S(1)} %pad_maximum_fusion), channel_id=1, source_target_pairs={{0,16},{16,0},{1,17},{17,1},{2,18},{18,2},{3,19},{19,3},{4,20},{20... | collective-permute-start | bytes 1572872 | tf_op jit(solution)/shard_map/ppermute | solution.py:89
  25.6 8.7 %copy-start.2 = (bf16[4,128,256]{2,1,0:T(8,128)(2,1)S(1)}, bf16[4,128,256]{2,1,0:T(8,128)(2,1)}, u32[]{:S(2)}) copy-start(bf16[4,128,256]{2,1,0:T(8,128)(2,1)} %param.13) | copy-start | bytes 786436
  34.3 38.9 %copy-start = (bf16[96,4608]{1,0:T(8,128)(2,1)S(1)}, bf16[96,4608]{1,0:T(8,128)(2,1)}, u32[]{:S(2)}) copy-start(bf16[96,4608]{1,0:T(8,128)(2,1)} %w_hbm.1) | copy-start | bytes 2654212
  35.2 15.0 %all-to-all-start.1 = ((bf16[16,16,256]{2,1,0:T(8,128)(2,1)}), bf16[16,16,256]{2,1,0:T(8,128)(2,1)S(1)}, u32[]{:S(2)}, u32[]{:S(2)}) async-start(bf16[16,16,256]{2,1,0:T(8,128)(2,1)} %fusion.7), calls=%async_computation.1 | async-start | bytes 262144 | tf_op jit(solution)/shard_map/all_to_all | solution.py:79
  42.3 8.3 %collective-permute-start.2 = (bf16[2,2,16,288]{3,2,1,0:T(8,128)(2,1)S(1)}, bf16[2,2,16,288]{3,2,1,0:T(8,128)(2,1)S(1)}, u32[]{:S(2)}, u32[]{:S(2)}) collective-permute-start(bf16[2,2,16,288]{3,2,1,0:T(8,128)(2,1)S(1)} %maximum_select_fusion.1), channel_id=1, source_target_pairs={{0,256},{128,384},{256,0},{384,128},{1,257},{129,385},{257,1},{385... | collective-permute-start | bytes 110600 | tf_op jit(solution)/shard_map/ppermute | solution.py:95
  51.3 21.9 %all-to-all-start.2 = ((bf16[64,2,96]{2,1,0:T(2,128)(2,1)}), bf16[64,2,96]{2,1,0:T(2,128)(2,1)S(1)}, u32[]{:S(2)}, u32[]{:S(2)}) async-start(bf16[64,2,96]{2,1,0:T(2,128)(2,1)} %bitcast.13), calls=%async_computation.2 | async-start | bytes 65536 | tf_op jit(solution)/shard_map/all_to_all | solution.py:79
  76.5 3.9 %collective-permute-start.3 = (bf16[2304,128]{1,0:T(8,128)(2,1)S(1)}, bf16[2304,128]{1,0:T(8,128)(2,1)S(1)}, u32[]{:S(2)}, u32[]{:S(2)}) collective-permute-start(bf16[2304,128]{1,0:T(8,128)(2,1)S(1)} %get-tuple-element.20), channel_id=1, source_target_pairs={{0,16},{16,0},{1,17},{17,1},{2,18},{18,2},{3,19},{19,3},{4,20},{20... | collective-permute-start | bytes 1769480 | tf_op jit(solution)/shard_map/ppermute | solution.py:141
  80.5 33.5 %copy-start.4 = (bf16[2,64,36]{1,0,2:T(2,128)(2,1)S(1)}, bf16[2,64,36]{1,0,2:T(2,128)(2,1)}, u32[]{:S(2)}) copy-start(bf16[2,64,36]{1,0,2:T(2,128)(2,1)} %param.9) | copy-start | bytes 27652

commit v5 on v3

--- a/solution.py
+++ b/solution.py
@@ -15,48 +15,78 @@
 TILE = 1152
 
 
-def split_product(core, x, out_weight, gathered, down_weight):
-    rows, depth = x.shape
+def turned_product(gathered, w):
     shares, held, width = gathered.shape
-    columns = out_weight.shape[1]
-    half = TILE // 2
+    rows = shares * held
+    columns = w.shape[1]
+    tiles = columns // TILE
 
-    def kernel(core_ref, x_ref, w_ref, h_ref, d_ref, ours_ref, theirs_ref, full_ref):
+    def kernel(h_ref, w_hbm, o_ref, w_buf, sems):
+        copies = []
+        for i in range(tiles):
+            place = pl.ds(i * TILE, TILE)
+            copies.append(pltpu.make_async_copy(w_hbm.at[:, place], w_buf.at[i], sems.at[i]))
+            copies[-1].start()
         hidden = jnp.concatenate(
             [h_ref[s, 16 * t : 16 * t + 16, :] for t in range(2) for s in range(shares)], 0
         )
-        y = jnp.dot(hidden, d_ref[...], preferred_element_type=F32)
-        y = y + jnp.dot(x_ref[...], w_ref[...], preferred_element_type=F32)
-        full_ref[...] = y.T
-        mine = core_ref[0]
-        ours_ref[...] = full_ref[pl.ds(pl.multiple_of(mine * half, half), half), :]
-        theirs = full_ref[pl.ds(pl.multiple_of((1 - mine) * half, half), half), :]
+        for i in range(tiles):
+            copies[i].wait()
+            y = jnp.dot(hidden, w_buf[i], preferred_element_type=F32)
+            o_ref[pl.ds(i * TILE, TILE), :] = y.T
+
+    in_vmem = pl.BlockSpec(memory_space=pltpu.VMEM)
+    return pl.pallas_call(
+        kernel,
+        in_specs=[in_vmem, pl.BlockSpec(memory_space=pltpu.HBM)],
+        out_specs=in_vmem,
+        out_shape=jax.ShapeDtypeStruct((columns, rows), F32),
+        scratch_shapes=[
+            pltpu.VMEM((tiles, width, TILE), BF16),
+            pltpu.SemaphoreType.DMA((tiles,)),
+        ],
+        compiler_params=pltpu.CompilerParams(vmem_limit_bytes=51 * 2**20),
+        cost_estimate=pl.CostEstimate(
+            flops=2 * rows * width * columns,
+            bytes_accessed=2 * width * columns + 4 * rows * columns,
+            transcendentals=0,
+        ),
+    )(gathered, w)
+
+
+def split_product(place, xs, weights, more):
+    many, rows, depth = xs.shape
+    half = TILE // 2
+
+    def kernel(place_ref, x_ref, *refs):
+        w_refs, (more_ref, ours_ref, theirs_ref, full) = refs[:many], refs[many:]
+        chip, mine = place_ref[0], place_ref[1]
+        y = jnp.dot(x_ref[chip], w_refs[0][...], preferred_element_type=F32)
+        for j in range(1, many):
+            x = x_ref[lax.rem(chip + (many - j), many)]
+            y = y + jnp.dot(x, w_refs[j][...], preferred_element_type=F32)
+        full[...] = y.T + more_ref[...]
+        ours_ref[...] = full[pl.ds(pl.multiple_of(mine * half, half), half), :]
+        theirs = full[pl.ds(pl.multiple_of((1 - mine) * half, half), half), :]
         theirs_ref[...] = theirs.astype(BF16)
 
-    half_block = pl.BlockSpec((half, rows), lambda i: (i, 0))
+    in_vmem = pl.BlockSpec(memory_space=pltpu.VMEM)
     return pl.pallas_call(
         kernel,
-        grid=(columns // TILE,),
-        in_specs=[
-            pl.BlockSpec(memory_space=pltpu.SMEM),
-            pl.BlockSpec((rows, depth), lambda i: (0, 0)),
-            pl.BlockSpec((depth, TILE), lambda i: (0, i)),
-            pl.BlockSpec((shares, held, width), lambda i: (0, 0, 0)),
-            pl.BlockSpec((width, TILE), lambda i: (0, i)),
-        ],
-        out_specs=[half_block, half_block],
+        in_specs=[pl.BlockSpec(memory_space=pltpu.SMEM)] + [in_vmem] * (many + 2),
+        out_specs=[in_vmem, in_vmem],
         out_shape=[
-            jax.ShapeDtypeStruct((columns // 2, rows), F32),
-            jax.ShapeDtypeStruct((columns // 2, rows), BF16),
+            jax.ShapeDtypeStruct((half, rows), F32),
+            jax.ShapeDtypeStruct((half, rows), BF16),
         ],
         scratch_shapes=[pltpu.VMEM((TILE, rows), F32)],
         compiler_params=pltpu.CompilerParams(vmem_limit_bytes=16 * 2**20),
         cost_estimate=pl.CostEstimate(
-            flops=2 * rows * (depth + width) * columns,
-            bytes_accessed=2 * (depth + width) * columns + 3 * rows * columns,
+            flops=2 * rows * depth * many * TILE,
+            bytes_accessed=2 * depth * many * TILE + 7 * rows * TILE,
             transcendentals=0,
         ),
-    )(core.reshape(1), x, out_weight, gathered, down_weight)
+    )(place, xs, *weights, more)
 
 
 def exchange(x, axes):
@@ -68,13 +98,17 @@
 ):
     gx, gyx, core = lax.axis_index("gx"), lax.axis_index("gyx"), lax.axis_index("core")
 
-    spread = jnp.pad(hidden.reshape(32, 288), ((0, 480), (0, 0)))
-    spread = lax.all_gather(spread, "gx", axis=0, tiled=True).reshape(4, 512, 288)[:, :32]
-
     pair = jnp.concatenate([key_cache, value_cache], -1)
+    pair, own = lax.optimization_barrier((pair, hidden))
     pair = lax.ppermute(pair, "core", [(0, 1), (1, 0)])
+    near = lax.ppermute(own, "gx", [(i, i ^ 1) for i in range(4)])
     keys = jnp.concatenate([key_cache, pair[..., :HD]], 1)
     values = jnp.concatenate([value_cache, pair[..., HD:]], 1)
+    near = jnp.where(gx % 2 == 0, jnp.stack([hidden, near]), jnp.stack([near, hidden]))
+    far = lax.ppermute(near, "gx", [(i, i ^ 2) for i in range(4)])
+    keys, near, far = lax.optimization_barrier((keys, near, far))
+    spread = jnp.where(gx < 2, jnp.concatenate([near, far]), jnp.concatenate([far, near]))
+    feed = turned_product(spread.reshape(4, 32, 288), down_weight)
     q = exchange(query.reshape(2, 16, 4, 768).transpose(1, 2, 0, 3), "gz")
     q = lax.dynamic_index_in_dim(q.reshape(4, 2, 2, 4, 2, 768), core, 1, keepdims=False)
     qf = q.reshape(4, 2, 4, 2, 3, HD).transpose(2, 0, 1, 3, 4, 5).reshape(4, 48, HD)
@@ -111,17 +145,24 @@
     share = share / jnp.sum(share * totals, 0)
     attn = jnp.sum(message[:, :12].astype(F32) * share[..., None], 0).astype(BF16)
     attn = attn.reshape(2, 2, 3, HD).transpose(1, 0, 2, 3).reshape(2, 16, 96).transpose(1, 0, 2)
-    attn = jnp.broadcast_to(attn[:, None], (16, 4, 2, 96)).reshape(64, 2, 96)
 
-    attn, spread = lax.optimization_barrier((attn, spread))
+    weights = [
+        lax.dynamic_slice_in_dim(out_weight, ((gyx + hop) & 3) * TILE, TILE, 1) for hop in range(4)
+    ]
+    feed_sum = lax.psum_scatter(feed, "gyx", scatter_dimension=0, tiled=True)
+    attn, feed, *weights = lax.optimization_barrier((attn, feed, *weights))
+    for hop in range(1, 4):
+        weights[hop] = lax.ppermute(weights[hop], "gyx", [(i, (i + hop) % 4) for i in range(4)])
 
-    mine = exchange(attn, ("gz", "gx")).transpose(1, 0, 2).reshape(128, 96)
-    ours, theirs = split_product(core, mine, out_weight, spread, down_weight)
+    attn = exchange(jnp.pad(attn, ((0, 0), (0, 14), (0, 160))), "gz")[:, :2, :96]
+    place = jnp.stack([gyx, core])
+    attn, place, *weights = lax.optimization_barrier((attn, place, *weights))
+    attn = exchange(jnp.broadcast_to(attn[None], (16, 16, 2, 96)), ("gx", "gyx"))
+    attn = attn.reshape(4, 4, 16, 2, 96).transpose(1, 3, 2, 0, 4).reshape(4, 128, 96)
+    ours, theirs = split_product(place, attn, weights, feed_sum)
 
     theirs = lax.ppermute(theirs, "core", [(0, 1), (1, 0)])
-    row = (ours + theirs.astype(F32)).astype(BF16).reshape(4, 576, 128)
-    row = exchange(row, "gyx")
-    row = jnp.sum(row.astype(F32), 0).astype(BF16).reshape(16, 36, 128)
+    row = (ours + theirs.astype(F32)).astype(BF16).reshape(16, 36, 128)
     column = exchange(row, "gz")
     summed = jnp.sum(column.astype(F32), 0).reshape(36, 2, 64).transpose(1, 2, 0)
     return (summed + resid.astype(F32)).astype(BF16)

time: 140 us -> 148 us (1.057)
  starting transfers between devices: 19.2 us -> 55.7 us
  blocking collectives: 75.5 us -> 40.4 us
  waiting for transfers between devices: 14.9 us -> 20.9 us
  Pallas kernels: 2.47 us -> 5.45 us
  local copies, waits for them, and re-layouts: 7.86 us -> 5.22 us
  other arithmetic: 2.5 us -> 4.75 us
  matrix products: 3.12 us -> 0.97 us
    all_to_all x4 -> x2, blocking collectives: 75.5 us -> 40.4 us  [exchange(): return lax.all_to_all(x, axes, split_axis=0, concat_axis=0, tiled=True)]
    all_to_all x1 -> x3, starting transfers between devices: 15.3 us -> 34 us  [exchange(): return lax.all_to_all(x, axes, split_axis=0, concat_axis=0, tiled=True)]
    ppermute x0 -> x5, starting transfers between devices: none -> 17.8 us  [the longest x3 9.54 us: per_device(): lax.ppermute(weights[hop], 'gyx', [(i, (i + hop) % 4) for i in range(4)])]
    ppermute x0 -> x5, waiting for transfers between devices: none -> 8.86 us  [the longest x3 6.24 us: per_device(): lax.ppermute(weights[hop], 'gyx', [(i, (i + hop) % 4) for i in range(4)])]
    pallas_call x1 -> x2, Pallas kernels: 2.47 us -> 5.45 us  [the longest x1 4.27 us: turned_product(): pl.pallas_call(kernel, in_specs=[in_vmem, pl.BlockSpec(memory_space=pltpu...]
    all_gather x1 -> x0, waiting for transfers between devices: 2.22 us -> none  [per_device(): lax.all_gather(spread, 'gx', axis=0, tiled=True).reshape(4, 512, 288)]
    reshape x1, local copies, waits for them, and re-layouts: 1.58 us -> 0.03 us  [per_device(): message = jnp.concatenate([acc.astype(BF16).reshape(16, 12, HD), stats], 1)]
    all_to_all x1 -> x3, waiting for transfers between devices: 9.62 us -> 10.6 us  [exchange(): return lax.all_to_all(x, axes, split_axis=0, concat_axis=0, tiled=True)]
  transfers between devices with their start and end apart: 4 -> 11, of which waited for: 4 -> 6; matrix products, arithmetic and copies ran while one was open for 7% -> 5% of each run, Pallas kernels for 0% -> 3%
where the time goes in v5:
time: 148 us; the launch traced here: 147 us
  starting transfers between devices  55.7 us (38%)
  blocking collectives  40.4 us (27%)
  waiting for transfers between devices  20.9 us (14%)
  between operations  13.8 us (9%)
  Pallas kernels  5.45 us (4%)
  local copies, waits for them, and re-layouts  5.22 us (4%)
  other arithmetic  4.75 us (3%)
    all_to_all x2, blocking collectives, exchange(): return lax.all_to_all(x, axes, split_axis=0, concat_axis=0, tiled=True)  40.4 us
    all_to_all x3, starting transfers between devices, exchange(): return lax.all_to_all(x, axes, split_axis=0, concat_axis=0, tiled=True)  34 us
    all_to_all x3, waiting for transfers between devices, exchange(): return lax.all_to_all(x, axes, split_axis=0, concat_axis=0, tiled=True)  10.6 us
    ppermute x3, starting transfers between devices, per_device(): lax.ppermute(weights[hop], 'gyx', [(i, (i + hop) % 4) for i in range(4)])  9.54 us
    ppermute x3, waiting for transfers between devices, per_device(): lax.ppermute(weights[hop], 'gyx', [(i, (i + hop) % 4) for i in range(4)])  6.24 us
    ppermute x1, starting transfers between devices, per_device(): far = lax.ppermute(near, 'gx', [(i, i ^ 2) for i in range(4)])  4.81 us
    pallas_call x1, Pallas kernels, turned_product(): pl.pallas_call(kernel, in_specs=[in_vmem, pl.BlockSpec(memory_space=pltpu...  4.27 us
    ppermute x1, starting transfers between devices, per_device(): near = lax.ppermute(own, 'gx', [(i, i ^ 1) for i in range(4)])  3.49 us
  transfers between devices with their start and end apart: 11, of which 6 were waited for; matrix products, arithmetic and copies ran while one was open for 5% of the time, Pallas kernels for 3%

profile of v5, /device:TPU:32, one launch (start us, length us, event | category | flops | bytes accessed | tf_op | source)
XLA Modules:
  0.0 147.1 jit_solution(15752684614169063170)
XLA Ops:
  6.5 1.9 %copy.45 = bf16[2,64,768]{2,0,1:T(2,128)(2,1)} copy(bf16[2,64,768]{2,1,0:T(8,128)(2,1)} %param.10) | data formatting | bytes 393216 | tf_op jit(solution)/shard_map/reshape | solution.py:112
  8.4 15.2 %all-to-all-start = ((bf16[16,4,2,768]{3,2,1,0:T(2,128)(2,1)}), bf16[16,4,2,768]{3,2,1,0:T(2,128)(2,1)S(1)}, u32[]{:S(2)}, u32[]{:S(2)}) async-start(bf16[16,4,2,768]{3,2,1,0:T(2,128)(2,1)} %bitcast.1), calls=%async_computation | async-start | bytes 393216 | tf_op jit(solution)/shard_map/all_to_all | solution.py:93
  23.7 1.1 pad_maximum_fusion
  24.7 3.5 %collective-permute-start.1 = (bf16[2,16,288]{2,1,0:T(8,128)(2,1)}, bf16[2,16,288]{2,1,0:T(8,128)(2,1)S(1)}, u32[]{:S(2)}, u32[]{:S(2)}) collective-permute-start(bf16[2,16,288]{2,1,0:T(8,128)(2,1)} %param.16), channel_id=1, source_target_pairs={{0,128},{128,0},{256,384},{384,256},{1,129},{129,1},{257,385},{385... | collective-permute-start | bytes 55304 | tf_op jit(solution)/shard_map/ppermute | solution.py:104
  28.2 1.9 %collective-permute-start = (bf16[4,128,512]{2,1,0:T(8,128)(2,1)S(1)}, bf16[4,128,512]{2,1,0:T(8,128)(2,1)S(1)}, u32[]{:S(2)}, u32[]{:S(2)}) collective-permute-start(bf16[4,128,512]{2,1,0:T(8,128)(2,1)S(1)} %pad_maximum_fusion), channel_id=1, source_target_pairs={{0,16},{16,0},{1,17},{17,1},{2,18},{18,2},{3,19},{19,3},{4,20},{20... | collective-permute-start | bytes 1572872 | tf_op jit(solution)/shard_map/ppermute | solution.py:103
  30.2 0.7 broadcast_compare_fusion
  30.9 0.7 fusion.29
  31.7 0.8 maximum_select_fusion.1
  32.6 4.8 %collective-permute-start.2 = (bf16[2,2,16,288]{3,2,1,0:T(8,128)(2,1)S(1)}, bf16[2,2,16,288]{3,2,1,0:T(8,128)(2,1)S(1)}, u32[]{:S(2)}, u32[]{:S(2)}) collective-permute-start(bf16[2,2,16,288]{3,2,1,0:T(8,128)(2,1)S(1)} %maximum_select_fusion.1), channel_id=1, source_target_pairs={{0,256},{128,384},{256,0},{384,128},{1,257},{129,385},{257,1},{385... | collective-permute-start | bytes 110600 | tf_op jit(solution)/shard_map/ppermute | solution.py:108
  37.5 2.6 %collective-permute-done.2 = bf16[2,2,16,288]{3,2,1,0:T(8,128)(2,1)S(1)} collective-permute-done((bf16[2,2,16,288]{3,2,1,0:T(8,128)(2,1)S(1)}, bf16[2,2,16,288]{3,2,1,0:T(8,128)(2,1)S(1)}, u32[]{:S(2)}, u32[]{:S(2)}) %collective-permute-start.2) | collective-permute-done | bytes 36896 | tf_op jit(solution)/shard_map/ppermute | solution.py:108
  40.1 4.3 %shard_map.91 = f32[4608,128]{1,0:T(8,128)} custom-call(bf16[4,32,288]{2,1,0:T(8,128)(2,1)S(1)} %maximum_select_fusion.h_ref, bf16[288,4608]{1,0:T(8,128)(2,1)} %w_hbm.1), custom_call_target="tpu_custom_call" | custom-call | flops 339738624 | bytes 5013504 | tf_op jit(solution)/shard_map/pallas_call | solution.py:39
  44.9 0.4 fusion.31
  45.7 0.2 fusion.16
  45.9 0.3 fusion.1
  46.2 0.7 fusion.7
  46.9 6.7 %all-to-all-start.1 = ((bf16[16,16,256]{2,1,0:T(8,128)(2,1)}), bf16[16,16,256]{2,1,0:T(8,128)(2,1)S(1)}, u32[]{:S(2)}, u32[]{:S(2)}) async-start(bf16[16,16,256]{2,1,0:T(8,128)(2,1)} %fusion.7), calls=%async_computation.1 | async-start | bytes 262144 | tf_op jit(solution)/shard_map/all_to_all | solution.py:93
  53.8 7.9 %all-to-all-done.1 = bf16[16,16,256]{2,1,0:T(8,128)(2,1)S(1)} async-done(((bf16[16,16,256]{2,1,0:T(8,128)(2,1)}), bf16[16,16,256]{2,1,0:T(8,128)(2,1)S(1)}, u32[]{:S(2)}, u32[]{:S(2)}) %all-to-all-start.1) | async-done | bytes 131104 | tf_op jit(solution)/shard_map/all_to_all | solution.py:93
  62.0 0.7 pad.9.clone
  62.7 12.0 %all-to-all-start.2 = ((bf16[16,16,256]{2,1,0:T(8,128)(2,1)}), bf16[16,16,256]{2,1,0:T(8,128)(2,1)S(1)}, u32[]{:S(2)}, u32[]{:S(2)}) async-start(bf16[16,16,256]{2,1,0:T(8,128)(2,1)} %pad.9.clone), calls=%async_computation.2 | async-start | bytes 262144 | tf_op jit(solution)/shard_map/all_to_all | solution.py:93
  74.7 2.5 %collective-permute-start.3 = (bf16[96,1152]{1,0:T(8,128)(2,1)S(1)}, bf16[96,1152]{1,0:T(8,128)(2,1)S(1)}, u32[]{:S(2)}, u32[]{:S(2)}) collective-permute-start(bf16[96,1152]{1,0:T(8,128)(2,1)S(1)} %get-tuple-element.30), channel_id=1, source_target_pairs={{0,32},{32,64},{64,96},{96,0},{1,33},{33,65},{65,97},{97,1},{2,34}... | collective-permute-start | bytes 663560 | tf_op jit(solution)/shard_map/ppermute | solution.py:155
  77.2 3.7 %collective-permute-start.4 = (bf16[96,1152]{1,0:T(8,128)(2,1)S(1)}, bf16[96,1152]{1,0:T(8,128)(2,1)S(1)}, u32[]{:S(2)}, u32[]{:S(2)}) collective-permute-start(bf16[96,1152]{1,0:T(8,128)(2,1)S(1)} %get-tuple-element.31), channel_id=1, source_target_pairs={{0,64},{32,96},{64,0},{96,32},{1,65},{33,97},{65,1},{97,33},{2,66}... | collective-permute-start | bytes 663560 | tf_op jit(solution)/shard_map/ppermute | solution.py:155
  80.9 3.3 %collective-permute-start.5 = (bf16[96,1152]{1,0:T(8,128)(2,1)S(1)}, bf16[96,1152]{1,0:T(8,128)(2,1)S(1)}, u32[]{:S(2)}, u32[]{:S(2)}) collective-permute-start(bf16[96,1152]{1,0:T(8,128)(2,1)S(1)} %get-tuple-element.32), channel_id=1, source_target_pairs={{0,96},{32,0},{64,32},{96,64},{1,97},{33,1},{65,33},{97,65},{2,98}... | collective-permute-start | bytes 663560 | tf_op jit(solution)/shard_map/ppermute | solution.py:155
  84.4 2.8 %all-to-all-done.2 = bf16[16,16,256]{2,1,0:T(8,128)(2,1)S(1)} async-done(((bf16[16,16,256]{2,1,0:T(8,128)(2,1)}), bf16[16,16,256]{2,1,0:T(8,128)(2,1)S(1)}, u32[]{:S(2)}, u32[]{:S(2)}) %all-to-all-start.2) | async-done | bytes 131104 | tf_op jit(solution)/shard_map/all_to_all | solution.py:93
  87.1 2.1 %collective-permute-done.3.refs_1_ = bf16[96,1152]{1,0:T(8,128)(2,1)S(1)} collective-permute-done((bf16[96,1152]{1,0:T(8,128)(2,1)S(1)}, bf16[96,1152]{1,0:T(8,128)(2,1)S(1)}, u32[]{:S(2)}, u32[]{:S(2)}) %collective-permute-start.3) | collective-permute-done | bytes 221216 | tf_op jit(solution)/shard_map/ppermute | solution.py:155
  89.2 4.2 %collective-permute-done.4.refs_2_ = bf16[96,1152]{1,0:T(8,128)(2,1)S(1)} collective-permute-done((bf16[96,1152]{1,0:T(8,128)(2,1)S(1)}, bf16[96,1152]{1,0:T(8,128)(2,1)S(1)}, u32[]{:S(2)}, u32[]{:S(2)}) %collective-permute-start.4) | collective-permute-done | bytes 221216 | tf_op jit(solution)/shard_map/ppermute | solution.py:155
  93.4 12.8 %all_to_all.25 = bf16[16,16,2,96]{3,1,2,0:T(8,128)(2,1)S(1)} all-to-all(bf16[16,16,2,96]{3,1,2,0:T(8,128)(2,1)S(1)} %broadcast_in_dim.61), channel_id=1, replica_groups=mesh['gx'=4,'gyx'=4,'core'=2,'gz'=16] {'gx','gyx'}, dimensions={0} | all-to-all | bytes 196608 | tf_op jit(solution)/shard_map/all_to_all | solution.py:93
  106.3 1.1 copy-done
  107.4 1.2 shard_map.92
  108.6 1.9 %collective-permute-start.6 = (bf16[576,128]{1,0:T(8,128)(2,1)S(1)}, bf16[576,128]{1,0:T(8,128)(2,1)S(1)}, u32[]{:S(2)}, u32[]{:S(2)}) collective-permute-start(bf16[576,128]{1,0:T(8,128)(2,1)S(1)} %get-tuple-element.40), channel_id=1, source_target_pairs={{0,16},{16,0},{1,17},{17,1},{2,18},{18,2},{3,19},{19,3},{4,20},{20... | collective-permute-start | bytes 442376 | tf_op jit(solution)/shard_map/ppermute | solution.py:164
  110.5 1.3 collective-permute-done.6
  111.9 27.6 %all_to_all.26 = bf16[16,36,128]{2,1,0:T(8,128)(2,1)S(1)} all-to-all(bf16[16,36,128]{2,1,0:T(8,128)(2,1)S(1)} %reshape.209), channel_id=1, replica_groups=mesh['gx'=4,'gyx'=4,'core'=2,'gz'=16] {'gz'}, dimensions={0} | all-to-all | bytes 294912 | tf_op jit(solution)/shard_map/all_to_all | solution.py:93
  139.6 0.6 fusion.10
  (57 shorter events, 1.9 us)
Async XLA Ops:
  6.5 30.9 %copy-start.1 = (bf16[4,128,256]{2,1,0:T(8,128)(2,1)S(1)}, bf16[4,128,256]{2,1,0:T(8,128)(2,1)}, u32[]{:S(2)}) copy-start(bf16[4,128,256]{2,1,0:T(8,128)(2,1)} %param.12) | copy-start | bytes 786436
  8.4 36.1 %all-to-all-start = ((bf16[16,4,2,768]{3,2,1,0:T(2,128)(2,1)}), bf16[16,4,2,768]{3,2,1,0:T(2,128)(2,1)S(1)}, u32[]{:S(2)}, u32[]{:S(2)}) async-start(bf16[16,4,2,768]{3,2,1,0:T(2,128)(2,1)} %bitcast.1), calls=%async_computation | async-start | bytes 393216 | tf_op jit(solution)/shard_map/all_to_all | solution.py:93
  23.6 82.7 %reduce-scatter.2.cloned.1.call-start = ((), (), s32[]{:S(2)}) async-start(), calls=%async_computation.6 | async-start | bytes 2949120 | tf_op jit(solution)/shard_map/reduce_scatter | solution.py:152
  24.7 7.0 %collective-permute-start.1 = (bf16[2,16,288]{2,1,0:T(8,128)(2,1)}, bf16[2,16,288]{2,1,0:T(8,128)(2,1)S(1)}, u32[]{:S(2)}, u32[]{:S(2)}) collective-permute-start(bf16[2,16,288]{2,1,0:T(8,128)(2,1)} %param.16), channel_id=1, source_target_pairs={{0,128},{128,0},{256,384},{384,256},{1,129},{129,1},{257,385},{385... | collective-permute-start | bytes 55304 | tf_op jit(solution)/shard_map/ppermute | solution.py:104
  28.2 9.2 %collective-permute-start = (bf16[4,128,512]{2,1,0:T(8,128)(2,1)S(1)}, bf16[4,128,512]{2,1,0:T(8,128)(2,1)S(1)}, u32[]{:S(2)}, u32[]{:S(2)}) collective-permute-start(bf16[4,128,512]{2,1,0:T(8,128)(2,1)S(1)} %pad_maximum_fusion), channel_id=1, source_target_pairs={{0,16},{16,0},{1,17},{17,1},{2,18},{18,2},{3,19},{19,3},{4,20},{20... | collective-permute-start | bytes 1572872 | tf_op jit(solution)/shard_map/ppermute | solution.py:103
  32.6 7.5 %collective-permute-start.2 = (bf16[2,2,16,288]{3,2,1,0:T(8,128)(2,1)S(1)}, bf16[2,2,16,288]{3,2,1,0:T(8,128)(2,1)S(1)}, u32[]{:S(2)}, u32[]{:S(2)}) collective-permute-start(bf16[2,2,16,288]{3,2,1,0:T(8,128)(2,1)S(1)} %maximum_select_fusion.1), channel_id=1, source_target_pairs={{0,256},{128,384},{256,0},{384,128},{1,257},{129,385},{257,1},{385... | collective-permute-start | bytes 110600 | tf_op jit(solution)/shard_map/ppermute | solution.py:108
  44.4 1.5 %copy-start.3 = (bf16[4,128,256]{2,1,0:T(8,128)(2,1)S(1)}, bf16[4,128,256]{2,1,0:T(8,128)(2,1)}, u32[]{:S(2)}) copy-start(bf16[4,128,256]{2,1,0:T(8,128)(2,1)} %param.13) | copy-start | bytes 786436
  44.4 9.2 %copy-start.2 = (bf16[96,4608]{1,0:T(8,128)(2,1)S(1)}, bf16[96,4608]{1,0:T(8,128)(2,1)}, u32[]{:S(2)}) copy-start(bf16[96,4608]{1,0:T(8,128)(2,1)} %param.15) | copy-start | bytes 2654212
  46.9 14.7 %all-to-all-start.1 = ((bf16[16,16,256]{2,1,0:T(8,128)(2,1)}), bf16[16,16,256]{2,1,0:T(8,128)(2,1)S(1)}, u32[]{:S(2)}, u32[]{:S(2)}) async-start(bf16[16,16,256]{2,1,0:T(8,128)(2,1)} %fusion.7), calls=%async_computation.1 | async-start | bytes 262144 | tf_op jit(solution)/shard_map/all_to_all | solution.py:93
  53.8 85.9 %copy-start.4 = (bf16[2,64,36]{1,0,2:T(2,128)(2,1)S(1)}, bf16[2,64,36]{1,0,2:T(2,128)(2,1)}, u32[]{:S(2)}) copy-start(bf16[2,64,36]{1,0,2:T(2,128)(2,1)} %param.9) | copy-start | bytes 27652
  62.7 24.4 %all-to-all-start.2 = ((bf16[16,16,256]{2,1,0:T(8,128)(2,1)}), bf16[16,16,256]{2,1,0:T(8,128)(2,1)S(1)}, u32[]{:S(2)}, u32[]{:S(2)}) async-start(bf16[16,16,256]{2,1,0:T(8,128)(2,1)} %pad.9.clone), calls=%async_computation.2 | async-start | bytes 262144 | tf_op jit(solution)/shard_map/all_to_all | solution.py:93
  74.7 14.5 %collective-permute-start.3 = (bf16[96,1152]{1,0:T(8,128)(2,1)S(1)}, bf16[96,1152]{1,0:T(8,128)(2,1)S(1)}, u32[]{:S(2)}, u32[]{:S(2)}) collective-permute-start(bf16[96,1152]{1,0:T(8,128)(2,1)S(1)} %get-tuple-element.30), channel_id=1, source_target_pairs={{0,32},{32,64},{64,96},{96,0},{1,33},{33,65},{65,97},{97,1},{2,34}... | collective-permute-start | bytes 663560 | tf_op jit(solution)/shard_map/ppermute | solution.py:155
  77.2 16.2 %collective-permute-start.4 = (bf16[96,1152]{1,0:T(8,128)(2,1)S(1)}, bf16[96,1152]{1,0:T(8,128)(2,1)S(1)}, u32[]{:S(2)}, u32[]{:S(2)}) collective-permute-start(bf16[96,1152]{1,0:T(8,128)(2,1)S(1)} %get-tuple-element.31), channel_id=1, source_target_pairs={{0,64},{32,96},{64,0},{96,32},{1,65},{33,97},{65,1},{97,33},{2,66}... | collective-permute-start | bytes 663560 | tf_op jit(solution)/shard_map/ppermute | solution.py:155
  80.9 12.4 %collective-permute-start.5 = (bf16[96,1152]{1,0:T(8,128)(2,1)S(1)}, bf16[96,1152]{1,0:T(8,128)(2,1)S(1)}, u32[]{:S(2)}, u32[]{:S(2)}) collective-permute-start(bf16[96,1152]{1,0:T(8,128)(2,1)S(1)} %get-tuple-element.32), channel_id=1, source_target_pairs={{0,96},{32,0},{64,32},{96,64},{1,97},{33,1},{65,33},{97,65},{2,98}... | collective-permute-start | bytes 663560 | tf_op jit(solution)/shard_map/ppermute | solution.py:155
  106.3 1.1 copy-start
  108.6 3.3 %collective-permute-start.6 = (bf16[576,128]{1,0:T(8,128)(2,1)S(1)}, bf16[576,128]{1,0:T(8,128)(2,1)S(1)}, u32[]{:S(2)}, u32[]{:S(2)}) collective-permute-start(bf16[576,128]{1,0:T(8,128)(2,1)S(1)} %get-tuple-element.40), channel_id=1, source_target_pairs={{0,16},{16,0},{1,17},{17,1},{2,18},{18,2},{3,19},{19,3},{4,20},{20... | collective-permute-start | bytes 442376 | tf_op jit(solution)/shard_map/ppermute | solution.py:164
Sparse Core Ops, SparseCore 0:
  44.6 44.7 reduce-scatter.1

commit v6 on v5

--- a/solution.py
+++ b/solution.py
@@ -54,39 +54,39 @@
     )(gathered, w)
 
 
-def split_product(place, xs, weights, more):
-    many, rows, depth = xs.shape
+def split_product(core, x, w, more):
+    rows, depth = x.shape
+    columns = w.shape[1]
     half = TILE // 2
 
-    def kernel(place_ref, x_ref, *refs):
-        w_refs, (more_ref, ours_ref, theirs_ref, full) = refs[:many], refs[many:]
-        chip, mine = place_ref[0], place_ref[1]
-        y = jnp.dot(x_ref[chip], w_refs[0][...], preferred_element_type=F32)
-        for j in range(1, many):
-            x = x_ref[lax.rem(chip + (many - j), many)]
-            y = y + jnp.dot(x, w_refs[j][...], preferred_element_type=F32)
-        full[...] = y.T + more_ref[...]
-        ours_ref[...] = full[pl.ds(pl.multiple_of(mine * half, half), half), :]
-        theirs = full[pl.ds(pl.multiple_of((1 - mine) * half, half), half), :]
-        theirs_ref[...] = theirs.astype(BF16)
+    def kernel(core_ref, x_ref, w_ref, more_ref, ours_ref, theirs_ref, full):
+        mine = core_ref[0]
+        for i in range(columns // TILE):
+            place = pl.ds(i * TILE, TILE)
+            y = jnp.dot(x_ref[...], w_ref[:, place], preferred_element_type=F32)
+            full[...] = y.T + more_ref[place, :]
+            rows_i = pl.ds(i * half, half)
+            ours_ref[rows_i, :] = full[pl.ds(pl.multiple_of(mine * half, half), half), :]
+            theirs = full[pl.ds(pl.multiple_of((1 - mine) * half, half), half), :]
+            theirs_ref[rows_i, :] = theirs.astype(BF16)
 
     in_vmem = pl.BlockSpec(memory_space=pltpu.VMEM)
     return pl.pallas_call(
         kernel,
-        in_specs=[pl.BlockSpec(memory_space=pltpu.SMEM)] + [in_vmem] * (many + 2),
+        in_specs=[pl.BlockSpec(memory_space=pltpu.SMEM), in_vmem, in_vmem, in_vmem],
         out_specs=[in_vmem, in_vmem],
         out_shape=[
-            jax.ShapeDtypeStruct((half, rows), F32),
-            jax.ShapeDtypeStruct((half, rows), BF16),
+            jax.ShapeDtypeStruct((columns // 2, rows), F32),
+            jax.ShapeDtypeStruct((columns // 2, rows), BF16),
         ],
         scratch_shapes=[pltpu.VMEM((TILE, rows), F32)],
         compiler_params=pltpu.CompilerParams(vmem_limit_bytes=16 * 2**20),
         cost_estimate=pl.CostEstimate(
-            flops=2 * rows * depth * many * TILE,
-            bytes_accessed=2 * depth * many * TILE + 7 * rows * TILE,
+            flops=2 * rows * depth * columns,
+            bytes_accessed=2 * depth * columns + 7 * rows * columns,
             transcendentals=0,
         ),
-    )(place, xs, *weights, more)
+    )(core.reshape(1), x, w, more)
 
 
 def exchange(x, axes):
@@ -104,11 +104,9 @@
     near = lax.ppermute(own, "gx", [(i, i ^ 1) for i in range(4)])
     keys = jnp.concatenate([key_cache, pair[..., :HD]], 1)
     values = jnp.concatenate([value_cache, pair[..., HD:]], 1)
+    keys, near = lax.optimization_barrier((keys, near))
     near = jnp.where(gx % 2 == 0, jnp.stack([hidden, near]), jnp.stack([near, hidden]))
     far = lax.ppermute(near, "gx", [(i, i ^ 2) for i in range(4)])
-    keys, near, far = lax.optimization_barrier((keys, near, far))
-    spread = jnp.where(gx < 2, jnp.concatenate([near, far]), jnp.concatenate([far, near]))
-    feed = turned_product(spread.reshape(4, 32, 288), down_weight)
     q = exchange(query.reshape(2, 16, 4, 768).transpose(1, 2, 0, 3), "gz")
     q = lax.dynamic_index_in_dim(q.reshape(4, 2, 2, 4, 2, 768), core, 1, keepdims=False)
     qf = q.reshape(4, 2, 4, 2, 3, HD).transpose(2, 0, 1, 3, 4, 5).reshape(4, 48, HD)
@@ -145,24 +143,18 @@
     share = share / jnp.sum(share * totals, 0)
     attn = jnp.sum(message[:, :12].astype(F32) * share[..., None], 0).astype(BF16)
     attn = attn.reshape(2, 2, 3, HD).transpose(1, 0, 2, 3).reshape(2, 16, 96).transpose(1, 0, 2)
+    attn = jnp.broadcast_to(attn[:, None], (16, 4, 2, 96)).reshape(64, 2, 96)
 
-    weights = [
-        lax.dynamic_slice_in_dim(out_weight, ((gyx + hop) & 3) * TILE, TILE, 1) for hop in range(4)
-    ]
-    feed_sum = lax.psum_scatter(feed, "gyx", scatter_dimension=0, tiled=True)
-    attn, feed, *weights = lax.optimization_barrier((attn, feed, *weights))
-    for hop in range(1, 4):
-        weights[hop] = lax.ppermute(weights[hop], "gyx", [(i, (i + hop) % 4) for i in range(4)])
+    spread = jnp.where(gx < 2, jnp.concatenate([near, far]), jnp.concatenate([far, near]))
+    feed = turned_product(spread.reshape(4, 32, 288), down_weight)
 
-    attn = exchange(jnp.pad(attn, ((0, 0), (0, 14), (0, 160))), "gz")[:, :2, :96]
-    place = jnp.stack([gyx, core])
-    attn, place, *weights = lax.optimization_barrier((attn, place, *weights))
-    attn = exchange(jnp.broadcast_to(attn[None], (16, 16, 2, 96)), ("gx", "gyx"))
-    attn = attn.reshape(4, 4, 16, 2, 96).transpose(1, 3, 2, 0, 4).reshape(4, 128, 96)
-    ours, theirs = split_product(place, attn, weights, feed_sum)
+    mine = exchange(attn, ("gz", "gx")).transpose(1, 0, 2).reshape(128, 96)
+    ours, theirs = split_product(core, mine, out_weight, feed)
 
     theirs = lax.ppermute(theirs, "core", [(0, 1), (1, 0)])
-    row = (ours + theirs.astype(F32)).astype(BF16).reshape(16, 36, 128)
+    row = (ours + theirs.astype(F32)).astype(BF16).reshape(4, 576, 128)
+    row = exchange(row, "gyx")
+    row = jnp.sum(row.astype(F32), 0).astype(BF16).reshape(16, 36, 128)
     column = exchange(row, "gz")
     summed = jnp.sum(column.astype(F32), 0).reshape(36, 2, 64).transpose(1, 2, 0)
     return (summed + resid.astype(F32)).astype(BF16)

time: 148 us -> 110 us (0.74)
  starting transfers between devices: 55.7 us -> 41.4 us
  between operations: 13.8 us -> 0.37 us
  blocking collectives: 40.4 us -> 31.9 us
  waiting for transfers between devices: 20.9 us -> 24.2 us
  local copies, waits for them, and re-layouts: 5.22 us -> 3.15 us
  Pallas kernels: 5.45 us -> 3.89 us
    all_to_all x3, waiting for transfers between devices: 10.6 us -> 20.6 us  [exchange(): return lax.all_to_all(x, axes, split_axis=0, concat_axis=0, tiled=True)]
    ppermute x3 -> x0, starting transfers between devices: 9.54 us -> none  [per_device(): lax.ppermute(weights[hop], 'gyx', [(i, (i + hop) % 4) for i in range(4)])]
    all_to_all x2, blocking collectives: 40.4 us -> 31.9 us  [exchange(): return lax.all_to_all(x, axes, split_axis=0, concat_axis=0, tiled=True)]
    ppermute x3 -> x0, waiting for transfers between devices: 6.24 us -> none  [per_device(): lax.ppermute(weights[hop], 'gyx', [(i, (i + hop) % 4) for i in range(4)])]
    all_to_all x3, starting transfers between devices: 34 us -> 28.8 us  [exchange(): return lax.all_to_all(x, axes, split_axis=0, concat_axis=0, tiled=True)]
    ppermute x1, waiting for transfers between devices: 2.62 us -> 0.01 us  [per_device(): far = lax.ppermute(near, 'gx', [(i, i ^ 2) for i in range(4)])]
    ppermute x1, waiting for transfers between devices: 0.01 us -> 1.63 us  [per_device(): pair = lax.ppermute(pair, 'core', [(0, 1), (1, 0)])]
  transfers between devices with their start and end apart: 11 -> 7, of which waited for: 6 -> 5; matrix products, arithmetic and copies ran while one was open for 5% -> 2% of each run, Pallas kernels for 3% -> 3%
where the time goes in v6:
time: 110 us; the launch traced here: 109 us
  starting transfers between devices  41.4 us (38%)
  blocking collectives  31.9 us (29%)
  waiting for transfers between devices  24.2 us (22%)
  Pallas kernels  3.89 us (4%)
  other arithmetic  3.44 us (3%)
  local copies, waits for them, and re-layouts  3.15 us (3%)
    all_to_all x2, blocking collectives, exchange(): return lax.all_to_all(x, axes, split_axis=0, concat_axis=0, tiled=True)  31.9 us
    all_to_all x3, starting transfers between devices, exchange(): return lax.all_to_all(x, axes, split_axis=0, concat_axis=0, tiled=True)  28.8 us
    all_to_all x3, waiting for transfers between devices, exchange(): return lax.all_to_all(x, axes, split_axis=0, concat_axis=0, tiled=True)  20.6 us
    ppermute x1, starting transfers between devices, per_device(): far = lax.ppermute(near, 'gx', [(i, i ^ 2) for i in range(4)])  5.34 us
    ppermute x1, starting transfers between devices, per_device(): near = lax.ppermute(own, 'gx', [(i, i ^ 1) for i in range(4)])  3.48 us
    pallas_call x1, Pallas kernels, turned_product(): pl.pallas_call(kernel, in_specs=[in_vmem, pl.BlockSpec(memory_space=pltpu...  2.92 us
  transfers between devices with their start and end apart: 7, of which 5 were waited for; matrix products, arithmetic and copies ran while one was open for 2% of the time, Pallas kernels for 3%

profile of v6, /device:TPU:32, one launch (start us, length us, event | category | flops | bytes accessed | tf_op | source)
XLA Modules:
  0.0 109.4 jit_solution(14531414205923397481)
XLA Ops:
  0.0 1.8 %copy.41 = bf16[2,64,768]{2,0,1:T(2,128)(2,1)} copy(bf16[2,64,768]{2,1,0:T(8,128)(2,1)} %param.10) | data formatting | bytes 393216 | tf_op jit(solution)/shard_map/reshape | solution.py:110
  1.8 15.2 %all-to-all-start = ((bf16[16,4,2,768]{3,2,1,0:T(2,128)(2,1)}), bf16[16,4,2,768]{3,2,1,0:T(2,128)(2,1)S(1)}, u32[]{:S(2)}, u32[]{:S(2)}) async-start(bf16[16,4,2,768]{3,2,1,0:T(2,128)(2,1)} %bitcast.2), calls=%async_computation | async-start | bytes 393216 | tf_op jit(solution)/shard_map/all_to_all | solution.py:93
  17.1 1.1 %pad_maximum_fusion = bf16[4,128,512]{2,1,0:T(8,128)(2,1)S(1)} fusion(bf16[4,128,256]{2,1,0:T(8,128)(2,1)} %param.13, bf16[4,128,256]{2,1,0:T(8,128)(2,1)} %param.12), kind=kLoop, calls=%fused_computation.7 | loop fusion | flops 1048576 | bytes 1048576 | tf_op jit(solution)/shard_map/concatenate | solution.py:101
  18.2 3.5 %collective-permute-start.1 = (bf16[2,16,288]{2,1,0:T(8,128)(2,1)S(1)}, bf16[2,16,288]{2,1,0:T(8,128)(2,1)S(1)}, u32[]{:S(2)}, u32[]{:S(2)}) collective-permute-start(bf16[2,16,288]{2,1,0:T(8,128)(2,1)S(1)} %copy-done.3), channel_id=1, source_target_pairs={{0,128},{128,0},{256,384},{384,256},{1,129},{129,1},{257,385},{385... | collective-permute-start | bytes 55304 | tf_op jit(solution)/shard_map/ppermute | solution.py:104
  21.7 1.9 %collective-permute-start = (bf16[4,128,512]{2,1,0:T(8,128)(2,1)S(1)}, bf16[4,128,512]{2,1,0:T(8,128)(2,1)S(1)}, u32[]{:S(2)}, u32[]{:S(2)}) collective-permute-start(bf16[4,128,512]{2,1,0:T(8,128)(2,1)S(1)} %pad_maximum_fusion), channel_id=1, source_target_pairs={{0,16},{16,0},{1,17},{17,1},{2,18},{18,2},{3,19},{19,3},{4,20},{20... | collective-permute-start | bytes 1572872 | tf_op jit(solution)/shard_map/ppermute | solution.py:103
  23.9 1.6 %collective-permute-done = bf16[4,128,512]{2,1,0:T(8,128)(2,1)S(1)} collective-permute-done((bf16[4,128,512]{2,1,0:T(8,128)(2,1)S(1)}, bf16[4,128,512]{2,1,0:T(8,128)(2,1)S(1)}, u32[]{:S(2)}, u32[]{:S(2)}) %collective-permute-start) | collective-permute-done | bytes 524320 | tf_op jit(solution)/shard_map/ppermute | solution.py:103
  25.6 7.3 %all-to-all-done = bf16[16,4,2,768]{3,2,1,0:T(2,128)(2,1)S(1)} async-done(((bf16[16,4,2,768]{3,2,1,0:T(2,128)(2,1)}), bf16[16,4,2,768]{3,2,1,0:T(2,128)(2,1)S(1)}, u32[]{:S(2)}, u32[]{:S(2)}) %all-to-all-start) | async-done | bytes 196640 | tf_op jit(solution)/shard_map/all_to_all | solution.py:93
  33.1 0.1 fusion.32
  33.2 0.4 fusion.31
  33.6 0.2 convert_reduce_fusion.1
  33.9 0.1 fusion.30
  34.0 0.2 fusion.16
  34.3 0.3 fusion.1
  34.6 0.7 fusion.7
  35.2 7.0 %all-to-all-start.1 = ((bf16[16,16,256]{2,1,0:T(8,128)(2,1)}), bf16[16,16,256]{2,1,0:T(8,128)(2,1)S(1)}, u32[]{:S(2)}, u32[]{:S(2)}) async-start(bf16[16,16,256]{2,1,0:T(8,128)(2,1)} %fusion.7), calls=%async_computation.1 | async-start | bytes 262144 | tf_op jit(solution)/shard_map/all_to_all | solution.py:93
  42.3 5.3 %collective-permute-start.2 = (bf16[2,2,16,288]{3,2,1,0:T(8,128)(2,1)S(1)}, bf16[2,2,16,288]{3,2,1,0:T(8,128)(2,1)S(1)}, u32[]{:S(2)}, u32[]{:S(2)}) collective-permute-start(bf16[2,2,16,288]{3,2,1,0:T(8,128)(2,1)S(1)} %maximum_select_fusion.2), channel_id=1, source_target_pairs={{0,256},{128,384},{256,0},{384,128},{1,257},{129,385},{257,1},{385... | collective-permute-start | bytes 110600 | tf_op jit(solution)/shard_map/ppermute | solution.py:109
  47.7 2.6 %all-to-all-done.1 = bf16[16,16,256]{2,1,0:T(8,128)(2,1)S(1)} async-done(((bf16[16,16,256]{2,1,0:T(8,128)(2,1)}), bf16[16,16,256]{2,1,0:T(8,128)(2,1)S(1)}, u32[]{:S(2)}, u32[]{:S(2)}) %all-to-all-start.1) | async-done | bytes 131104 | tf_op jit(solution)/shard_map/all_to_all | solution.py:93
  50.4 0.1 multiply_reduce_fusion
  50.5 0.1 reshape.221
  50.6 0.6 broadcast_in_dim.61
  51.2 6.5 %all-to-all-start.2 = ((bf16[64,2,96]{2,1,0:T(2,128)(2,1)}), bf16[64,2,96]{2,1,0:T(2,128)(2,1)S(1)}, u32[]{:S(2)}, u32[]{:S(2)}) async-start(bf16[64,2,96]{2,1,0:T(2,128)(2,1)} %bitcast.13), calls=%async_computation.2 | async-start | bytes 65536 | tf_op jit(solution)/shard_map/all_to_all | solution.py:93
  57.8 2.9 %shard_map.91.more_ref = f32[4608,128]{1,0:T(8,128)S(1)} custom-call(bf16[4,32,288]{2,1,0:T(8,128)(2,1)S(1)} %maximum_select_fusion.h_ref, bf16[288,4608]{1,0:T(8,128)(2,1)} %w_hbm.1), custom_call_target="tpu_custom_call" | custom-call | flops 339738624 | bytes 5013504 | tf_op jit(solution)/shard_map/pallas_call | solution.py:39
  60.7 10.8 %all-to-all-done.2 = bf16[64,2,96]{2,1,0:T(2,128)(2,1)S(1)} async-done(((bf16[64,2,96]{2,1,0:T(2,128)(2,1)}), bf16[64,2,96]{2,1,0:T(2,128)(2,1)S(1)}, u32[]{:S(2)}, u32[]{:S(2)}) %all-to-all-start.2) | async-done | bytes 24608 | tf_op jit(solution)/shard_map/all_to_all | solution.py:93
  71.5 1.0 shard_map.92
  72.5 1.9 %collective-permute-start.3 = (bf16[2304,128]{1,0:T(8,128)(2,1)S(1)}, bf16[2304,128]{1,0:T(8,128)(2,1)S(1)}, u32[]{:S(2)}, u32[]{:S(2)}) collective-permute-start(bf16[2304,128]{1,0:T(8,128)(2,1)S(1)} %get-tuple-element.16), channel_id=1, source_target_pairs={{0,16},{16,0},{1,17},{17,1},{2,18},{18,2},{3,19},{19,3},{4,20},{20... | collective-permute-start | bytes 1769480 | tf_op jit(solution)/shard_map/ppermute | solution.py:154
  74.4 2.0 %collective-permute-done.3 = bf16[2304,128]{1,0:T(8,128)(2,1)S(1)} collective-permute-done((bf16[2304,128]{1,0:T(8,128)(2,1)S(1)}, bf16[2304,128]{1,0:T(8,128)(2,1)S(1)}, u32[]{:S(2)}, u32[]{:S(2)}) %collective-permute-start.3) | collective-permute-done | bytes 589856 | tf_op jit(solution)/shard_map/ppermute | solution.py:154
  76.4 0.2 add_convert_fusion
  76.6 13.1 %all_to_all.25 = bf16[4,576,128]{2,1,0:T(8,128)(2,1)S(1)} all-to-all(bf16[4,576,128]{2,1,0:T(8,128)(2,1)S(1)} %bitcast.43), channel_id=1, replica_groups=mesh['gx'=4,'gyx'=4,'core'=2,'gz'=16] {'gyx'}, dimensions={0} | all-to-all | bytes 1179648 | tf_op jit(solution)/shard_map/all_to_all | solution.py:93
  89.7 0.1 reduce_sum.61
  89.9 18.7 %all_to_all.26 = bf16[16,36,128]{2,1,0:T(8,128)(2,1)S(1)} all-to-all(bf16[16,36,128]{2,1,0:T(8,128)(2,1)S(1)} %reshape.225), channel_id=1, replica_groups=mesh['gx'=4,'gyx'=4,'core'=2,'gz'=16] {'gz'}, dimensions={0} | all-to-all | bytes 294912 | tf_op jit(solution)/shard_map/all_to_all | solution.py:93
  108.6 0.1 reshape.226
  108.7 0.6 fusion.10
  (49 shorter events, 0.9 us)
Async XLA Ops:
  0.0 18.2 %copy-start.3 = (bf16[2,16,288]{2,1,0:T(8,128)(2,1)S(1)}, bf16[2,16,288]{2,1,0:T(8,128)(2,1)}, u32[]{:S(2)}) copy-start(bf16[2,16,288]{2,1,0:T(8,128)(2,1)} %param.16) | copy-start | bytes 55300
  0.0 23.6 %copy-start.6 = (s32[4]{0:T(128)S(1)}, s32[4]{0:T(128)}, u32[]{:S(2)}) copy-start(s32[4]{0:T(128)} %param.14) | copy-start | bytes 52
  0.0 23.8 %copy-start.5 = (bf16[2,4,512]{2,1,0:T(4,128)(2,1)S(1)}, bf16[2,4,512]{2,1,0:T(4,128)(2,1)}, u32[]{:S(2)}) copy-start(bf16[2,4,512]{2,1,0:T(4,128)(2,1)} %param.11) | copy-start | bytes 24580
  1.8 31.0 %all-to-all-start = ((bf16[16,4,2,768]{3,2,1,0:T(2,128)(2,1)}), bf16[16,4,2,768]{3,2,1,0:T(2,128)(2,1)S(1)}, u32[]{:S(2)}, u32[]{:S(2)}) async-start(bf16[16,4,2,768]{3,2,1,0:T(2,128)(2,1)} %bitcast.2), calls=%async_computation | async-start | bytes 393216 | tf_op jit(solution)/shard_map/all_to_all | solution.py:93
  17.1 8.5 %copy-start.1 = (bf16[4,128,256]{2,1,0:T(8,128)(2,1)S(1)}, bf16[4,128,256]{2,1,0:T(8,128)(2,1)}, u32[]{:S(2)}) copy-start(bf16[4,128,256]{2,1,0:T(8,128)(2,1)} %param.12) | copy-start | bytes 786436
  18.2 7.4 %collective-permute-start.1 = (bf16[2,16,288]{2,1,0:T(8,128)(2,1)S(1)}, bf16[2,16,288]{2,1,0:T(8,128)(2,1)S(1)}, u32[]{:S(2)}, u32[]{:S(2)}) collective-permute-start(bf16[2,16,288]{2,1,0:T(8,128)(2,1)S(1)} %copy-done.3), channel_id=1, source_target_pairs={{0,128},{128,0},{256,384},{384,256},{1,129},{129,1},{257,385},{385... | collective-permute-start | bytes 55304 | tf_op jit(solution)/shard_map/ppermute | solution.py:104
  21.7 3.8 %collective-permute-start = (bf16[4,128,512]{2,1,0:T(8,128)(2,1)S(1)}, bf16[4,128,512]{2,1,0:T(8,128)(2,1)S(1)}, u32[]{:S(2)}, u32[]{:S(2)}) collective-permute-start(bf16[4,128,512]{2,1,0:T(8,128)(2,1)S(1)} %pad_maximum_fusion), channel_id=1, source_target_pairs={{0,16},{16,0},{1,17},{17,1},{2,18},{18,2},{3,19},{19,3},{4,20},{20... | collective-permute-start | bytes 1572872 | tf_op jit(solution)/shard_map/ppermute | solution.py:103
  25.6 8.7 %copy-start.2 = (bf16[4,128,256]{2,1,0:T(8,128)(2,1)S(1)}, bf16[4,128,256]{2,1,0:T(8,128)(2,1)}, u32[]{:S(2)}) copy-start(bf16[4,128,256]{2,1,0:T(8,128)(2,1)} %param.13) | copy-start | bytes 786436
  35.2 15.0 %all-to-all-start.1 = ((bf16[16,16,256]{2,1,0:T(8,128)(2,1)}), bf16[16,16,256]{2,1,0:T(8,128)(2,1)S(1)}, u32[]{:S(2)}, u32[]{:S(2)}) async-start(bf16[16,16,256]{2,1,0:T(8,128)(2,1)} %fusion.7), calls=%async_computation.1 | async-start | bytes 262144 | tf_op jit(solution)/shard_map/all_to_all | solution.py:93
  42.3 15.5 %collective-permute-start.2 = (bf16[2,2,16,288]{3,2,1,0:T(8,128)(2,1)S(1)}, bf16[2,2,16,288]{3,2,1,0:T(8,128)(2,1)S(1)}, u32[]{:S(2)}, u32[]{:S(2)}) collective-permute-start(bf16[2,2,16,288]{3,2,1,0:T(8,128)(2,1)S(1)} %maximum_select_fusion.2), channel_id=1, source_target_pairs={{0,256},{128,384},{256,0},{384,128},{1,257},{129,385},{257,1},{385... | collective-permute-start | bytes 110600 | tf_op jit(solution)/shard_map/ppermute | solution.py:109
  51.2 20.3 %all-to-all-start.2 = ((bf16[64,2,96]{2,1,0:T(2,128)(2,1)}), bf16[64,2,96]{2,1,0:T(2,128)(2,1)S(1)}, u32[]{:S(2)}, u32[]{:S(2)}) async-start(bf16[64,2,96]{2,1,0:T(2,128)(2,1)} %bitcast.13), calls=%async_computation.2 | async-start | bytes 65536 | tf_op jit(solution)/shard_map/all_to_all | solution.py:93
  57.8 13.7 %copy-start = (bf16[96,4608]{1,0:T(8,128)(2,1)S(1)}, bf16[96,4608]{1,0:T(8,128)(2,1)}, u32[]{:S(2)}) copy-start(bf16[96,4608]{1,0:T(8,128)(2,1)} %w_ref.1) | copy-start | bytes 2654212
  72.5 3.9 %collective-permute-start.3 = (bf16[2304,128]{1,0:T(8,128)(2,1)S(1)}, bf16[2304,128]{1,0:T(8,128)(2,1)S(1)}, u32[]{:S(2)}, u32[]{:S(2)}) collective-permute-start(bf16[2304,128]{1,0:T(8,128)(2,1)S(1)} %get-tuple-element.16), channel_id=1, source_target_pairs={{0,16},{16,0},{1,17},{17,1},{2,18},{18,2},{3,19},{19,3},{4,20},{20... | collective-permute-start | bytes 1769480 | tf_op jit(solution)/shard_map/ppermute | solution.py:154
  76.6 32.2 %copy-start.4 = (bf16[2,64,36]{1,0,2:T(2,128)(2,1)S(1)}, bf16[2,64,36]{1,0,2:T(2,128)(2,1)}, u32[]{:S(2)}) copy-start(bf16[2,64,36]{1,0,2:T(2,128)(2,1)} %param.9) | copy-start | bytes 27652

commit v7 on v6

--- a/solution.py
+++ b/solution.py
@@ -107,9 +107,9 @@
     keys, near = lax.optimization_barrier((keys, near))
     near = jnp.where(gx % 2 == 0, jnp.stack([hidden, near]), jnp.stack([near, hidden]))
     far = lax.ppermute(near, "gx", [(i, i ^ 2) for i in range(4)])
-    q = exchange(query.reshape(2, 16, 4, 768).transpose(1, 2, 0, 3), "gz")
-    q = lax.dynamic_index_in_dim(q.reshape(4, 2, 2, 4, 2, 768), core, 1, keepdims=False)
-    qf = q.reshape(4, 2, 4, 2, 3, HD).transpose(2, 0, 1, 3, 4, 5).reshape(4, 48, HD)
+    q = lax.dynamic_index_in_dim(query, core, 0, keepdims=False)
+    q = exchange(q.reshape(16, 4, 768), "gz")
+    qf = q.reshape(16, 4, 3, HD).transpose(1, 0, 2, 3).reshape(4, HEADS, HD)
 
     at = jnp.arange(256, dtype=jnp.int32)
     owner = gx * 8 + gyx * 2 + jnp.where(at < 128, core, 1 - core)
@@ -118,8 +118,7 @@
     scale = HD**-0.5
     s = jnp.einsum("bqd,bpd->bqp", qf, keys, preferred_element_type=F32) * scale
     s = jnp.where(present, s, NEG)
-    step = (jnp.arange(48) // 3) % 2
-    allowed = (jnp.arange(2)[None, :] <= step[:, None]) & (gx + gyx == 0)
+    allowed = ((jnp.arange(2) <= core) & (gx + gyx == 0))[None, None]
     sn = jnp.einsum("bqd,ubd->bqu", qf, new_kv[..., :HD], preferred_element_type=F32) * scale
     sn = jnp.where(allowed, sn, NEG)
     peak = jnp.maximum(jnp.max(s, -1), jnp.max(sn, -1)).astype(BF16)
@@ -142,13 +141,14 @@
     share = jnp.exp(peaks - jnp.max(peaks, 0))
     share = share / jnp.sum(share * totals, 0)
     attn = jnp.sum(message[:, :12].astype(F32) * share[..., None], 0).astype(BF16)
-    attn = attn.reshape(2, 2, 3, HD).transpose(1, 0, 2, 3).reshape(2, 16, 96).transpose(1, 0, 2)
-    attn = jnp.broadcast_to(attn[:, None], (16, 4, 2, 96)).reshape(64, 2, 96)
+    attn = attn.reshape(2, 16, 96).transpose(1, 0, 2)
+    attn = jnp.broadcast_to(attn[:, None], (16, 4, 2, 96)).reshape(128, 1, 96)
 
     spread = jnp.where(gx < 2, jnp.concatenate([near, far]), jnp.concatenate([far, near]))
     feed = turned_product(spread.reshape(4, 32, 288), down_weight)
 
-    mine = exchange(attn, ("gz", "gx")).transpose(1, 0, 2).reshape(128, 96)
+    mine = exchange(attn, ("gz", "gx", "core"))
+    mine = mine.reshape(64, 2, 96).transpose(1, 0, 2).reshape(128, 96)
     ours, theirs = split_product(core, mine, out_weight, feed)
 
     theirs = lax.ppermute(theirs, "core", [(0, 1), (1, 0)])

time: 110 us -> 109 us (level)
  starting transfers between devices: 41.4 us -> 43.7 us
  waiting for transfers between devices: 24.2 us -> 22.1 us
    all_to_all x3, starting transfers between devices: 28.8 us -> 30.9 us  [exchange(): return lax.all_to_all(x, axes, split_axis=0, concat_axis=0, tiled=True)]
    ppermute x1, waiting for transfers between devices: 1.63 us -> 0.01 us  [per_device(): pair = lax.ppermute(pair, 'core', [(0, 1), (1, 0)])]
  transfers between devices with their start and end apart: 7 -> 7, of which waited for: 5 -> 4; matrix products, arithmetic and copies ran while one was open for 2% -> 2% of each run, Pallas kernels for 3% -> 3%
where the time goes in v7:
time: 109 us
  starting transfers between devices  43.7 us (40%)
  blocking collectives  31.3 us (29%)
  waiting for transfers between devices  22.1 us (20%)
  Pallas kernels  3.9 us (4%)
  other arithmetic  3.45 us (3%)
  local copies, waits for them, and re-layouts  2.92 us (3%)
    all_to_all x2, blocking collectives, exchange(): return lax.all_to_all(x, axes, split_axis=0, concat_axis=0, tiled=True)  31.3 us
    all_to_all x3, starting transfers between devices, exchange(): return lax.all_to_all(x, axes, split_axis=0, concat_axis=0, tiled=True)  30.9 us
    all_to_all x3, waiting for transfers between devices, exchange(): return lax.all_to_all(x, axes, split_axis=0, concat_axis=0, tiled=True)  20.2 us
    ppermute x1, starting transfers between devices, per_device(): far = lax.ppermute(near, 'gx', [(i, i ^ 2) for i in range(4)])  5.34 us
    ppermute x1, starting transfers between devices, per_device(): near = lax.ppermute(own, 'gx', [(i, i ^ 1) for i in range(4)])  3.62 us
    pallas_call x1, Pallas kernels, turned_product(): pl.pallas_call(kernel, in_specs=[in_vmem, pl.BlockSpec(memory_space=pltpu...  2.92 us
  transfers between devices with their start and end apart: 7, of which 4 were waited for; matrix products, arithmetic and copies ran while one was open for 2% of the time, Pallas kernels for 3%

profile of v7, /device:TPU:32, one launch (start us, length us, event | category | flops | bytes accessed | tf_op | source)
XLA Modules:
  0.0 108.8 jit_solution(5223274064586421202)
XLA Ops:
  0.0 0.9 copy-done
  0.9 0.7 reshape.193
  1.6 15.2 %all-to-all-start = ((bf16[16,4,768]{2,1,0:T(4,128)(2,1)}), bf16[16,4,768]{2,1,0:T(4,128)(2,1)S(1)}, u32[]{:S(2)}, u32[]{:S(2)}) async-start(bf16[16,4,768]{2,1,0:T(4,128)(2,1)} %reshape.193), calls=%async_computation | async-start | bytes 196608 | tf_op jit(solution)/shard_map/all_to_all | solution.py:93
  16.8 1.1 pad_maximum_fusion
  17.9 3.6 %collective-permute-start.1 = (bf16[2,16,288]{2,1,0:T(8,128)(2,1)S(1)}, bf16[2,16,288]{2,1,0:T(8,128)(2,1)S(1)}, u32[]{:S(2)}, u32[]{:S(2)}) collective-permute-start(bf16[2,16,288]{2,1,0:T(8,128)(2,1)S(1)} %copy-done.4), channel_id=1, source_target_pairs={{0,128},{128,0},{256,384},{384,256},{1,129},{129,1},{257,385},{385... | collective-permute-start | bytes 55304 | tf_op jit(solution)/shard_map/ppermute | solution.py:104
  21.5 1.9 %collective-permute-start = (bf16[4,128,512]{2,1,0:T(8,128)(2,1)S(1)}, bf16[4,128,512]{2,1,0:T(8,128)(2,1)S(1)}, u32[]{:S(2)}, u32[]{:S(2)}) collective-permute-start(bf16[4,128,512]{2,1,0:T(8,128)(2,1)S(1)} %pad_maximum_fusion), channel_id=1, source_target_pairs={{0,16},{16,0},{1,17},{17,1},{2,18},{18,2},{3,19},{19,3},{4,20},{20... | collective-permute-start | bytes 1572872 | tf_op jit(solution)/shard_map/ppermute | solution.py:103
  23.7 6.1 %all-to-all-done = bf16[16,4,768]{2,1,0:T(4,128)(2,1)S(1)} async-done(((bf16[16,4,768]{2,1,0:T(4,128)(2,1)}), bf16[16,4,768]{2,1,0:T(4,128)(2,1)S(1)}, u32[]{:S(2)}, u32[]{:S(2)}) %all-to-all-start) | async-done | bytes 98336 | tf_op jit(solution)/shard_map/all_to_all | solution.py:93
  29.9 0.1 copy.43
  30.0 0.2 fusion.31
  30.3 0.4 fusion.30
  30.7 0.2 convert_reduce_fusion.1
  31.1 0.2 fusion.16
  31.4 0.3 fusion.1
  31.7 0.7 fusion.7
  32.3 7.0 %all-to-all-start.1 = ((bf16[16,16,256]{2,1,0:T(8,128)(2,1)}), bf16[16,16,256]{2,1,0:T(8,128)(2,1)S(1)}, u32[]{:S(2)}, u32[]{:S(2)}) async-start(bf16[16,16,256]{2,1,0:T(8,128)(2,1)} %fusion.7), calls=%async_computation.1 | async-start | bytes 262144 | tf_op jit(solution)/shard_map/all_to_all | solution.py:93
  39.4 5.3 %collective-permute-start.2 = (bf16[2,2,16,288]{3,2,1,0:T(8,128)(2,1)S(1)}, bf16[2,2,16,288]{3,2,1,0:T(8,128)(2,1)S(1)}, u32[]{:S(2)}, u32[]{:S(2)}) collective-permute-start(bf16[2,2,16,288]{3,2,1,0:T(8,128)(2,1)S(1)} %maximum_select_fusion.2), channel_id=1, source_target_pairs={{0,256},{128,384},{256,0},{384,128},{1,257},{129,385},{257,1},{385... | collective-permute-start | bytes 110600 | tf_op jit(solution)/shard_map/ppermute | solution.py:109
  44.8 2.6 %all-to-all-done.1 = bf16[16,16,256]{2,1,0:T(8,128)(2,1)S(1)} async-done(((bf16[16,16,256]{2,1,0:T(8,128)(2,1)}), bf16[16,16,256]{2,1,0:T(8,128)(2,1)S(1)}, u32[]{:S(2)}, u32[]{:S(2)}) %all-to-all-start.1) | async-done | bytes 131104 | tf_op jit(solution)/shard_map/all_to_all | solution.py:93
  47.5 0.1 multiply_reduce_fusion
  47.6 0.1 convert_element_type.137
  47.7 0.7 copy.51
  48.4 8.7 %all-to-all-start.2 = ((bf16[128,1,96]{2,1,0:T(2,128)(2,1)}), bf16[128,1,96]{2,1,0:T(2,128)(2,1)S(1)}, u32[]{:S(2)}, u32[]{:S(2)}) async-start(bf16[128,1,96]{2,1,0:T(2,128)(2,1)} %copy.51), calls=%async_computation.2 | async-start | bytes 131072 | tf_op jit(solution)/shard_map/all_to_all | solution.py:93
  57.2 2.9 %shard_map.91.more_ref = f32[4608,128]{1,0:T(8,128)S(1)} custom-call(bf16[4,32,288]{2,1,0:T(8,128)(2,1)S(1)} %maximum_select_fusion.h_ref, bf16[288,4608]{1,0:T(8,128)(2,1)} %w_hbm.1), custom_call_target="tpu_custom_call" | custom-call | flops 339738624 | bytes 5013504 | tf_op jit(solution)/shard_map/pallas_call | solution.py:39
  60.1 11.4 %all-to-all-done.2 = bf16[128,1,96]{2,1,0:T(2,128)(2,1)S(1)} async-done(((bf16[128,1,96]{2,1,0:T(2,128)(2,1)}), bf16[128,1,96]{2,1,0:T(2,128)(2,1)S(1)}, u32[]{:S(2)}, u32[]{:S(2)}) %all-to-all-start.2) | async-done | bytes 24608 | tf_op jit(solution)/shard_map/all_to_all | solution.py:93
  71.5 1.0 shard_map.92
  72.5 1.9 %collective-permute-start.3 = (bf16[2304,128]{1,0:T(8,128)(2,1)S(1)}, bf16[2304,128]{1,0:T(8,128)(2,1)S(1)}, u32[]{:S(2)}, u32[]{:S(2)}) collective-permute-start(bf16[2304,128]{1,0:T(8,128)(2,1)S(1)} %get-tuple-element.16), channel_id=1, source_target_pairs={{0,16},{16,0},{1,17},{17,1},{2,18},{18,2},{3,19},{19,3},{4,20},{20... | collective-permute-start | bytes 1769480 | tf_op jit(solution)/shard_map/ppermute | solution.py:154
  74.4 2.0 %collective-permute-done.3 = bf16[2304,128]{1,0:T(8,128)(2,1)S(1)} collective-permute-done((bf16[2304,128]{1,0:T(8,128)(2,1)S(1)}, bf16[2304,128]{1,0:T(8,128)(2,1)S(1)}, u32[]{:S(2)}, u32[]{:S(2)}) %collective-permute-start.3) | collective-permute-done | bytes 589856 | tf_op jit(solution)/shard_map/ppermute | solution.py:154
  76.4 0.2 add_convert_fusion
  76.6 13.1 %all_to_all.25 = bf16[4,576,128]{2,1,0:T(8,128)(2,1)S(1)} all-to-all(bf16[4,576,128]{2,1,0:T(8,128)(2,1)S(1)} %bitcast.42), channel_id=1, replica_groups=mesh['gx'=4,'gyx'=4,'core'=2,'gz'=16] {'gyx'}, dimensions={0} | all-to-all | bytes 1179648 | tf_op jit(solution)/shard_map/all_to_all | solution.py:93
  89.7 0.1 reduce_sum.61
  89.9 18.1 %all_to_all.26 = bf16[16,36,128]{2,1,0:T(8,128)(2,1)S(1)} all-to-all(bf16[16,36,128]{2,1,0:T(8,128)(2,1)S(1)} %reshape.202), channel_id=1, replica_groups=mesh['gx'=4,'gyx'=4,'core'=2,'gz'=16] {'gz'}, dimensions={0} | all-to-all | bytes 294912 | tf_op jit(solution)/shard_map/all_to_all | solution.py:93
  108.0 0.1 reshape.203
  108.1 0.6 fusion.10
  (51 shorter events, 0.9 us)
Async XLA Ops:
  0.0 0.9 copy-start
  0.0 17.9 %copy-start.4 = (bf16[2,16,288]{2,1,0:T(8,128)(2,1)S(1)}, bf16[2,16,288]{2,1,0:T(8,128)(2,1)}, u32[]{:S(2)}) copy-start(bf16[2,16,288]{2,1,0:T(8,128)(2,1)} %param.16) | copy-start | bytes 55300
  0.0 23.5 %copy-start.7 = (s32[4]{0:T(128)S(1)}, s32[4]{0:T(128)}, u32[]{:S(2)}) copy-start(s32[4]{0:T(128)} %param.14) | copy-start | bytes 52
  0.0 23.6 %copy-start.6 = (bf16[2,4,512]{2,1,0:T(4,128)(2,1)S(1)}, bf16[2,4,512]{2,1,0:T(4,128)(2,1)}, u32[]{:S(2)}) copy-start(bf16[2,4,512]{2,1,0:T(4,128)(2,1)} %param.11) | copy-start | bytes 24580
  1.6 28.2 %all-to-all-start = ((bf16[16,4,768]{2,1,0:T(4,128)(2,1)}), bf16[16,4,768]{2,1,0:T(4,128)(2,1)S(1)}, u32[]{:S(2)}, u32[]{:S(2)}) async-start(bf16[16,4,768]{2,1,0:T(4,128)(2,1)} %reshape.193), calls=%async_computation | async-start | bytes 196608 | tf_op jit(solution)/shard_map/all_to_all | solution.py:93
  17.9 12.3 %copy-start.2 = (bf16[4,128,256]{2,1,0:T(8,128)(2,1)S(1)}, bf16[4,128,256]{2,1,0:T(8,128)(2,1)}, u32[]{:S(2)}) copy-start(bf16[4,128,256]{2,1,0:T(8,128)(2,1)} %param.12) | copy-start | bytes 786436
  17.9 12.4 %collective-permute-start.1 = (bf16[2,16,288]{2,1,0:T(8,128)(2,1)S(1)}, bf16[2,16,288]{2,1,0:T(8,128)(2,1)S(1)}, u32[]{:S(2)}, u32[]{:S(2)}) collective-permute-start(bf16[2,16,288]{2,1,0:T(8,128)(2,1)S(1)} %copy-done.4), channel_id=1, source_target_pairs={{0,128},{128,0},{256,384},{384,256},{1,129},{129,1},{257,385},{385... | collective-permute-start | bytes 55304 | tf_op jit(solution)/shard_map/ppermute | solution.py:104
  21.5 8.6 %collective-permute-start = (bf16[4,128,512]{2,1,0:T(8,128)(2,1)S(1)}, bf16[4,128,512]{2,1,0:T(8,128)(2,1)S(1)}, u32[]{:S(2)}, u32[]{:S(2)}) collective-permute-start(bf16[4,128,512]{2,1,0:T(8,128)(2,1)S(1)} %pad_maximum_fusion), channel_id=1, source_target_pairs={{0,16},{16,0},{1,17},{17,1},{2,18},{18,2},{3,19},{19,3},{4,20},{20... | collective-permute-start | bytes 1572872 | tf_op jit(solution)/shard_map/ppermute | solution.py:103
  30.2 1.2 %copy-start.3 = (bf16[4,128,256]{2,1,0:T(8,128)(2,1)S(1)}, bf16[4,128,256]{2,1,0:T(8,128)(2,1)}, u32[]{:S(2)}) copy-start(bf16[4,128,256]{2,1,0:T(8,128)(2,1)} %param.13) | copy-start | bytes 786436
  32.3 15.0 %all-to-all-start.1 = ((bf16[16,16,256]{2,1,0:T(8,128)(2,1)}), bf16[16,16,256]{2,1,0:T(8,128)(2,1)S(1)}, u32[]{:S(2)}, u32[]{:S(2)}) async-start(bf16[16,16,256]{2,1,0:T(8,128)(2,1)} %fusion.7), calls=%async_computation.1 | async-start | bytes 262144 | tf_op jit(solution)/shard_map/all_to_all | solution.py:93
  39.4 17.7 %collective-permute-start.2 = (bf16[2,2,16,288]{3,2,1,0:T(8,128)(2,1)S(1)}, bf16[2,2,16,288]{3,2,1,0:T(8,128)(2,1)S(1)}, u32[]{:S(2)}, u32[]{:S(2)}) collective-permute-start(bf16[2,2,16,288]{3,2,1,0:T(8,128)(2,1)S(1)} %maximum_select_fusion.2), channel_id=1, source_target_pairs={{0,256},{128,384},{256,0},{384,128},{1,257},{129,385},{257,1},{385... | collective-permute-start | bytes 110600 | tf_op jit(solution)/shard_map/ppermute | solution.py:109
  48.4 23.1 %all-to-all-start.2 = ((bf16[128,1,96]{2,1,0:T(2,128)(2,1)}), bf16[128,1,96]{2,1,0:T(2,128)(2,1)S(1)}, u32[]{:S(2)}, u32[]{:S(2)}) async-start(bf16[128,1,96]{2,1,0:T(2,128)(2,1)} %copy.51), calls=%async_computation.2 | async-start | bytes 131072 | tf_op jit(solution)/shard_map/all_to_all | solution.py:93
  57.1 14.4 %copy-start.1 = (bf16[96,4608]{1,0:T(8,128)(2,1)S(1)}, bf16[96,4608]{1,0:T(8,128)(2,1)}, u32[]{:S(2)}) copy-start(bf16[96,4608]{1,0:T(8,128)(2,1)} %w_ref.1) | copy-start | bytes 2654212
  72.5 3.9 %collective-permute-start.3 = (bf16[2304,128]{1,0:T(8,128)(2,1)S(1)}, bf16[2304,128]{1,0:T(8,128)(2,1)S(1)}, u32[]{:S(2)}, u32[]{:S(2)}) collective-permute-start(bf16[2304,128]{1,0:T(8,128)(2,1)S(1)} %get-tuple-element.16), channel_id=1, source_target_pairs={{0,16},{16,0},{1,17},{17,1},{2,18},{18,2},{3,19},{19,3},{4,20},{20... | collective-permute-start | bytes 1769480 | tf_op jit(solution)/shard_map/ppermute | solution.py:154
  76.6 31.6 %copy-start.5 = (bf16[2,64,36]{1,0,2:T(2,128)(2,1)S(1)}, bf16[2,64,36]{1,0,2:T(2,128)(2,1)}, u32[]{:S(2)}) copy-start(bf16[2,64,36]{1,0,2:T(2,128)(2,1)} %param.9) | copy-start | bytes 27652

commit v8 on v7

--- a/solution.py
+++ b/solution.py
@@ -104,9 +104,10 @@
     near = lax.ppermute(own, "gx", [(i, i ^ 1) for i in range(4)])
     keys = jnp.concatenate([key_cache, pair[..., :HD]], 1)
     values = jnp.concatenate([value_cache, pair[..., HD:]], 1)
-    keys, near = lax.optimization_barrier((keys, near))
     near = jnp.where(gx % 2 == 0, jnp.stack([hidden, near]), jnp.stack([near, hidden]))
     far = lax.ppermute(near, "gx", [(i, i ^ 2) for i in range(4)])
+    spread = jnp.where(gx < 2, jnp.concatenate([near, far]), jnp.concatenate([far, near]))
+    keys, spread = lax.optimization_barrier((keys, spread))
     q = lax.dynamic_index_in_dim(query, core, 0, keepdims=False)
     q = exchange(q.reshape(16, 4, 768), "gz")
     qf = q.reshape(16, 4, 3, HD).transpose(1, 0, 2, 3).reshape(4, HEADS, HD)
@@ -130,32 +131,29 @@
     acc = acc + jnp.einsum("bqu,ubd->bqd", wn, new_kv[..., HD:], preferred_element_type=F32)
     total_hi = total.astype(BF16)
     total_lo = (total - total_hi.astype(F32)).astype(BF16)
-    stats = jnp.stack([peak, total_hi, total_lo, jnp.zeros_like(peak)], 1)
-    stats = stats.reshape(4, 4, 4, 12).transpose(0, 2, 1, 3).reshape(16, 4, 12)
-    stats = jnp.pad(stats, ((0, 0), (0, 0), (0, HD - 12)))
-    message = jnp.concatenate([acc.astype(BF16).reshape(16, 12, HD), stats], 1)
+    stats = jnp.stack([peak, total_hi, total_lo], 1)
+    stats = stats.reshape(4, 3, 8, 6).transpose(0, 2, 1, 3).reshape(32, 1, 18)
+    stats = jnp.pad(stats, ((0, 0), (0, 1), (0, HD - 18)))
+    message = jnp.concatenate([acc.astype(BF16).reshape(32, 6, HD), stats], 1)
 
-    message = exchange(message, ("gx", "gyx"))
-    peaks = message[:, 12, :12].astype(F32)
-    totals = message[:, 13, :12].astype(F32) + message[:, 14, :12].astype(F32)
+    message = exchange(message, ("gx",) + GY).reshape(16, 2, 8, HD)
+    peaks = message[:, :, 6, :6].astype(F32)
+    totals = message[:, :, 6, 6:12].astype(F32) + message[:, :, 6, 12:18].astype(F32)
     share = jnp.exp(peaks - jnp.max(peaks, 0))
     share = share / jnp.sum(share * totals, 0)
-    attn = jnp.sum(message[:, :12].astype(F32) * share[..., None], 0).astype(BF16)
+    attn = jnp.sum(message[:, :, :6].astype(F32) * share[..., None], 0).astype(BF16)
     attn = attn.reshape(2, 16, 96).transpose(1, 0, 2)
-    attn = jnp.broadcast_to(attn[:, None], (16, 4, 2, 96)).reshape(128, 1, 96)
-
-    spread = jnp.where(gx < 2, jnp.concatenate([near, far]), jnp.concatenate([far, near]))
+    attn = jnp.broadcast_to(attn[:, None], (16, 4, 2, 96)).reshape(64, 2, 96)
     feed = turned_product(spread.reshape(4, 32, 288), down_weight)
 
-    mine = exchange(attn, ("gz", "gx", "core"))
-    mine = mine.reshape(64, 2, 96).transpose(1, 0, 2).reshape(128, 96)
+    mine = exchange(attn, ("gz", "gx")).transpose(1, 0, 2).reshape(128, 96)
     ours, theirs = split_product(core, mine, out_weight, feed)
 
     theirs = lax.ppermute(theirs, "core", [(0, 1), (1, 0)])
     row = (ours + theirs.astype(F32)).astype(BF16).reshape(4, 576, 128)
     row = exchange(row, "gyx")
-    row = jnp.sum(row.astype(F32), 0).astype(BF16).reshape(16, 36, 128)
-    column = exchange(row, "gz")
+    row = jnp.sum(row.astype(F32), 0).astype(BF16).reshape(16, 9, 4, 128)
+    column = exchange(row, "gz").reshape(16, 36, 128)
     summed = jnp.sum(column.astype(F32), 0).reshape(36, 2, 64).transpose(1, 2, 0)
     return (summed + resid.astype(F32)).astype(BF16)
 

time: 109 us -> 115 us (1.055)
  blocking collectives: 31.3 us -> 45.9 us
  waiting for transfers between devices: 22.1 us -> 15.1 us
  starting transfers between devices: 43.7 us -> 41.2 us
    all_to_all x2 -> x3, blocking collectives: 31.3 us -> 45.9 us  [exchange(): return lax.all_to_all(x, axes, split_axis=0, concat_axis=0, tiled=True)]
    all_to_all x3 -> x2, waiting for transfers between devices: 20.2 us -> 10.6 us  [exchange(): return lax.all_to_all(x, axes, split_axis=0, concat_axis=0, tiled=True)]
    ppermute x1, waiting for transfers between devices: 0.01 us -> 2.35 us  [per_device(): far = lax.ppermute(near, 'gx', [(i, i ^ 2) for i in range(4)])]
    all_to_all x3 -> x2, starting transfers between devices: 30.9 us -> 28.7 us  [exchange(): return lax.all_to_all(x, axes, split_axis=0, concat_axis=0, tiled=True)]
  transfers between devices with their start and end apart: 7 -> 6, of which waited for: 4 -> 4; matrix products, arithmetic and copies ran while one was open for 2% -> 1% of each run, Pallas kernels for 3% -> 3%
where the time goes in v8:
time: 115 us; the launch traced here: 114 us
  blocking collectives  45.9 us (40%)
  starting transfers between devices  41.2 us (36%)
  waiting for transfers between devices  15.1 us (13%)
  local copies, waits for them, and re-layouts  3.93 us (3%)
  Pallas kernels  3.89 us (3%)
  other arithmetic  2.87 us (2%)
    all_to_all x3, blocking collectives, exchange(): return lax.all_to_all(x, axes, split_axis=0, concat_axis=0, tiled=True)  45.9 us
    all_to_all x2, starting transfers between devices, exchange(): return lax.all_to_all(x, axes, split_axis=0, concat_axis=0, tiled=True)  28.7 us
    all_to_all x2, waiting for transfers between devices, exchange(): return lax.all_to_all(x, axes, split_axis=0, concat_axis=0, tiled=True)  10.6 us
    ppermute x1, starting transfers between devices, per_device(): far = lax.ppermute(near, 'gx', [(i, i ^ 2) for i in range(4)])  5.1 us
    ppermute x1, starting transfers between devices, per_device(): near = lax.ppermute(own, 'gx', [(i, i ^ 1) for i in range(4)])  3.62 us
    pallas_call x1, Pallas kernels, turned_product(): pl.pallas_call(kernel, in_specs=[in_vmem, pl.BlockSpec(memory_space=pltpu...  2.92 us
    ppermute x1, waiting for transfers between devices, per_device(): far = lax.ppermute(near, 'gx', [(i, i ^ 2) for i in range(4)])  2.35 us
  transfers between devices with their start and end apart: 6, of which 4 were waited for; matrix products, arithmetic and copies ran while one was open for 1% of the time, Pallas kernels for 3%

profile of v8, /device:TPU:32, one launch (start us, length us, event | category | flops | bytes accessed | tf_op | source)
XLA Modules:
  0.0 114.3 jit_solution(11966438945111371788)
XLA Ops:
  0.0 0.9 copy-done
  0.9 0.7 reshape.185
  1.6 15.2 %all-to-all-start = ((bf16[16,4,768]{2,1,0:T(4,128)(2,1)}), bf16[16,4,768]{2,1,0:T(4,128)(2,1)S(1)}, u32[]{:S(2)}, u32[]{:S(2)}) async-start(bf16[16,4,768]{2,1,0:T(4,128)(2,1)} %reshape.185), calls=%async_computation | async-start | bytes 196608 | tf_op jit(solution)/shard_map/all_to_all | solution.py:93
  16.8 1.1 pad_maximum_fusion
  17.9 3.6 %collective-permute-start.1 = (bf16[2,16,288]{2,1,0:T(8,128)(2,1)S(1)}, bf16[2,16,288]{2,1,0:T(8,128)(2,1)S(1)}, u32[]{:S(2)}, u32[]{:S(2)}) collective-permute-start(bf16[2,16,288]{2,1,0:T(8,128)(2,1)S(1)} %copy-done.4), channel_id=1, source_target_pairs={{0,128},{128,0},{256,384},{384,256},{1,129},{129,1},{257,385},{385... | collective-permute-start | bytes 55304 | tf_op jit(solution)/shard_map/ppermute | solution.py:104
  21.5 1.9 %collective-permute-start = (bf16[4,128,512]{2,1,0:T(8,128)(2,1)S(1)}, bf16[4,128,512]{2,1,0:T(8,128)(2,1)S(1)}, u32[]{:S(2)}, u32[]{:S(2)}) collective-permute-start(bf16[4,128,512]{2,1,0:T(8,128)(2,1)S(1)} %pad_maximum_fusion), channel_id=1, source_target_pairs={{0,16},{16,0},{1,17},{17,1},{2,18},{18,2},{3,19},{19,3},{4,20},{20... | collective-permute-start | bytes 1572872 | tf_op jit(solution)/shard_map/ppermute | solution.py:103
  23.6 0.2 collective-permute-done.1
  23.8 5.1 %collective-permute-start.2 = (bf16[2,2,16,288]{3,2,1,0:T(8,128)(2,1)S(1)}, bf16[2,2,16,288]{3,2,1,0:T(8,128)(2,1)S(1)}, u32[]{:S(2)}, u32[]{:S(2)}) collective-permute-start(bf16[2,2,16,288]{3,2,1,0:T(8,128)(2,1)S(1)} %maximum_select_fusion.1), channel_id=1, source_target_pairs={{0,256},{128,384},{256,0},{384,128},{1,257},{129,385},{257,1},{385... | collective-permute-start | bytes 110600 | tf_op jit(solution)/shard_map/ppermute | solution.py:108
  28.9 2.4 %collective-permute-done.2 = bf16[2,2,16,288]{3,2,1,0:T(8,128)(2,1)S(1)} collective-permute-done((bf16[2,2,16,288]{3,2,1,0:T(8,128)(2,1)S(1)}, bf16[2,2,16,288]{3,2,1,0:T(8,128)(2,1)S(1)}, u32[]{:S(2)}, u32[]{:S(2)}) %collective-permute-start.2) | collective-permute-done | bytes 36896 | tf_op jit(solution)/shard_map/ppermute | solution.py:108
  31.5 0.2 fusion.27
  31.8 0.4 fusion.26
  32.2 0.2 convert_reduce_fusion.1
  32.6 0.2 copy.75
  32.8 0.1 copy.76
  33.0 0.2 fusion.14
  33.2 0.3 fusion.1
  33.6 14.9 %all_to_all.25 = bf16[32,8,256]{2,1,0:T(8,128)(2,1)S(1)} all-to-all(bf16[32,8,256]{2,1,0:T(8,128)(2,1)S(1)} %fusion.7), channel_id=1, replica_groups=mesh['gx'=4,'gyx'=4,'core'=2,'gz'=16] {'gx','gyx','core'}, dimensions={0} | all-to-all | bytes 262144 | tf_op jit(solution)/shard_map/all_to_all | solution.py:93
  48.5 0.1 fusion.11
  48.7 0.1 multiply_reduce_fusion
  48.9 0.6 broadcast_in_dim.66
  49.5 13.4 %all-to-all-start.2 = ((bf16[64,2,96]{2,1,0:T(2,128)(2,1)}), bf16[64,2,96]{2,1,0:T(2,128)(2,1)}, u32[]{:S(2)}, u32[]{:S(2)}) async-start(bf16[64,2,96]{2,1,0:T(2,128)(2,1)} %bitcast.10), calls=%async_computation.2 | async-start | bytes 65536 | tf_op jit(solution)/shard_map/all_to_all | solution.py:93
  63.0 2.9 %shard_map.91.more_ref = f32[4608,128]{1,0:T(8,128)S(1)} custom-call(bf16[4,32,288]{2,1,0:T(8,128)(2,1)S(1)} %bitcast.33, bf16[288,4608]{1,0:T(8,128)(2,1)} %w_hbm.1), custom_call_target="tpu_custom_call" | custom-call | flops 339738624 | bytes 5013504 | tf_op jit(solution)/shard_map/pallas_call | solution.py:39
  65.9 10.6 %all-to-all-done.2 = bf16[64,2,96]{2,1,0:T(2,128)(2,1)} async-done(((bf16[64,2,96]{2,1,0:T(2,128)(2,1)}), bf16[64,2,96]{2,1,0:T(2,128)(2,1)}, u32[]{:S(2)}, u32[]{:S(2)}) %all-to-all-start.2) | async-done | bytes 24608 | tf_op jit(solution)/shard_map/all_to_all | solution.py:93
  76.6 0.8 copy.79
  77.3 1.0 shard_map.92
  78.3 1.9 %collective-permute-start.3 = (bf16[2304,128]{1,0:T(8,128)(2,1)S(1)}, bf16[2304,128]{1,0:T(8,128)(2,1)S(1)}, u32[]{:S(2)}, u32[]{:S(2)}) collective-permute-start(bf16[2304,128]{1,0:T(8,128)(2,1)S(1)} %get-tuple-element.16), channel_id=1, source_target_pairs={{0,16},{16,0},{1,17},{17,1},{2,18},{18,2},{3,19},{19,3},{4,20},{20... | collective-permute-start | bytes 1769480 | tf_op jit(solution)/shard_map/ppermute | solution.py:152
  80.3 2.0 %collective-permute-done.3 = bf16[2304,128]{1,0:T(8,128)(2,1)S(1)} collective-permute-done((bf16[2304,128]{1,0:T(8,128)(2,1)S(1)}, bf16[2304,128]{1,0:T(8,128)(2,1)S(1)}, u32[]{:S(2)}, u32[]{:S(2)}) %collective-permute-start.3) | collective-permute-done | bytes 589856 | tf_op jit(solution)/shard_map/ppermute | solution.py:152
  82.2 0.2 add_convert_fusion
  82.4 13.1 %all_to_all.26 = bf16[4,576,128]{2,1,0:T(8,128)(2,1)S(1)} all-to-all(bf16[4,576,128]{2,1,0:T(8,128)(2,1)S(1)} %bitcast.35), channel_id=1, replica_groups=mesh['gx'=4,'gyx'=4,'core'=2,'gz'=16] {'gyx'}, dimensions={0} | all-to-all | bytes 1179648 | tf_op jit(solution)/shard_map/all_to_all | solution.py:93
  95.5 0.1 reduce_sum.61
  95.6 17.9 %all_to_all.27 = bf16[16,9,4,128]{3,2,1,0:T(4,128)(2,1)S(1)} all-to-all(bf16[16,9,4,128]{3,2,1,0:T(4,128)(2,1)S(1)} %bitcast.39), channel_id=1, replica_groups=mesh['gx'=4,'gyx'=4,'core'=2,'gz'=16] {'gz'}, dimensions={0} | all-to-all | bytes 294912 | tf_op jit(solution)/shard_map/all_to_all | solution.py:93
  113.7 0.6 fusion.10
  (47 shorter events, 1.3 us)
Async XLA Ops:
  0.0 0.9 copy-start
  0.0 17.9 %copy-start.4 = (bf16[2,16,288]{2,1,0:T(8,128)(2,1)S(1)}, bf16[2,16,288]{2,1,0:T(8,128)(2,1)}, u32[]{:S(2)}) copy-start(bf16[2,16,288]{2,1,0:T(8,128)(2,1)} %param.16) | copy-start | bytes 55300
  0.0 23.4 %copy-start.6 = (bf16[2,4,512]{2,1,0:T(4,128)(2,1)S(1)}, bf16[2,4,512]{2,1,0:T(4,128)(2,1)}, u32[]{:S(2)}) copy-start(bf16[2,4,512]{2,1,0:T(4,128)(2,1)} %param.11) | copy-start | bytes 24580
  0.0 23.5 %copy-start.7 = (s32[4]{0:T(128)S(1)}, s32[4]{0:T(128)}, u32[]{:S(2)}) copy-start(s32[4]{0:T(128)} %param.14) | copy-start | bytes 52
  1.6 29.7 %all-to-all-start = ((bf16[16,4,768]{2,1,0:T(4,128)(2,1)}), bf16[16,4,768]{2,1,0:T(4,128)(2,1)S(1)}, u32[]{:S(2)}, u32[]{:S(2)}) async-start(bf16[16,4,768]{2,1,0:T(4,128)(2,1)} %reshape.185), calls=%async_computation | async-start | bytes 196608 | tf_op jit(solution)/shard_map/all_to_all | solution.py:93
  17.9 13.8 %copy-start.2 = (bf16[4,128,256]{2,1,0:T(8,128)(2,1)S(1)}, bf16[4,128,256]{2,1,0:T(8,128)(2,1)}, u32[]{:S(2)}) copy-start(bf16[4,128,256]{2,1,0:T(8,128)(2,1)} %param.12) | copy-start | bytes 786436
  17.9 5.9 %collective-permute-start.1 = (bf16[2,16,288]{2,1,0:T(8,128)(2,1)S(1)}, bf16[2,16,288]{2,1,0:T(8,128)(2,1)S(1)}, u32[]{:S(2)}, u32[]{:S(2)}) collective-permute-start(bf16[2,16,288]{2,1,0:T(8,128)(2,1)S(1)} %copy-done.4), channel_id=1, source_target_pairs={{0,128},{128,0},{256,384},{384,256},{1,129},{129,1},{257,385},{385... | collective-permute-start | bytes 55304 | tf_op jit(solution)/shard_map/ppermute | solution.py:104
  21.5 10.1 %collective-permute-start = (bf16[4,128,512]{2,1,0:T(8,128)(2,1)S(1)}, bf16[4,128,512]{2,1,0:T(8,128)(2,1)S(1)}, u32[]{:S(2)}, u32[]{:S(2)}) collective-permute-start(bf16[4,128,512]{2,1,0:T(8,128)(2,1)S(1)} %pad_maximum_fusion), channel_id=1, source_target_pairs={{0,16},{16,0},{1,17},{17,1},{2,18},{18,2},{3,19},{19,3},{4,20},{20... | collective-permute-start | bytes 1572872 | tf_op jit(solution)/shard_map/ppermute | solution.py:103
  23.8 7.5 %collective-permute-start.2 = (bf16[2,2,16,288]{3,2,1,0:T(8,128)(2,1)S(1)}, bf16[2,2,16,288]{3,2,1,0:T(8,128)(2,1)S(1)}, u32[]{:S(2)}, u32[]{:S(2)}) collective-permute-start(bf16[2,2,16,288]{3,2,1,0:T(8,128)(2,1)S(1)} %maximum_select_fusion.1), channel_id=1, source_target_pairs={{0,256},{128,384},{256,0},{384,128},{1,257},{129,385},{257,1},{385... | collective-permute-start | bytes 110600 | tf_op jit(solution)/shard_map/ppermute | solution.py:108
  31.7 1.5 %copy-start.3 = (bf16[4,128,256]{2,1,0:T(8,128)(2,1)S(1)}, bf16[4,128,256]{2,1,0:T(8,128)(2,1)}, u32[]{:S(2)}) copy-start(bf16[4,128,256]{2,1,0:T(8,128)(2,1)} %param.13) | copy-start | bytes 786436
  49.5 27.0 %all-to-all-start.2 = ((bf16[64,2,96]{2,1,0:T(2,128)(2,1)}), bf16[64,2,96]{2,1,0:T(2,128)(2,1)}, u32[]{:S(2)}, u32[]{:S(2)}) async-start(bf16[64,2,96]{2,1,0:T(2,128)(2,1)} %bitcast.10), calls=%async_computation.2 | async-start | bytes 65536 | tf_op jit(solution)/shard_map/all_to_all | solution.py:93
  63.0 14.3 %copy-start.1 = (bf16[96,4608]{1,0:T(8,128)(2,1)S(1)}, bf16[96,4608]{1,0:T(8,128)(2,1)}, u32[]{:S(2)}) copy-start(bf16[96,4608]{1,0:T(8,128)(2,1)} %w_ref.1) | copy-start | bytes 2654212
  78.3 3.9 %collective-permute-start.3 = (bf16[2304,128]{1,0:T(8,128)(2,1)S(1)}, bf16[2304,128]{1,0:T(8,128)(2,1)S(1)}, u32[]{:S(2)}, u32[]{:S(2)}) collective-permute-start(bf16[2304,128]{1,0:T(8,128)(2,1)S(1)} %get-tuple-element.16), channel_id=1, source_target_pairs={{0,16},{16,0},{1,17},{17,1},{2,18},{18,2},{3,19},{19,3},{4,20},{20... | collective-permute-start | bytes 1769480 | tf_op jit(solution)/shard_map/ppermute | solution.py:152
  82.4 31.3 %copy-start.5 = (bf16[2,64,36]{1,0,2:T(2,128)(2,1)S(1)}, bf16[2,64,36]{1,0,2:T(2,128)(2,1)}, u32[]{:S(2)}) copy-start(bf16[2,64,36]{1,0,2:T(2,128)(2,1)} %param.9) | copy-start | bytes 27652

commit v9 on v6

--- a/solution.py
+++ b/solution.py
@@ -104,9 +104,8 @@
     near = lax.ppermute(own, "gx", [(i, i ^ 1) for i in range(4)])
     keys = jnp.concatenate([key_cache, pair[..., :HD]], 1)
     values = jnp.concatenate([value_cache, pair[..., HD:]], 1)
+    near = jnp.where(gx % 2 == 0, jnp.stack([hidden, near]), jnp.stack([near, hidden]))
     keys, near = lax.optimization_barrier((keys, near))
-    near = jnp.where(gx % 2 == 0, jnp.stack([hidden, near]), jnp.stack([near, hidden]))
-    far = lax.ppermute(near, "gx", [(i, i ^ 2) for i in range(4)])
     q = exchange(query.reshape(2, 16, 4, 768).transpose(1, 2, 0, 3), "gz")
     q = lax.dynamic_index_in_dim(q.reshape(4, 2, 2, 4, 2, 768), core, 1, keepdims=False)
     qf = q.reshape(4, 2, 4, 2, 3, HD).transpose(2, 0, 1, 3, 4, 5).reshape(4, 48, HD)
@@ -145,17 +144,20 @@
     attn = attn.reshape(2, 2, 3, HD).transpose(1, 0, 2, 3).reshape(2, 16, 96).transpose(1, 0, 2)
     attn = jnp.broadcast_to(attn[:, None], (16, 4, 2, 96)).reshape(64, 2, 96)
 
+    attn, near = lax.optimization_barrier((attn, near))
+    far = lax.ppermute(near, "gx", [(i, i ^ 2) for i in range(4)])
     spread = jnp.where(gx < 2, jnp.concatenate([near, far]), jnp.concatenate([far, near]))
     feed = turned_product(spread.reshape(4, 32, 288), down_weight)
 
-    mine = exchange(attn, ("gz", "gx")).transpose(1, 0, 2).reshape(128, 96)
+    attn = jnp.pad(attn, ((0, 0), (0, 0), (0, 160)))
+    mine = exchange(attn, ("gz", "gx"))[..., :96].transpose(1, 0, 2).reshape(128, 96)
     ours, theirs = split_product(core, mine, out_weight, feed)
 
     theirs = lax.ppermute(theirs, "core", [(0, 1), (1, 0)])
     row = (ours + theirs.astype(F32)).astype(BF16).reshape(4, 576, 128)
     row = exchange(row, "gyx")
-    row = jnp.sum(row.astype(F32), 0).astype(BF16).reshape(16, 36, 128)
-    column = exchange(row, "gz")
+    row = jnp.sum(row.astype(F32), 0).astype(BF16).reshape(16, 9, 4, 128)
+    column = exchange(row, "gz").reshape(16, 36, 128)
     summed = jnp.sum(column.astype(F32), 0).reshape(36, 2, 64).transpose(1, 2, 0)
     return (summed + resid.astype(F32)).astype(BF16)
 

time: 110 us -> 113 us (1.027)
  the two profiles are of different devices: /device:TPU:32 before, /device:TPU:8 now
where the time goes in v9:
time: 113 us
  blocking collectives  48.7 us (43%)
  starting transfers between devices  32.9 us (29%)
  waiting for transfers between devices  19.8 us (18%)
  Pallas kernels  3.89 us (3%)
  local copies, waits for them, and re-layouts  3.22 us (3%)
  other arithmetic  2.81 us (2%)
    all_to_all x3, blocking collectives, exchange(): return lax.all_to_all(x, axes, split_axis=0, concat_axis=0, tiled=True)  48.7 us
    all_to_all x2, starting transfers between devices, exchange(): return lax.all_to_all(x, axes, split_axis=0, concat_axis=0, tiled=True)  22.7 us
    all_to_all x2, waiting for transfers between devices, exchange(): return lax.all_to_all(x, axes, split_axis=0, concat_axis=0, tiled=True)  12.7 us
    ppermute x1, starting transfers between devices, per_device(): far = lax.ppermute(near, 'gx', [(i, i ^ 2) for i in range(4)])  3.98 us
    ppermute x1, waiting for transfers between devices, per_device(): far = lax.ppermute(near, 'gx', [(i, i ^ 2) for i in range(4)])  3.53 us
    pallas_call x1, Pallas kernels, turned_product(): pl.pallas_call(kernel, in_specs=[in_vmem, pl.BlockSpec(memory_space=pltpu...  2.92 us
    ppermute x1, starting transfers between devices, per_device(): near = lax.ppermute(own, 'gx', [(i, i ^ 1) for i in range(4)])  2.36 us
  transfers between devices with their start and end apart: 6, of which 6 were waited for; matrix products, arithmetic and copies ran while one was open for 1% of the time, Pallas kernels for 3%

profile of v9, /device:TPU:8, one launch (start us, length us, event | category | flops | bytes accessed | tf_op | source)
XLA Modules:
  0.0 112.7 jit_solution(1531470524610493034)
XLA Ops:
  0.0 1.8 %copy.88 = bf16[2,64,768]{2,0,1:T(2,128)(2,1)} copy(bf16[2,64,768]{2,1,0:T(8,128)(2,1)} %param.10) | data formatting | bytes 393216 | tf_op jit(solution)/shard_map/reshape | solution.py:109
  1.8 15.2 %all-to-all-start = ((bf16[16,4,2,768]{3,2,1,0:T(2,128)(2,1)}), bf16[16,4,2,768]{3,2,1,0:T(2,128)(2,1)S(1)}, u32[]{:S(2)}, u32[]{:S(2)}) async-start(bf16[16,4,2,768]{3,2,1,0:T(2,128)(2,1)} %bitcast.2), calls=%async_computation | async-start | bytes 393216 | tf_op jit(solution)/shard_map/all_to_all | solution.py:93
  17.1 1.1 pad_maximum_fusion
  18.2 2.4 %collective-permute-start.1 = (bf16[2,16,288]{2,1,0:T(8,128)(2,1)S(1)}, bf16[2,16,288]{2,1,0:T(8,128)(2,1)S(1)}, u32[]{:S(2)}, u32[]{:S(2)}) collective-permute-start(bf16[2,16,288]{2,1,0:T(8,128)(2,1)S(1)} %copy-done.3), channel_id=1, source_target_pairs={{0,128},{128,0},{256,384},{384,256},{1,129},{129,1},{257,385},{385... | collective-permute-start | bytes 55304 | tf_op jit(solution)/shard_map/ppermute | solution.py:104
  20.6 1.9 %collective-permute-start = (bf16[4,128,512]{2,1,0:T(8,128)(2,1)S(1)}, bf16[4,128,512]{2,1,0:T(8,128)(2,1)S(1)}, u32[]{:S(2)}, u32[]{:S(2)}) collective-permute-start(bf16[4,128,512]{2,1,0:T(8,128)(2,1)S(1)} %pad_maximum_fusion), channel_id=1, source_target_pairs={{0,16},{16,0},{1,17},{17,1},{2,18},{18,2},{3,19},{19,3},{4,20},{20... | collective-permute-start | bytes 1572872 | tf_op jit(solution)/shard_map/ppermute | solution.py:103
  22.7 1.2 %collective-permute-done.1 = bf16[2,16,288]{2,1,0:T(8,128)(2,1)S(1)} collective-permute-done((bf16[2,16,288]{2,1,0:T(8,128)(2,1)S(1)}, bf16[2,16,288]{2,1,0:T(8,128)(2,1)S(1)}, u32[]{:S(2)}, u32[]{:S(2)}) %collective-permute-start.1) | collective-permute-done | bytes 18464 | tf_op jit(solution)/shard_map/ppermute | solution.py:104
  23.9 0.4 collective-permute-done
  24.5 9.0 %all-to-all-done = bf16[16,4,2,768]{3,2,1,0:T(2,128)(2,1)S(1)} async-done(((bf16[16,4,2,768]{3,2,1,0:T(2,128)(2,1)}), bf16[16,4,2,768]{3,2,1,0:T(2,128)(2,1)S(1)}, u32[]{:S(2)}, u32[]{:S(2)}) %all-to-all-start) | async-done | bytes 196640 | tf_op jit(solution)/shard_map/all_to_all | solution.py:93
  33.7 0.1 fusion.32
  33.8 0.4 fusion.31
  34.2 0.2 convert_reduce_fusion.1
  34.5 0.1 fusion.30
  34.7 0.2 fusion.16
  34.9 0.3 fusion.1
  35.2 13.6 %all_to_all.25 = bf16[16,16,256]{2,1,0:T(8,128)(2,1)S(1)} all-to-all(bf16[16,16,256]{2,1,0:T(8,128)(2,1)S(1)} %fusion.7), channel_id=1, replica_groups=mesh['gx'=4,'gyx'=4,'core'=2,'gz'=16] {'gx','gyx'}, dimensions={0} | all-to-all | bytes 262144 | tf_op jit(solution)/shard_map/all_to_all | solution.py:93
  48.9 0.1 multiply_reduce_fusion
  49.0 0.1 reshape.216
  49.1 0.7 pad.9
  49.8 7.5 %all-to-all-start.2 = ((bf16[64,2,256]{2,1,0:T(2,128)(2,1)}), bf16[64,2,256]{2,1,0:T(2,128)(2,1)S(1)}, u32[]{:S(2)}, u32[]{:S(2)}) async-start(bf16[64,2,256]{2,1,0:T(2,128)(2,1)} %pad.9), calls=%async_computation.2 | async-start | bytes 131072 | tf_op jit(solution)/shard_map/all_to_all | solution.py:93
  57.3 4.0 %collective-permute-start.2 = (bf16[2,2,16,288]{3,2,1,0:T(8,128)(2,1)S(1)}, bf16[2,2,16,288]{3,2,1,0:T(8,128)(2,1)S(1)}, u32[]{:S(2)}, u32[]{:S(2)}) collective-permute-start(bf16[2,2,16,288]{3,2,1,0:T(8,128)(2,1)S(1)} %maximum_select_fusion.1), channel_id=1, source_target_pairs={{0,256},{128,384},{256,0},{384,128},{1,257},{129,385},{257,1},{385... | collective-permute-start | bytes 110600 | tf_op jit(solution)/shard_map/ppermute | solution.py:148
  61.3 3.5 %collective-permute-done.2 = bf16[2,2,16,288]{3,2,1,0:T(8,128)(2,1)S(1)} collective-permute-done((bf16[2,2,16,288]{3,2,1,0:T(8,128)(2,1)S(1)}, bf16[2,2,16,288]{3,2,1,0:T(8,128)(2,1)S(1)}, u32[]{:S(2)}, u32[]{:S(2)}) %collective-permute-start.2) | collective-permute-done | bytes 36896 | tf_op jit(solution)/shard_map/ppermute | solution.py:148
  64.9 2.9 %shard_map.91.more_ref = f32[4608,128]{1,0:T(8,128)S(1)} custom-call(bf16[4,32,288]{2,1,0:T(8,128)(2,1)S(1)} %maximum_select_fusion.h_ref, bf16[288,4608]{1,0:T(8,128)(2,1)} %w_hbm.1), custom_call_target="tpu_custom_call" | custom-call | flops 339738624 | bytes 5013504 | tf_op jit(solution)/shard_map/pallas_call | solution.py:39
  67.8 3.7 %all-to-all-done.2 = bf16[64,2,256]{2,1,0:T(2,128)(2,1)S(1)} async-done(((bf16[64,2,256]{2,1,0:T(2,128)(2,1)}), bf16[64,2,256]{2,1,0:T(2,128)(2,1)S(1)}, u32[]{:S(2)}, u32[]{:S(2)}) %all-to-all-start.2) | async-done | bytes 65568 | tf_op jit(solution)/shard_map/all_to_all | solution.py:93
  71.6 1.0 shard_map.92
  72.5 1.9 %collective-permute-start.3 = (bf16[2304,128]{1,0:T(8,128)(2,1)S(1)}, bf16[2304,128]{1,0:T(8,128)(2,1)S(1)}, u32[]{:S(2)}, u32[]{:S(2)}) collective-permute-start(bf16[2304,128]{1,0:T(8,128)(2,1)S(1)} %get-tuple-element.20), channel_id=1, source_target_pairs={{0,16},{16,0},{1,17},{17,1},{2,18},{18,2},{3,19},{19,3},{4,20},{20... | collective-permute-start | bytes 1769480 | tf_op jit(solution)/shard_map/ppermute | solution.py:156
  74.5 2.0 %collective-permute-done.3 = bf16[2304,128]{1,0:T(8,128)(2,1)S(1)} collective-permute-done((bf16[2304,128]{1,0:T(8,128)(2,1)S(1)}, bf16[2304,128]{1,0:T(8,128)(2,1)S(1)}, u32[]{:S(2)}, u32[]{:S(2)}) %collective-permute-start.3) | collective-permute-done | bytes 589856 | tf_op jit(solution)/shard_map/ppermute | solution.py:156
  76.4 0.2 add_convert_fusion
  76.6 13.1 %all_to_all.26 = bf16[4,576,128]{2,1,0:T(8,128)(2,1)S(1)} all-to-all(bf16[4,576,128]{2,1,0:T(8,128)(2,1)S(1)} %bitcast.44), channel_id=1, replica_groups=mesh['gx'=4,'gyx'=4,'core'=2,'gz'=16] {'gyx'}, dimensions={0} | all-to-all | bytes 1179648 | tf_op jit(solution)/shard_map/all_to_all | solution.py:93
  89.8 0.1 reduce_sum.61
  89.9 22.0 %all_to_all.27 = bf16[16,9,4,128]{3,2,1,0:T(4,128)(2,1)S(1)} all-to-all(bf16[16,9,4,128]{3,2,1,0:T(4,128)(2,1)S(1)} %bitcast.45), channel_id=1, replica_groups=mesh['gx'=4,'gyx'=4,'core'=2,'gz'=16] {'gz'}, dimensions={0} | all-to-all | bytes 294912 | tf_op jit(solution)/shard_map/all_to_all | solution.py:93
  111.9 0.1 reshape.221
  112.0 0.6 fusion.10
  (48 shorter events, 1.0 us)
Async XLA Ops:
  0.0 18.2 %copy-start.3 = (bf16[2,16,288]{2,1,0:T(8,128)(2,1)S(1)}, bf16[2,16,288]{2,1,0:T(8,128)(2,1)}, u32[]{:S(2)}) copy-start(bf16[2,16,288]{2,1,0:T(8,128)(2,1)} %param.16) | copy-start | bytes 55300
  0.0 22.5 %copy-start.5 = (bf16[2,4,512]{2,1,0:T(4,128)(2,1)S(1)}, bf16[2,4,512]{2,1,0:T(4,128)(2,1)}, u32[]{:S(2)}) copy-start(bf16[2,4,512]{2,1,0:T(4,128)(2,1)} %param.11) | copy-start | bytes 24580
  0.0 22.5 %copy-start.6 = (s32[4]{0:T(128)S(1)}, s32[4]{0:T(128)}, u32[]{:S(2)}) copy-start(s32[4]{0:T(128)} %param.14) | copy-start | bytes 52
  1.8 31.6 %all-to-all-start = ((bf16[16,4,2,768]{3,2,1,0:T(2,128)(2,1)}), bf16[16,4,2,768]{3,2,1,0:T(2,128)(2,1)S(1)}, u32[]{:S(2)}, u32[]{:S(2)}) async-start(bf16[16,4,2,768]{3,2,1,0:T(2,128)(2,1)} %bitcast.2), calls=%async_computation | async-start | bytes 393216 | tf_op jit(solution)/shard_map/all_to_all | solution.py:93
  17.0 7.3 %copy-start.1 = (bf16[4,128,256]{2,1,0:T(8,128)(2,1)S(1)}, bf16[4,128,256]{2,1,0:T(8,128)(2,1)}, u32[]{:S(2)}) copy-start(bf16[4,128,256]{2,1,0:T(8,128)(2,1)} %param.12) | copy-start | bytes 786436
  18.2 5.7 %collective-permute-start.1 = (bf16[2,16,288]{2,1,0:T(8,128)(2,1)S(1)}, bf16[2,16,288]{2,1,0:T(8,128)(2,1)S(1)}, u32[]{:S(2)}, u32[]{:S(2)}) collective-permute-start(bf16[2,16,288]{2,1,0:T(8,128)(2,1)S(1)} %copy-done.3), channel_id=1, source_target_pairs={{0,128},{128,0},{256,384},{384,256},{1,129},{129,1},{257,385},{385... | collective-permute-start | bytes 55304 | tf_op jit(solution)/shard_map/ppermute | solution.py:104
  20.6 3.8 %collective-permute-start = (bf16[4,128,512]{2,1,0:T(8,128)(2,1)S(1)}, bf16[4,128,512]{2,1,0:T(8,128)(2,1)S(1)}, u32[]{:S(2)}, u32[]{:S(2)}) collective-permute-start(bf16[4,128,512]{2,1,0:T(8,128)(2,1)S(1)} %pad_maximum_fusion), channel_id=1, source_target_pairs={{0,16},{16,0},{1,17},{17,1},{2,18},{18,2},{3,19},{19,3},{4,20},{20... | collective-permute-start | bytes 1572872 | tf_op jit(solution)/shard_map/ppermute | solution.py:103
  24.4 10.4 %copy-start.2 = (bf16[4,128,256]{2,1,0:T(8,128)(2,1)S(1)}, bf16[4,128,256]{2,1,0:T(8,128)(2,1)}, u32[]{:S(2)}) copy-start(bf16[4,128,256]{2,1,0:T(8,128)(2,1)} %param.13) | copy-start | bytes 786436
  49.8 21.7 %all-to-all-start.2 = ((bf16[64,2,256]{2,1,0:T(2,128)(2,1)}), bf16[64,2,256]{2,1,0:T(2,128)(2,1)S(1)}, u32[]{:S(2)}, u32[]{:S(2)}) async-start(bf16[64,2,256]{2,1,0:T(2,128)(2,1)} %pad.9), calls=%async_computation.2 | async-start | bytes 131072 | tf_op jit(solution)/shard_map/all_to_all | solution.py:93
  57.3 7.5 %collective-permute-start.2 = (bf16[2,2,16,288]{3,2,1,0:T(8,128)(2,1)S(1)}, bf16[2,2,16,288]{3,2,1,0:T(8,128)(2,1)S(1)}, u32[]{:S(2)}, u32[]{:S(2)}) collective-permute-start(bf16[2,2,16,288]{3,2,1,0:T(8,128)(2,1)S(1)} %maximum_select_fusion.1), channel_id=1, source_target_pairs={{0,256},{128,384},{256,0},{384,128},{1,257},{129,385},{257,1},{385... | collective-permute-start | bytes 110600 | tf_op jit(solution)/shard_map/ppermute | solution.py:148
  64.9 6.7 %copy-start = (bf16[96,4608]{1,0:T(8,128)(2,1)S(1)}, bf16[96,4608]{1,0:T(8,128)(2,1)}, u32[]{:S(2)}) copy-start(bf16[96,4608]{1,0:T(8,128)(2,1)} %w_ref.1) | copy-start | bytes 2654212
  72.5 3.9 %collective-permute-start.3 = (bf16[2304,128]{1,0:T(8,128)(2,1)S(1)}, bf16[2304,128]{1,0:T(8,128)(2,1)S(1)}, u32[]{:S(2)}, u32[]{:S(2)}) collective-permute-start(bf16[2304,128]{1,0:T(8,128)(2,1)S(1)} %get-tuple-element.20), channel_id=1, source_target_pairs={{0,16},{16,0},{1,17},{17,1},{2,18},{18,2},{3,19},{19,3},{4,20},{20... | collective-permute-start | bytes 1769480 | tf_op jit(solution)/shard_map/ppermute | solution.py:156
  76.6 35.4 %copy-start.4 = (bf16[2,64,36]{1,0,2:T(2,128)(2,1)S(1)}, bf16[2,64,36]{1,0,2:T(2,128)(2,1)}, u32[]{:S(2)}) copy-start(bf16[2,64,36]{1,0,2:T(2,128)(2,1)} %param.9) | copy-start | bytes 27652

commit v10 on v7

--- a/solution.py
+++ b/solution.py
@@ -154,8 +154,8 @@
     theirs = lax.ppermute(theirs, "core", [(0, 1), (1, 0)])
     row = (ours + theirs.astype(F32)).astype(BF16).reshape(4, 576, 128)
     row = exchange(row, "gyx")
-    row = jnp.sum(row.astype(F32), 0).astype(BF16).reshape(16, 36, 128)
-    column = exchange(row, "gz")
+    row = jnp.sum(row.astype(F32), 0).astype(BF16).reshape(16, 9, 4, 128)
+    column = exchange(row, "gz").reshape(16, 36, 128)
     summed = jnp.sum(column.astype(F32), 0).reshape(36, 2, 64).transpose(1, 2, 0)
     return (summed + resid.astype(F32)).astype(BF16)
 

time: 109 us -> 109 us (level)
  no operation moved by 1% of the time
where the time goes in v10:
time: 109 us; the launch traced here: 108 us
  starting transfers between devices  43.7 us (40%)
  blocking collectives  30.7 us (28%)
  waiting for transfers between devices  22.1 us (20%)
  Pallas kernels  3.9 us (4%)
  other arithmetic  3.48 us (3%)
  local copies, waits for them, and re-layouts  2.9 us (3%)
    all_to_all x3, starting transfers between devices, exchange(): return lax.all_to_all(x, axes, split_axis=0, concat_axis=0, tiled=True)  30.9 us
    all_to_all x2, blocking collectives, exchange(): return lax.all_to_all(x, axes, split_axis=0, concat_axis=0, tiled=True)  30.7 us
    all_to_all x3, waiting for transfers between devices, exchange(): return lax.all_to_all(x, axes, split_axis=0, concat_axis=0, tiled=True)  20.2 us
    ppermute x1, starting transfers between devices, per_device(): far = lax.ppermute(near, 'gx', [(i, i ^ 2) for i in range(4)])  5.34 us
    ppermute x1, starting transfers between devices, per_device(): near = lax.ppermute(own, 'gx', [(i, i ^ 1) for i in range(4)])  3.62 us
    pallas_call x1, Pallas kernels, turned_product(): pl.pallas_call(kernel, in_specs=[in_vmem, pl.BlockSpec(memory_space=pltpu...  2.92 us
  transfers between devices with their start and end apart: 7, of which 4 were waited for; matrix products, arithmetic and copies ran while one was open for 2% of the time, Pallas kernels for 3%

profile of v10, /device:TPU:32, one launch (start us, length us, event | category | flops | bytes accessed | tf_op | source)
XLA Modules:
  0.0 108.2 jit_solution(9922106220613250720)
XLA Ops:
  0.0 0.9 copy-done
  0.9 0.7 reshape.196
  1.6 15.2 %all-to-all-start = ((bf16[16,4,768]{2,1,0:T(4,128)(2,1)}), bf16[16,4,768]{2,1,0:T(4,128)(2,1)S(1)}, u32[]{:S(2)}, u32[]{:S(2)}) async-start(bf16[16,4,768]{2,1,0:T(4,128)(2,1)} %reshape.196), calls=%async_computation | async-start | bytes 196608 | tf_op jit(solution)/shard_map/all_to_all | solution.py:93
  16.8 1.1 pad_maximum_fusion
  17.9 3.6 %collective-permute-start.1 = (bf16[2,16,288]{2,1,0:T(8,128)(2,1)S(1)}, bf16[2,16,288]{2,1,0:T(8,128)(2,1)S(1)}, u32[]{:S(2)}, u32[]{:S(2)}) collective-permute-start(bf16[2,16,288]{2,1,0:T(8,128)(2,1)S(1)} %copy-done.4), channel_id=1, source_target_pairs={{0,128},{128,0},{256,384},{384,256},{1,129},{129,1},{257,385},{385... | collective-permute-start | bytes 55304 | tf_op jit(solution)/shard_map/ppermute | solution.py:104
  21.5 1.9 %collective-permute-start = (bf16[4,128,512]{2,1,0:T(8,128)(2,1)S(1)}, bf16[4,128,512]{2,1,0:T(8,128)(2,1)S(1)}, u32[]{:S(2)}, u32[]{:S(2)}) collective-permute-start(bf16[4,128,512]{2,1,0:T(8,128)(2,1)S(1)} %pad_maximum_fusion), channel_id=1, source_target_pairs={{0,16},{16,0},{1,17},{17,1},{2,18},{18,2},{3,19},{19,3},{4,20},{20... | collective-permute-start | bytes 1572872 | tf_op jit(solution)/shard_map/ppermute | solution.py:103
  23.7 6.1 %all-to-all-done = bf16[16,4,768]{2,1,0:T(4,128)(2,1)S(1)} async-done(((bf16[16,4,768]{2,1,0:T(4,128)(2,1)}), bf16[16,4,768]{2,1,0:T(4,128)(2,1)S(1)}, u32[]{:S(2)}, u32[]{:S(2)}) %all-to-all-start) | async-done | bytes 98336 | tf_op jit(solution)/shard_map/all_to_all | solution.py:93
  29.9 0.1 copy.89
  30.0 0.2 fusion.31
  30.3 0.4 fusion.30
  30.7 0.2 convert_reduce_fusion.1
  31.1 0.2 fusion.16
  31.4 0.3 fusion.1
  31.7 0.7 fusion.7
  32.3 7.0 %all-to-all-start.1 = ((bf16[16,16,256]{2,1,0:T(8,128)(2,1)}), bf16[16,16,256]{2,1,0:T(8,128)(2,1)S(1)}, u32[]{:S(2)}, u32[]{:S(2)}) async-start(bf16[16,16,256]{2,1,0:T(8,128)(2,1)} %fusion.7), calls=%async_computation.1 | async-start | bytes 262144 | tf_op jit(solution)/shard_map/all_to_all | solution.py:93
  39.4 5.3 %collective-permute-start.2 = (bf16[2,2,16,288]{3,2,1,0:T(8,128)(2,1)S(1)}, bf16[2,2,16,288]{3,2,1,0:T(8,128)(2,1)S(1)}, u32[]{:S(2)}, u32[]{:S(2)}) collective-permute-start(bf16[2,2,16,288]{3,2,1,0:T(8,128)(2,1)S(1)} %maximum_select_fusion.2), channel_id=1, source_target_pairs={{0,256},{128,384},{256,0},{384,128},{1,257},{129,385},{257,1},{385... | collective-permute-start | bytes 110600 | tf_op jit(solution)/shard_map/ppermute | solution.py:109
  44.8 2.6 %all-to-all-done.1 = bf16[16,16,256]{2,1,0:T(8,128)(2,1)S(1)} async-done(((bf16[16,16,256]{2,1,0:T(8,128)(2,1)}), bf16[16,16,256]{2,1,0:T(8,128)(2,1)S(1)}, u32[]{:S(2)}, u32[]{:S(2)}) %all-to-all-start.1) | async-done | bytes 131104 | tf_op jit(solution)/shard_map/all_to_all | solution.py:93
  47.5 0.1 multiply_reduce_fusion
  47.6 0.1 convert_element_type.138
  47.7 0.7 copy.97
  48.4 8.7 %all-to-all-start.2 = ((bf16[128,1,96]{2,1,0:T(2,128)(2,1)}), bf16[128,1,96]{2,1,0:T(2,128)(2,1)S(1)}, u32[]{:S(2)}, u32[]{:S(2)}) async-start(bf16[128,1,96]{2,1,0:T(2,128)(2,1)} %copy.97), calls=%async_computation.2 | async-start | bytes 131072 | tf_op jit(solution)/shard_map/all_to_all | solution.py:93
  57.2 2.9 %shard_map.91.more_ref = f32[4608,128]{1,0:T(8,128)S(1)} custom-call(bf16[4,32,288]{2,1,0:T(8,128)(2,1)S(1)} %maximum_select_fusion.h_ref, bf16[288,4608]{1,0:T(8,128)(2,1)} %w_hbm.1), custom_call_target="tpu_custom_call" | custom-call | flops 339738624 | bytes 5013504 | tf_op jit(solution)/shard_map/pallas_call | solution.py:39
  60.1 11.4 %all-to-all-done.2 = bf16[128,1,96]{2,1,0:T(2,128)(2,1)S(1)} async-done(((bf16[128,1,96]{2,1,0:T(2,128)(2,1)}), bf16[128,1,96]{2,1,0:T(2,128)(2,1)S(1)}, u32[]{:S(2)}, u32[]{:S(2)}) %all-to-all-start.2) | async-done | bytes 24608 | tf_op jit(solution)/shard_map/all_to_all | solution.py:93
  71.5 1.0 shard_map.92
  72.5 1.9 %collective-permute-start.3 = (bf16[2304,128]{1,0:T(8,128)(2,1)S(1)}, bf16[2304,128]{1,0:T(8,128)(2,1)S(1)}, u32[]{:S(2)}, u32[]{:S(2)}) collective-permute-start(bf16[2304,128]{1,0:T(8,128)(2,1)S(1)} %get-tuple-element.16), channel_id=1, source_target_pairs={{0,16},{16,0},{1,17},{17,1},{2,18},{18,2},{3,19},{19,3},{4,20},{20... | collective-permute-start | bytes 1769480 | tf_op jit(solution)/shard_map/ppermute | solution.py:154
  74.4 2.0 %collective-permute-done.3 = bf16[2304,128]{1,0:T(8,128)(2,1)S(1)} collective-permute-done((bf16[2304,128]{1,0:T(8,128)(2,1)S(1)}, bf16[2304,128]{1,0:T(8,128)(2,1)S(1)}, u32[]{:S(2)}, u32[]{:S(2)}) %collective-permute-start.3) | collective-permute-done | bytes 589856 | tf_op jit(solution)/shard_map/ppermute | solution.py:154
  76.4 0.2 add_convert_fusion
  76.6 13.1 %all_to_all.25 = bf16[4,576,128]{2,1,0:T(8,128)(2,1)S(1)} all-to-all(bf16[4,576,128]{2,1,0:T(8,128)(2,1)S(1)} %bitcast.43), channel_id=1, replica_groups=mesh['gx'=4,'gyx'=4,'core'=2,'gz'=16] {'gyx'}, dimensions={0} | all-to-all | bytes 1179648 | tf_op jit(solution)/shard_map/all_to_all | solution.py:93
  89.7 0.1 reduce_sum.61
  89.8 17.5 %all_to_all.26 = bf16[16,9,4,128]{3,2,1,0:T(4,128)(2,1)S(1)} all-to-all(bf16[16,9,4,128]{3,2,1,0:T(4,128)(2,1)S(1)} %bitcast.44), channel_id=1, replica_groups=mesh['gx'=4,'gyx'=4,'core'=2,'gz'=16] {'gz'}, dimensions={0} | all-to-all | bytes 294912 | tf_op jit(solution)/shard_map/all_to_all | solution.py:93
  107.4 0.1 reshape.206
  107.5 0.6 fusion.10
  (50 shorter events, 0.9 us)
Async XLA Ops:
  0.0 0.9 copy-start
  0.0 17.9 %copy-start.4 = (bf16[2,16,288]{2,1,0:T(8,128)(2,1)S(1)}, bf16[2,16,288]{2,1,0:T(8,128)(2,1)}, u32[]{:S(2)}) copy-start(bf16[2,16,288]{2,1,0:T(8,128)(2,1)} %param.16) | copy-start | bytes 55300
  0.0 23.5 %copy-start.7 = (s32[4]{0:T(128)S(1)}, s32[4]{0:T(128)}, u32[]{:S(2)}) copy-start(s32[4]{0:T(128)} %param.14) | copy-start | bytes 52
  0.0 23.6 %copy-start.6 = (bf16[2,4,512]{2,1,0:T(4,128)(2,1)S(1)}, bf16[2,4,512]{2,1,0:T(4,128)(2,1)}, u32[]{:S(2)}) copy-start(bf16[2,4,512]{2,1,0:T(4,128)(2,1)} %param.11) | copy-start | bytes 24580
  1.6 28.2 %all-to-all-start = ((bf16[16,4,768]{2,1,0:T(4,128)(2,1)}), bf16[16,4,768]{2,1,0:T(4,128)(2,1)S(1)}, u32[]{:S(2)}, u32[]{:S(2)}) async-start(bf16[16,4,768]{2,1,0:T(4,128)(2,1)} %reshape.196), calls=%async_computation | async-start | bytes 196608 | tf_op jit(solution)/shard_map/all_to_all | solution.py:93
  17.9 12.3 %copy-start.2 = (bf16[4,128,256]{2,1,0:T(8,128)(2,1)S(1)}, bf16[4,128,256]{2,1,0:T(8,128)(2,1)}, u32[]{:S(2)}) copy-start(bf16[4,128,256]{2,1,0:T(8,128)(2,1)} %param.12) | copy-start | bytes 786436
  17.9 12.4 %collective-permute-start.1 = (bf16[2,16,288]{2,1,0:T(8,128)(2,1)S(1)}, bf16[2,16,288]{2,1,0:T(8,128)(2,1)S(1)}, u32[]{:S(2)}, u32[]{:S(2)}) collective-permute-start(bf16[2,16,288]{2,1,0:T(8,128)(2,1)S(1)} %copy-done.4), channel_id=1, source_target_pairs={{0,128},{128,0},{256,384},{384,256},{1,129},{129,1},{257,385},{385... | collective-permute-start | bytes 55304 | tf_op jit(solution)/shard_map/ppermute | solution.py:104
  21.5 8.6 %collective-permute-start = (bf16[4,128,512]{2,1,0:T(8,128)(2,1)S(1)}, bf16[4,128,512]{2,1,0:T(8,128)(2,1)S(1)}, u32[]{:S(2)}, u32[]{:S(2)}) collective-permute-start(bf16[4,128,512]{2,1,0:T(8,128)(2,1)S(1)} %pad_maximum_fusion), channel_id=1, source_target_pairs={{0,16},{16,0},{1,17},{17,1},{2,18},{18,2},{3,19},{19,3},{4,20},{20... | collective-permute-start | bytes 1572872 | tf_op jit(solution)/shard_map/ppermute | solution.py:103
  30.2 1.2 %copy-start.3 = (bf16[4,128,256]{2,1,0:T(8,128)(2,1)S(1)}, bf16[4,128,256]{2,1,0:T(8,128)(2,1)}, u32[]{:S(2)}) copy-start(bf16[4,128,256]{2,1,0:T(8,128)(2,1)} %param.13) | copy-start | bytes 786436
  32.3 15.0 %all-to-all-start.1 = ((bf16[16,16,256]{2,1,0:T(8,128)(2,1)}), bf16[16,16,256]{2,1,0:T(8,128)(2,1)S(1)}, u32[]{:S(2)}, u32[]{:S(2)}) async-start(bf16[16,16,256]{2,1,0:T(8,128)(2,1)} %fusion.7), calls=%async_computation.1 | async-start | bytes 262144 | tf_op jit(solution)/shard_map/all_to_all | solution.py:93
  39.4 17.7 %collective-permute-start.2 = (bf16[2,2,16,288]{3,2,1,0:T(8,128)(2,1)S(1)}, bf16[2,2,16,288]{3,2,1,0:T(8,128)(2,1)S(1)}, u32[]{:S(2)}, u32[]{:S(2)}) collective-permute-start(bf16[2,2,16,288]{3,2,1,0:T(8,128)(2,1)S(1)} %maximum_select_fusion.2), channel_id=1, source_target_pairs={{0,256},{128,384},{256,0},{384,128},{1,257},{129,385},{257,1},{385... | collective-permute-start | bytes 110600 | tf_op jit(solution)/shard_map/ppermute | solution.py:109
  48.4 23.1 %all-to-all-start.2 = ((bf16[128,1,96]{2,1,0:T(2,128)(2,1)}), bf16[128,1,96]{2,1,0:T(2,128)(2,1)S(1)}, u32[]{:S(2)}, u32[]{:S(2)}) async-start(bf16[128,1,96]{2,1,0:T(2,128)(2,1)} %copy.97), calls=%async_computation.2 | async-start | bytes 131072 | tf_op jit(solution)/shard_map/all_to_all | solution.py:93
  57.1 14.4 %copy-start.1 = (bf16[96,4608]{1,0:T(8,128)(2,1)S(1)}, bf16[96,4608]{1,0:T(8,128)(2,1)}, u32[]{:S(2)}) copy-start(bf16[96,4608]{1,0:T(8,128)(2,1)} %w_ref.1) | copy-start | bytes 2654212
  72.5 3.9 %collective-permute-start.3 = (bf16[2304,128]{1,0:T(8,128)(2,1)S(1)}, bf16[2304,128]{1,0:T(8,128)(2,1)S(1)}, u32[]{:S(2)}, u32[]{:S(2)}) collective-permute-start(bf16[2304,128]{1,0:T(8,128)(2,1)S(1)} %get-tuple-element.16), channel_id=1, source_target_pairs={{0,16},{16,0},{1,17},{17,1},{2,18},{18,2},{3,19},{19,3},{4,20},{20... | collective-permute-start | bytes 1769480 | tf_op jit(solution)/shard_map/ppermute | solution.py:154
  76.6 31.0 %copy-start.5 = (bf16[2,64,36]{1,0,2:T(2,128)(2,1)S(1)}, bf16[2,64,36]{1,0,2:T(2,128)(2,1)}, u32[]{:S(2)}) copy-start(bf16[2,64,36]{1,0,2:T(2,128)(2,1)} %param.9) | copy-start | bytes 27652

commit v11 on v10

--- a/solution.py
+++ b/solution.py
@@ -10,6 +10,7 @@
 HD = 256
 F32 = jnp.float32
 BF16 = jnp.bfloat16
+GX = ("gxh", "gxl")
 GY = ("gyx", "core")
 NEG = -1e30
 TILE = 1152
@@ -96,30 +97,41 @@
 def per_device(
     resid, query, new_kv, key_cache, value_cache, lengths, out_weight, hidden, down_weight
 ):
-    gx, gyx, core = lax.axis_index("gx"), lax.axis_index("gyx"), lax.axis_index("core")
+    high, low, core = lax.axis_index("gxh"), lax.axis_index("gxl"), lax.axis_index("core")
+    gy = lax.axis_index(GY)
 
-    pair = jnp.concatenate([key_cache, value_cache], -1)
-    pair, own = lax.optimization_barrier((pair, hidden))
-    pair = lax.ppermute(pair, "core", [(0, 1), (1, 0)])
-    near = lax.ppermute(own, "gx", [(i, i ^ 1) for i in range(4)])
-    keys = jnp.concatenate([key_cache, pair[..., :HD]], 1)
-    values = jnp.concatenate([value_cache, pair[..., HD:]], 1)
+    cache = jnp.concatenate([key_cache, value_cache], -1).reshape(2, 2, 128, 2 * HD)
+    other = lax.dynamic_index_in_dim(cache, 1 - low, 1, False).reshape(256, 2 * HD)
+    own = jnp.pad(hidden.reshape(32, 288), ((0, 0), (0, 2 * HD - 288)))
+    other = lax.ppermute(jnp.concatenate([other, own], 0), "gxl", [(0, 1), (1, 0)])
+    near = other[256:, :288].reshape(2, 16, 288)
+    other = other[:256].reshape(2, 128, 2 * HD)
+    ours_of = lambda c: lax.dynamic_index_in_dim(c.reshape(2, 2, 128, HD), low, 1, False)
+    keys = jnp.concatenate([ours_of(key_cache), other[..., :HD]], 1)
+    values = jnp.concatenate([ours_of(value_cache), other[..., HD:]], 1)
     keys, near = lax.optimization_barrier((keys, near))
-    near = jnp.where(gx % 2 == 0, jnp.stack([hidden, near]), jnp.stack([near, hidden]))
-    far = lax.ppermute(near, "gx", [(i, i ^ 2) for i in range(4)])
-    q = lax.dynamic_index_in_dim(query, core, 0, keepdims=False)
+    near = jnp.where(low == 0, jnp.stack([hidden, near]), jnp.stack([near, hidden]))
+    far = lax.ppermute(near, "gxh", [(0, 1), (1, 0)])
+
+    pick = jnp.arange(64)
+    pick = (pick // 2 % 2) * 64 + (pick // 4) * 4 + (pick % 2) * 2 + low
+    pick = (pick[:, None] == jnp.arange(128)[None, :]).astype(BF16)
+    q = jnp.dot(pick, query.reshape(128, 768), preferred_element_type=F32).astype(BF16)
     q = exchange(q.reshape(16, 4, 768), "gz")
-    qf = q.reshape(16, 4, 3, HD).transpose(1, 0, 2, 3).reshape(4, HEADS, HD)
+    qf = q.reshape(16, 2, 2, 3, HD).transpose(2, 0, 1, 3, 4).reshape(2, 96, HD)
 
     at = jnp.arange(256, dtype=jnp.int32)
-    owner = gx * 8 + gyx * 2 + jnp.where(at < 128, core, 1 - core)
+    owner = (high * 2 + jnp.where(at < 128, low, 1 - low)) * 8 + gy
     positions = owner * 128 + at % 128
-    present = (positions[None] < lengths[:, None])[:, None]
+    length = lax.dynamic_index_in_dim(lengths.reshape(2, 2), low, 1, False)
+    fresh = lax.dynamic_index_in_dim(new_kv.reshape(2, 2, 2, 2 * HD), low, 2, False)
+    present = (positions[None] < length[:, None])[:, None]
     scale = HD**-0.5
     s = jnp.einsum("bqd,bpd->bqp", qf, keys, preferred_element_type=F32) * scale
     s = jnp.where(present, s, NEG)
-    allowed = ((jnp.arange(2) <= core) & (gx + gyx == 0))[None, None]
-    sn = jnp.einsum("bqd,ubd->bqu", qf, new_kv[..., :HD], preferred_element_type=F32) * scale
+    step = (jnp.arange(96) // 3) % 2
+    allowed = (jnp.arange(2)[None, :] <= step[:, None]) & (high + gy == 0)
+    sn = jnp.einsum("bqd,ubd->bqu", qf, fresh[..., :HD], preferred_element_type=F32) * scale
     sn = jnp.where(allowed, sn, NEG)
     peak = jnp.maximum(jnp.max(s, -1), jnp.max(sn, -1)).astype(BF16)
     pf = peak.astype(F32)[..., None]
@@ -127,28 +139,27 @@
     wn = jnp.where(allowed, jnp.exp(sn - pf), 0.0).astype(BF16)
     total = jnp.sum(w.astype(F32), -1) + jnp.sum(wn.astype(F32), -1)
     acc = jnp.einsum("bqp,bpd->bqd", w, values, preferred_element_type=F32)
-    acc = acc + jnp.einsum("bqu,ubd->bqd", wn, new_kv[..., HD:], preferred_element_type=F32)
+    acc = acc + jnp.einsum("bqu,ubd->bqd", wn, fresh[..., HD:], preferred_element_type=F32)
     total_hi = total.astype(BF16)
     total_lo = (total - total_hi.astype(F32)).astype(BF16)
     stats = jnp.stack([peak, total_hi, total_lo, jnp.zeros_like(peak)], 1)
-    stats = stats.reshape(4, 4, 4, 12).transpose(0, 2, 1, 3).reshape(16, 4, 12)
+    stats = stats.reshape(2, 4, 8, 12).transpose(0, 2, 1, 3).reshape(16, 4, 12)
     stats = jnp.pad(stats, ((0, 0), (0, 0), (0, HD - 12)))
     message = jnp.concatenate([acc.astype(BF16).reshape(16, 12, HD), stats], 1)
 
-    message = exchange(message, ("gx", "gyx"))
+    message = exchange(message, ("gxh",) + GY)
     peaks = message[:, 12, :12].astype(F32)
     totals = message[:, 13, :12].astype(F32) + message[:, 14, :12].astype(F32)
     share = jnp.exp(peaks - jnp.max(peaks, 0))
     share = share / jnp.sum(share * totals, 0)
     attn = jnp.sum(message[:, :12].astype(F32) * share[..., None], 0).astype(BF16)
-    attn = attn.reshape(2, 16, 96).transpose(1, 0, 2)
-    attn = jnp.broadcast_to(attn[:, None], (16, 4, 2, 96)).reshape(128, 1, 96)
+    attn = attn.reshape(2, 2, 3, HD).transpose(1, 0, 2, 3).reshape(2, 16, 96).transpose(1, 0, 2)
+    attn = jnp.broadcast_to(attn[:, None], (16, 4, 2, 96)).reshape(64, 2, 96)
 
-    spread = jnp.where(gx < 2, jnp.concatenate([near, far]), jnp.concatenate([far, near]))
+    spread = jnp.where(high == 0, jnp.concatenate([near, far]), jnp.concatenate([far, near]))
     feed = turned_product(spread.reshape(4, 32, 288), down_weight)
 
-    mine = exchange(attn, ("gz", "gx", "core"))
-    mine = mine.reshape(64, 2, 96).transpose(1, 0, 2).reshape(128, 96)
+    mine = exchange(attn, ("gz",) + GX).transpose(1, 0, 2).reshape(128, 96)
     ours, theirs = split_product(core, mine, out_weight, feed)
 
     theirs = lax.ppermute(theirs, "core", [(0, 1), (1, 0)])
@@ -161,19 +172,19 @@
 
 
 def solution(mesh):
-    mesh = Mesh(mesh.devices.reshape(4, 4, 2, 16), ("gx", "gyx", "core", "gz"))
+    mesh = Mesh(mesh.devices.reshape(2, 2, 4, 2, 16), GX + GY + ("gz",))
     rows = GY + ("gz",)
-    width = P(None, None, ("gx",) + rows)
+    width = P(None, None, GX + rows)
     in_specs = (
         width,
         P(None, None, "gz"),
         P(None, "gz", None),
-        P("gz", ("gx",) + GY, None),
-        P("gz", ("gx",) + GY, None),
+        P("gz", GX + GY, None),
+        P("gz", GX + GY, None),
         P("gz"),
-        P(rows, "gx"),
-        P(None, "gx", rows),
-        P(rows, "gx"),
+        P(rows, GX),
+        P(None, GX, rows),
+        P(rows, GX),
     )
     return jax.shard_map(
         per_device, mesh=mesh, in_specs=in_specs, out_specs=width, check_vma=False

time: 109 us -> 111 us (1.018)
    ppermute x3 -> x2, waiting for transfers between devices: 0.01 us -> 5.98 us  [the longest x1 5.98 us: per_device(): lax.ppermute(jnp.concatenate([other, own], 0), 'gxl', [(0, 1), (1, 0)])]
    all_to_all x3, waiting for transfers between devices: 20.2 us -> 15 us  [exchange(): return lax.all_to_all(x, axes, split_axis=0, concat_axis=0, tiled=True)]
    all_to_all x3, starting transfers between devices: 30.9 us -> 33.4 us  [exchange(): return lax.all_to_all(x, axes, split_axis=0, concat_axis=0, tiled=True)]
    ppermute x3 -> x2, starting transfers between devices: 10.9 us -> 8.82 us  [the longest x1 5.34 us: per_device(): far = lax.ppermute(near, 'gxh', [(0, 1), (1, 0)])]
  transfers between devices with their start and end apart: 7 -> 6, of which waited for: 4 -> 5; matrix products, arithmetic and copies ran while one was open for 2% -> 2% of each run, Pallas kernels for 3% -> 3%
where the time goes in v11:
time: 111 us
  starting transfers between devices  44.2 us (40%)
  blocking collectives  31.3 us (28%)
  waiting for transfers between devices  22.9 us (21%)
  Pallas kernels  3.9 us (4%)
  other arithmetic  3.49 us (3%)
  local copies, waits for them, and re-layouts  3.32 us (3%)
  matrix products  1.11 us (1%)
    all_to_all x3, starting transfers between devices, exchange(): return lax.all_to_all(x, axes, split_axis=0, concat_axis=0, tiled=True)  33.4 us
    all_to_all x2, blocking collectives, exchange(): return lax.all_to_all(x, axes, split_axis=0, concat_axis=0, tiled=True)  31.3 us
    all_to_all x3, waiting for transfers between devices, exchange(): return lax.all_to_all(x, axes, split_axis=0, concat_axis=0, tiled=True)  15 us
    ppermute x1, waiting for transfers between devices, per_device(): lax.ppermute(jnp.concatenate([other, own], 0), 'gxl', [(0, 1), (1, 0)])  5.98 us
    ppermute x1, starting transfers between devices, per_device(): far = lax.ppermute(near, 'gxh', [(0, 1), (1, 0)])  5.34 us
    ppermute x1, starting transfers between devices, per_device(): lax.ppermute(jnp.concatenate([other, own], 0), 'gxl', [(0, 1), (1, 0)])  3.48 us
    pallas_call x1, Pallas kernels, turned_product(): pl.pallas_call(kernel, in_specs=[in_vmem, pl.BlockSpec(memory_space=pltpu...  2.93 us
  transfers between devices with their start and end apart: 6, of which 5 were waited for; matrix products, arithmetic and copies ran while one was open for 2% of the time, Pallas kernels for 3%

profile of v11, /device:TPU:32, one launch (start us, length us, event | category | flops | bytes accessed | tf_op | source)
XLA Modules:
  0.0 110.6 jit_solution(3441359642271422344)
XLA Ops:
  0.0 0.9 copy-done
  0.9 0.2 convolution_convert_fusion
  1.1 0.7 reshape.317
  1.8 15.3 %all-to-all-start = ((bf16[16,4,768]{2,1,0:T(4,128)(2,1)}), bf16[16,4,768]{2,1,0:T(4,128)(2,1)S(1)}, u32[]{:S(2)}, u32[]{:S(2)}) async-start(bf16[16,4,768]{2,1,0:T(4,128)(2,1)} %reshape.317), calls=%async_computation | async-start | bytes 196608 | tf_op jit(solution)/shard_map/all_to_all | solution.py:94
  17.2 1.1 %pad_maximum_fusion = bf16[4,128,512]{2,1,0:T(8,128)(2,1)S(1)} fusion(bf16[4,128,256]{2,1,0:T(8,128)(2,1)} %param.13, bf16[4,128,256]{2,1,0:T(8,128)(2,1)} %param.12), kind=kLoop, calls=%fused_computation.10 | loop fusion | flops 1048576 | bytes 1048576 | tf_op jit(solution)/shard_map/concatenate | solution.py:103
  18.3 3.5 %collective-permute-start = (bf16[288,512]{1,0:T(8,128)(2,1)S(1)}, bf16[288,512]{1,0:T(8,128)(2,1)S(1)}, u32[]{:S(2)}, u32[]{:S(2)}) collective-permute-start(bf16[288,512]{1,0:T(8,128)(2,1)S(1)} %fusion.4), channel_id=1, source_target_pairs={{0,128},{128,0},{1,129},{129,1},{2,130},{130,2},{3,131},{131,3},{4... | collective-permute-start | bytes 884744 | tf_op jit(solution)/shard_map/ppermute | solution.py:106
  22.0 0.2 fusion.23
  22.5 6.0 %collective-permute-done = bf16[288,512]{1,0:T(8,128)(2,1)S(1)} collective-permute-done((bf16[288,512]{1,0:T(8,128)(2,1)S(1)}, bf16[288,512]{1,0:T(8,128)(2,1)S(1)}, u32[]{:S(2)}, u32[]{:S(2)}) %collective-permute-start) | collective-permute-done | bytes 294944 | tf_op jit(solution)/shard_map/ppermute | solution.py:106
  28.5 1.6 %all-to-all-done = bf16[16,4,768]{2,1,0:T(4,128)(2,1)S(1)} async-done(((bf16[16,4,768]{2,1,0:T(4,128)(2,1)}), bf16[16,4,768]{2,1,0:T(4,128)(2,1)S(1)}, u32[]{:S(2)}, u32[]{:S(2)}) %all-to-all-start) | async-done | bytes 98336 | tf_op jit(solution)/shard_map/all_to_all | solution.py:94
  30.2 0.1 copy.77
  30.3 0.1 fusion.43
  30.5 0.3 fusion.42
  30.8 0.2 convert_reduce_fusion.1
  31.3 0.2 fusion.5
  31.5 0.2 fusion.1
  31.8 0.7 fusion.10
  32.5 7.0 %all-to-all-start.1 = ((bf16[16,16,256]{2,1,0:T(8,128)(2,1)}), bf16[16,16,256]{2,1,0:T(8,128)(2,1)S(1)}, u32[]{:S(2)}, u32[]{:S(2)}) async-start(bf16[16,16,256]{2,1,0:T(8,128)(2,1)} %fusion.10), calls=%async_computation.1 | async-start | bytes 262144 | tf_op jit(solution)/shard_map/all_to_all | solution.py:94
  39.6 5.3 %collective-permute-start.1 = (bf16[2,2,16,288]{3,2,1,0:T(8,128)(2,1)S(1)}, bf16[2,2,16,288]{3,2,1,0:T(8,128)(2,1)S(1)}, u32[]{:S(2)}, u32[]{:S(2)}) collective-permute-start(bf16[2,2,16,288]{3,2,1,0:T(8,128)(2,1)S(1)} %maximum_select_fusion.2), channel_id=1, source_target_pairs={{0,256},{256,0},{1,257},{257,1},{2,258},{258,2},{3,259},{259,3},{4... | collective-permute-start | bytes 110600 | tf_op jit(solution)/shard_map/ppermute | solution.py:114
  44.9 2.6 %all-to-all-done.1 = bf16[16,16,256]{2,1,0:T(8,128)(2,1)S(1)} async-done(((bf16[16,16,256]{2,1,0:T(8,128)(2,1)}), bf16[16,16,256]{2,1,0:T(8,128)(2,1)S(1)}, u32[]{:S(2)}, u32[]{:S(2)}) %all-to-all-start.1) | async-done | bytes 131104 | tf_op jit(solution)/shard_map/all_to_all | solution.py:94
  47.6 0.1 multiply_reduce_fusion
  47.9 0.6 broadcast_in_dim.63
  48.5 11.1 %all-to-all-start.2 = ((bf16[64,2,96]{2,1,0:T(2,128)(2,1)}), bf16[64,2,96]{2,1,0:T(2,128)(2,1)S(1)}, u32[]{:S(2)}, u32[]{:S(2)}) async-start(bf16[64,2,96]{2,1,0:T(2,128)(2,1)} %bitcast.20), calls=%async_computation.2 | async-start | bytes 65536 | tf_op jit(solution)/shard_map/all_to_all | solution.py:94
  59.6 2.9 %shard_map.91.more_ref = f32[4608,128]{1,0:T(8,128)S(1)} custom-call(bf16[4,32,288]{2,1,0:T(8,128)(2,1)S(1)} %maximum_select_fusion.h_ref, bf16[288,4608]{1,0:T(8,128)(2,1)} %w_hbm.1), custom_call_target="tpu_custom_call" | custom-call | flops 339738624 | bytes 5013504 | tf_op jit(solution)/shard_map/pallas_call | solution.py:40
  62.6 10.8 %all-to-all-done.2 = bf16[64,2,96]{2,1,0:T(2,128)(2,1)S(1)} async-done(((bf16[64,2,96]{2,1,0:T(2,128)(2,1)}), bf16[64,2,96]{2,1,0:T(2,128)(2,1)S(1)}, u32[]{:S(2)}, u32[]{:S(2)}) %all-to-all-start.2) | async-done | bytes 24608 | tf_op jit(solution)/shard_map/all_to_all | solution.py:94
  73.3 1.0 shard_map.92
  74.3 1.9 %collective-permute-start.2 = (bf16[2304,128]{1,0:T(8,128)(2,1)S(1)}, bf16[2304,128]{1,0:T(8,128)(2,1)S(1)}, u32[]{:S(2)}, u32[]{:S(2)}) collective-permute-start(bf16[2304,128]{1,0:T(8,128)(2,1)S(1)} %get-tuple-element.12), channel_id=1, source_target_pairs={{0,16},{16,0},{1,17},{17,1},{2,18},{18,2},{3,19},{19,3},{4,20},{20... | collective-permute-start | bytes 1769480 | tf_op jit(solution)/shard_map/ppermute | solution.py:165
  76.2 2.0 %collective-permute-done.2 = bf16[2304,128]{1,0:T(8,128)(2,1)S(1)} collective-permute-done((bf16[2304,128]{1,0:T(8,128)(2,1)S(1)}, bf16[2304,128]{1,0:T(8,128)(2,1)S(1)}, u32[]{:S(2)}, u32[]{:S(2)}) %collective-permute-start.2) | collective-permute-done | bytes 589856 | tf_op jit(solution)/shard_map/ppermute | solution.py:165
  78.2 0.2 add_convert_fusion
  78.4 13.1 %all_to_all.25 = bf16[4,576,128]{2,1,0:T(8,128)(2,1)S(1)} all-to-all(bf16[4,576,128]{2,1,0:T(8,128)(2,1)S(1)} %bitcast.57), channel_id=1, replica_groups=mesh['gxh'=2,'gxl'=2,'gyx'=4,'core'=2,'gz'=16] {'gyx'}, dimensions={0} | all-to-all | bytes 1179648 | tf_op jit(solution)/shard_map/all_to_all | solution.py:94
  91.5 0.1 reduce_sum.61
  91.6 18.1 %all_to_all.26 = bf16[16,9,4,128]{3,2,1,0:T(4,128)(2,1)S(1)} all-to-all(bf16[16,9,4,128]{3,2,1,0:T(4,128)(2,1)S(1)} %bitcast.61), channel_id=1, replica_groups=mesh['gxh'=2,'gxl'=2,'gyx'=4,'core'=2,'gz'=16] {'gz'}, dimensions={0} | all-to-all | bytes 294912 | tf_op jit(solution)/shard_map/all_to_all | solution.py:94
  109.9 0.6 fusion.13
  (59 shorter events, 1.3 us)
Async XLA Ops:
  0.0 0.9 copy-start
  0.0 18.3 %copy-start.4 = (bf16[2,16,288]{2,1,0:T(8,128)(2,1)S(1)}, bf16[2,16,288]{2,1,0:T(8,128)(2,1)}, u32[]{:S(2)}) copy-start(bf16[2,16,288]{2,1,0:T(8,128)(2,1)} %param.16) | copy-start | bytes 55300
  1.8 20.1 %copy-start.7 = (s32[4]{0:T(128)S(1)}, s32[4]{0:T(128)}, u32[]{:S(2)}) copy-start(s32[4]{0:T(128)} %param.14) | copy-start | bytes 52
  1.8 20.2 %copy-start.6 = (bf16[2,4,512]{2,1,0:T(4,128)(2,1)S(1)}, bf16[2,4,512]{2,1,0:T(4,128)(2,1)}, u32[]{:S(2)}) copy-start(bf16[2,4,512]{2,1,0:T(4,128)(2,1)} %param.11) | copy-start | bytes 24580
  1.8 20.4 %copy-start.2 = (bf16[4,128,256]{2,1,0:T(8,128)(2,1)S(1)}, bf16[4,128,256]{2,1,0:T(8,128)(2,1)}, u32[]{:S(2)}) copy-start(bf16[4,128,256]{2,1,0:T(8,128)(2,1)} %param.13) | copy-start | bytes 786436
  1.8 28.3 %all-to-all-start = ((bf16[16,4,768]{2,1,0:T(4,128)(2,1)}), bf16[16,4,768]{2,1,0:T(4,128)(2,1)S(1)}, u32[]{:S(2)}, u32[]{:S(2)}) async-start(bf16[16,4,768]{2,1,0:T(4,128)(2,1)} %reshape.317), calls=%async_computation | async-start | bytes 196608 | tf_op jit(solution)/shard_map/all_to_all | solution.py:94
  17.2 5.1 %copy-start.3 = (bf16[4,128,256]{2,1,0:T(8,128)(2,1)S(1)}, bf16[4,128,256]{2,1,0:T(8,128)(2,1)}, u32[]{:S(2)}) copy-start(bf16[4,128,256]{2,1,0:T(8,128)(2,1)} %param.12) | copy-start | bytes 786436
  18.3 10.1 %collective-permute-start = (bf16[288,512]{1,0:T(8,128)(2,1)S(1)}, bf16[288,512]{1,0:T(8,128)(2,1)S(1)}, u32[]{:S(2)}, u32[]{:S(2)}) collective-permute-start(bf16[288,512]{1,0:T(8,128)(2,1)S(1)} %fusion.4), channel_id=1, source_target_pairs={{0,128},{128,0},{1,129},{129,1},{2,130},{130,2},{3,131},{131,3},{4... | collective-permute-start | bytes 884744 | tf_op jit(solution)/shard_map/ppermute | solution.py:106
  32.5 15.0 %all-to-all-start.1 = ((bf16[16,16,256]{2,1,0:T(8,128)(2,1)}), bf16[16,16,256]{2,1,0:T(8,128)(2,1)S(1)}, u32[]{:S(2)}, u32[]{:S(2)}) async-start(bf16[16,16,256]{2,1,0:T(8,128)(2,1)} %fusion.10), calls=%async_computation.1 | async-start | bytes 262144 | tf_op jit(solution)/shard_map/all_to_all | solution.py:94
  39.6 20.0 %collective-permute-start.1 = (bf16[2,2,16,288]{3,2,1,0:T(8,128)(2,1)S(1)}, bf16[2,2,16,288]{3,2,1,0:T(8,128)(2,1)S(1)}, u32[]{:S(2)}, u32[]{:S(2)}) collective-permute-start(bf16[2,2,16,288]{3,2,1,0:T(8,128)(2,1)S(1)} %maximum_select_fusion.2), channel_id=1, source_target_pairs={{0,256},{256,0},{1,257},{257,1},{2,258},{258,2},{3,259},{259,3},{4... | collective-permute-start | bytes 110600 | tf_op jit(solution)/shard_map/ppermute | solution.py:114
  48.5 24.8 %all-to-all-start.2 = ((bf16[64,2,96]{2,1,0:T(2,128)(2,1)}), bf16[64,2,96]{2,1,0:T(2,128)(2,1)S(1)}, u32[]{:S(2)}, u32[]{:S(2)}) async-start(bf16[64,2,96]{2,1,0:T(2,128)(2,1)} %bitcast.20), calls=%async_computation.2 | async-start | bytes 65536 | tf_op jit(solution)/shard_map/all_to_all | solution.py:94
  59.6 13.7 %copy-start.1 = (bf16[96,4608]{1,0:T(8,128)(2,1)S(1)}, bf16[96,4608]{1,0:T(8,128)(2,1)}, u32[]{:S(2)}) copy-start(bf16[96,4608]{1,0:T(8,128)(2,1)} %w_ref.1) | copy-start | bytes 2654212
  74.3 3.9 %collective-permute-start.2 = (bf16[2304,128]{1,0:T(8,128)(2,1)S(1)}, bf16[2304,128]{1,0:T(8,128)(2,1)S(1)}, u32[]{:S(2)}, u32[]{:S(2)}) collective-permute-start(bf16[2304,128]{1,0:T(8,128)(2,1)S(1)} %get-tuple-element.12), channel_id=1, source_target_pairs={{0,16},{16,0},{1,17},{17,1},{2,18},{18,2},{3,19},{19,3},{4,20},{20... | collective-permute-start | bytes 1769480 | tf_op jit(solution)/shard_map/ppermute | solution.py:165
  78.4 31.5 %copy-start.5 = (bf16[2,64,36]{1,0,2:T(2,128)(2,1)S(1)}, bf16[2,64,36]{1,0,2:T(2,128)(2,1)}, u32[]{:S(2)}) copy-start(bf16[2,64,36]{1,0,2:T(2,128)(2,1)} %param.9) | copy-start | bytes 27652

commit v12 on v10

--- a/solution.py
+++ b/solution.py
@@ -141,14 +141,13 @@
     share = jnp.exp(peaks - jnp.max(peaks, 0))
     share = share / jnp.sum(share * totals, 0)
     attn = jnp.sum(message[:, :12].astype(F32) * share[..., None], 0).astype(BF16)
-    attn = attn.reshape(2, 16, 96).transpose(1, 0, 2)
-    attn = jnp.broadcast_to(attn[:, None], (16, 4, 2, 96)).reshape(128, 1, 96)
+    attn = jnp.broadcast_to(attn.reshape(1, 32, 96), (4, 32, 96)).reshape(128, 1, 96)
 
     spread = jnp.where(gx < 2, jnp.concatenate([near, far]), jnp.concatenate([far, near]))
     feed = turned_product(spread.reshape(4, 32, 288), down_weight)
 
-    mine = exchange(attn, ("gz", "gx", "core"))
-    mine = mine.reshape(64, 2, 96).transpose(1, 0, 2).reshape(128, 96)
+    mine = exchange(attn, ("gx", "core", "gz"))
+    mine = mine.reshape(4, 2, 16, 96).transpose(1, 2, 0, 3).reshape(128, 96)
     ours, theirs = split_product(core, mine, out_weight, feed)
 
     theirs = lax.ppermute(theirs, "core", [(0, 1), (1, 0)])

time: 109 us -> 109 us (level)
  no operation moved by 1% of the time
where the time goes in v12:
time: 109 us
  starting transfers between devices  44 us (40%)
  blocking collectives  31.4 us (29%)
  waiting for transfers between devices  21.9 us (20%)
  Pallas kernels  3.9 us (4%)
  other arithmetic  3.48 us (3%)
  local copies, waits for them, and re-layouts  2.89 us (3%)
    all_to_all x2, blocking collectives, exchange(): return lax.all_to_all(x, axes, split_axis=0, concat_axis=0, tiled=True)  31.4 us
    all_to_all x3, starting transfers between devices, exchange(): return lax.all_to_all(x, axes, split_axis=0, concat_axis=0, tiled=True)  30.9 us
    all_to_all x3, waiting for transfers between devices, exchange(): return lax.all_to_all(x, axes, split_axis=0, concat_axis=0, tiled=True)  20.2 us
    ppermute x1, starting transfers between devices, per_device(): far = lax.ppermute(near, 'gx', [(i, i ^ 2) for i in range(4)])  5.34 us
    ppermute x1, starting transfers between devices, per_device(): near = lax.ppermute(own, 'gx', [(i, i ^ 1) for i in range(4)])  3.62 us
    pallas_call x1, Pallas kernels, turned_product(): pl.pallas_call(kernel, in_specs=[in_vmem, pl.BlockSpec(memory_space=pltpu...  2.92 us
  transfers between devices with their start and end apart: 7, of which 4 were waited for; matrix products, arithmetic and copies ran while one was open for 2% of the time, Pallas kernels for 3%

profile of v12, /device:TPU:32, one launch (start us, length us, event | category | flops | bytes accessed | tf_op | source)
XLA Modules:
  0.0 108.9 jit_solution(17452266984725728434)
XLA Ops:
  0.0 0.9 copy-done
  0.9 0.7 reshape.199
  1.6 15.2 %all-to-all-start = ((bf16[16,4,768]{2,1,0:T(4,128)(2,1)}), bf16[16,4,768]{2,1,0:T(4,128)(2,1)S(1)}, u32[]{:S(2)}, u32[]{:S(2)}) async-start(bf16[16,4,768]{2,1,0:T(4,128)(2,1)} %reshape.199), calls=%async_computation | async-start | bytes 196608 | tf_op jit(solution)/shard_map/all_to_all | solution.py:93
  16.8 1.1 pad_maximum_fusion
  17.9 3.6 %collective-permute-start.1 = (bf16[2,16,288]{2,1,0:T(8,128)(2,1)S(1)}, bf16[2,16,288]{2,1,0:T(8,128)(2,1)S(1)}, u32[]{:S(2)}, u32[]{:S(2)}) collective-permute-start(bf16[2,16,288]{2,1,0:T(8,128)(2,1)S(1)} %copy-done.4), channel_id=1, source_target_pairs={{0,128},{128,0},{256,384},{384,256},{1,129},{129,1},{257,385},{385... | collective-permute-start | bytes 55304 | tf_op jit(solution)/shard_map/ppermute | solution.py:104
  21.5 1.9 %collective-permute-start = (bf16[4,128,512]{2,1,0:T(8,128)(2,1)S(1)}, bf16[4,128,512]{2,1,0:T(8,128)(2,1)S(1)}, u32[]{:S(2)}, u32[]{:S(2)}) collective-permute-start(bf16[4,128,512]{2,1,0:T(8,128)(2,1)S(1)} %pad_maximum_fusion), channel_id=1, source_target_pairs={{0,16},{16,0},{1,17},{17,1},{2,18},{18,2},{3,19},{19,3},{4,20},{20... | collective-permute-start | bytes 1572872 | tf_op jit(solution)/shard_map/ppermute | solution.py:103
  23.7 6.1 %all-to-all-done = bf16[16,4,768]{2,1,0:T(4,128)(2,1)S(1)} async-done(((bf16[16,4,768]{2,1,0:T(4,128)(2,1)}), bf16[16,4,768]{2,1,0:T(4,128)(2,1)S(1)}, u32[]{:S(2)}, u32[]{:S(2)}) %all-to-all-start) | async-done | bytes 98336 | tf_op jit(solution)/shard_map/all_to_all | solution.py:93
  29.9 0.1 copy.82
  30.0 0.2 fusion.31
  30.3 0.4 fusion.30
  30.7 0.2 convert_reduce_fusion.1
  31.1 0.2 fusion.16
  31.4 0.3 fusion.1
  31.7 0.7 fusion.7
  32.3 7.0 %all-to-all-start.1 = ((bf16[16,16,256]{2,1,0:T(8,128)(2,1)}), bf16[16,16,256]{2,1,0:T(8,128)(2,1)S(1)}, u32[]{:S(2)}, u32[]{:S(2)}) async-start(bf16[16,16,256]{2,1,0:T(8,128)(2,1)} %fusion.7), calls=%async_computation.1 | async-start | bytes 262144 | tf_op jit(solution)/shard_map/all_to_all | solution.py:93
  39.4 5.3 %collective-permute-start.2 = (bf16[2,2,16,288]{3,2,1,0:T(8,128)(2,1)S(1)}, bf16[2,2,16,288]{3,2,1,0:T(8,128)(2,1)S(1)}, u32[]{:S(2)}, u32[]{:S(2)}) collective-permute-start(bf16[2,2,16,288]{3,2,1,0:T(8,128)(2,1)S(1)} %maximum_select_fusion.2), channel_id=1, source_target_pairs={{0,256},{128,384},{256,0},{384,128},{1,257},{129,385},{257,1},{385... | collective-permute-start | bytes 110600 | tf_op jit(solution)/shard_map/ppermute | solution.py:109
  44.8 2.6 %all-to-all-done.1 = bf16[16,16,256]{2,1,0:T(8,128)(2,1)S(1)} async-done(((bf16[16,16,256]{2,1,0:T(8,128)(2,1)}), bf16[16,16,256]{2,1,0:T(8,128)(2,1)S(1)}, u32[]{:S(2)}, u32[]{:S(2)}) %all-to-all-start.1) | async-done | bytes 131104 | tf_op jit(solution)/shard_map/all_to_all | solution.py:93
  47.5 0.1 multiply_reduce_fusion
  47.6 0.1 convert_element_type.141
  47.7 0.7 copy.89
  48.4 8.7 %all-to-all-start.2 = ((bf16[128,1,96]{2,1,0:T(2,128)(2,1)}), bf16[128,1,96]{2,1,0:T(2,128)(2,1)S(1)}, u32[]{:S(2)}, u32[]{:S(2)}) async-start(bf16[128,1,96]{2,1,0:T(2,128)(2,1)} %copy.89), calls=%async_computation.2 | async-start | bytes 131072 | tf_op jit(solution)/shard_map/all_to_all | solution.py:93
  57.1 2.9 %shard_map.91.more_ref = f32[4608,128]{1,0:T(8,128)S(1)} custom-call(bf16[4,32,288]{2,1,0:T(8,128)(2,1)S(1)} %maximum_select_fusion.h_ref, bf16[288,4608]{1,0:T(8,128)(2,1)} %w_hbm.1), custom_call_target="tpu_custom_call" | custom-call | flops 339738624 | bytes 5013504 | tf_op jit(solution)/shard_map/pallas_call | solution.py:39
  60.1 11.5 %all-to-all-done.2 = bf16[128,1,96]{2,1,0:T(2,128)(2,1)S(1)} async-done(((bf16[128,1,96]{2,1,0:T(2,128)(2,1)}), bf16[128,1,96]{2,1,0:T(2,128)(2,1)S(1)}, u32[]{:S(2)}, u32[]{:S(2)}) %all-to-all-start.2) | async-done | bytes 24608 | tf_op jit(solution)/shard_map/all_to_all | solution.py:93
  71.6 1.0 shard_map.92
  72.5 2.2 %collective-permute-start.3 = (bf16[2304,128]{1,0:T(8,128)(2,1)S(1)}, bf16[2304,128]{1,0:T(8,128)(2,1)S(1)}, u32[]{:S(2)}, u32[]{:S(2)}) collective-permute-start(bf16[2304,128]{1,0:T(8,128)(2,1)S(1)} %get-tuple-element.16), channel_id=1, source_target_pairs={{0,16},{16,0},{1,17},{17,1},{2,18},{18,2},{3,19},{19,3},{4,20},{20... | collective-permute-start | bytes 1769480 | tf_op jit(solution)/shard_map/ppermute | solution.py:153
  74.7 1.7 %collective-permute-done.3 = bf16[2304,128]{1,0:T(8,128)(2,1)S(1)} collective-permute-done((bf16[2304,128]{1,0:T(8,128)(2,1)S(1)}, bf16[2304,128]{1,0:T(8,128)(2,1)S(1)}, u32[]{:S(2)}, u32[]{:S(2)}) %collective-permute-start.3) | collective-permute-done | bytes 589856 | tf_op jit(solution)/shard_map/ppermute | solution.py:153
  76.4 0.2 add_convert_fusion
  76.6 13.3 %all_to_all.25 = bf16[4,576,128]{2,1,0:T(8,128)(2,1)S(1)} all-to-all(bf16[4,576,128]{2,1,0:T(8,128)(2,1)S(1)} %bitcast.42), channel_id=1, replica_groups=mesh['gx'=4,'gyx'=4,'core'=2,'gz'=16] {'gyx'}, dimensions={0} | all-to-all | bytes 1179648 | tf_op jit(solution)/shard_map/all_to_all | solution.py:93
  89.9 0.1 reduce_sum.61
  90.0 18.1 %all_to_all.26 = bf16[16,9,4,128]{3,2,1,0:T(4,128)(2,1)S(1)} all-to-all(bf16[16,9,4,128]{3,2,1,0:T(4,128)(2,1)S(1)} %bitcast.43), channel_id=1, replica_groups=mesh['gx'=4,'gyx'=4,'core'=2,'gz'=16] {'gz'}, dimensions={0} | all-to-all | bytes 294912 | tf_op jit(solution)/shard_map/all_to_all | solution.py:93
  108.2 0.1 reshape.209
  108.3 0.6 fusion.10
  (49 shorter events, 0.9 us)
Async XLA Ops:
  0.0 0.9 copy-start
  0.0 17.9 %copy-start.4 = (bf16[2,16,288]{2,1,0:T(8,128)(2,1)S(1)}, bf16[2,16,288]{2,1,0:T(8,128)(2,1)}, u32[]{:S(2)}) copy-start(bf16[2,16,288]{2,1,0:T(8,128)(2,1)} %param.16) | copy-start | bytes 55300
  0.0 23.5 %copy-start.7 = (s32[4]{0:T(128)S(1)}, s32[4]{0:T(128)}, u32[]{:S(2)}) copy-start(s32[4]{0:T(128)} %param.14) | copy-start | bytes 52
  0.0 23.6 %copy-start.6 = (bf16[2,4,512]{2,1,0:T(4,128)(2,1)S(1)}, bf16[2,4,512]{2,1,0:T(4,128)(2,1)}, u32[]{:S(2)}) copy-start(bf16[2,4,512]{2,1,0:T(4,128)(2,1)} %param.11) | copy-start | bytes 24580
  1.6 28.2 %all-to-all-start = ((bf16[16,4,768]{2,1,0:T(4,128)(2,1)}), bf16[16,4,768]{2,1,0:T(4,128)(2,1)S(1)}, u32[]{:S(2)}, u32[]{:S(2)}) async-start(bf16[16,4,768]{2,1,0:T(4,128)(2,1)} %reshape.199), calls=%async_computation | async-start | bytes 196608 | tf_op jit(solution)/shard_map/all_to_all | solution.py:93
  17.9 12.3 %copy-start.2 = (bf16[4,128,256]{2,1,0:T(8,128)(2,1)S(1)}, bf16[4,128,256]{2,1,0:T(8,128)(2,1)}, u32[]{:S(2)}) copy-start(bf16[4,128,256]{2,1,0:T(8,128)(2,1)} %param.12) | copy-start | bytes 786436
  17.9 12.4 %collective-permute-start.1 = (bf16[2,16,288]{2,1,0:T(8,128)(2,1)S(1)}, bf16[2,16,288]{2,1,0:T(8,128)(2,1)S(1)}, u32[]{:S(2)}, u32[]{:S(2)}) collective-permute-start(bf16[2,16,288]{2,1,0:T(8,128)(2,1)S(1)} %copy-done.4), channel_id=1, source_target_pairs={{0,128},{128,0},{256,384},{384,256},{1,129},{129,1},{257,385},{385... | collective-permute-start | bytes 55304 | tf_op jit(solution)/shard_map/ppermute | solution.py:104
  21.5 8.6 %collective-permute-start = (bf16[4,128,512]{2,1,0:T(8,128)(2,1)S(1)}, bf16[4,128,512]{2,1,0:T(8,128)(2,1)S(1)}, u32[]{:S(2)}, u32[]{:S(2)}) collective-permute-start(bf16[4,128,512]{2,1,0:T(8,128)(2,1)S(1)} %pad_maximum_fusion), channel_id=1, source_target_pairs={{0,16},{16,0},{1,17},{17,1},{2,18},{18,2},{3,19},{19,3},{4,20},{20... | collective-permute-start | bytes 1572872 | tf_op jit(solution)/shard_map/ppermute | solution.py:103
  30.2 1.2 %copy-start.3 = (bf16[4,128,256]{2,1,0:T(8,128)(2,1)S(1)}, bf16[4,128,256]{2,1,0:T(8,128)(2,1)}, u32[]{:S(2)}) copy-start(bf16[4,128,256]{2,1,0:T(8,128)(2,1)} %param.13) | copy-start | bytes 786436
  32.3 15.0 %all-to-all-start.1 = ((bf16[16,16,256]{2,1,0:T(8,128)(2,1)}), bf16[16,16,256]{2,1,0:T(8,128)(2,1)S(1)}, u32[]{:S(2)}, u32[]{:S(2)}) async-start(bf16[16,16,256]{2,1,0:T(8,128)(2,1)} %fusion.7), calls=%async_computation.1 | async-start | bytes 262144 | tf_op jit(solution)/shard_map/all_to_all | solution.py:93
  39.4 17.7 %collective-permute-start.2 = (bf16[2,2,16,288]{3,2,1,0:T(8,128)(2,1)S(1)}, bf16[2,2,16,288]{3,2,1,0:T(8,128)(2,1)S(1)}, u32[]{:S(2)}, u32[]{:S(2)}) collective-permute-start(bf16[2,2,16,288]{3,2,1,0:T(8,128)(2,1)S(1)} %maximum_select_fusion.2), channel_id=1, source_target_pairs={{0,256},{128,384},{256,0},{384,128},{1,257},{129,385},{257,1},{385... | collective-permute-start | bytes 110600 | tf_op jit(solution)/shard_map/ppermute | solution.py:109
  48.4 23.2 %all-to-all-start.2 = ((bf16[128,1,96]{2,1,0:T(2,128)(2,1)}), bf16[128,1,96]{2,1,0:T(2,128)(2,1)S(1)}, u32[]{:S(2)}, u32[]{:S(2)}) async-start(bf16[128,1,96]{2,1,0:T(2,128)(2,1)} %copy.89), calls=%async_computation.2 | async-start | bytes 131072 | tf_op jit(solution)/shard_map/all_to_all | solution.py:93
  57.1 14.4 %copy-start.1 = (bf16[96,4608]{1,0:T(8,128)(2,1)S(1)}, bf16[96,4608]{1,0:T(8,128)(2,1)}, u32[]{:S(2)}) copy-start(bf16[96,4608]{1,0:T(8,128)(2,1)} %w_ref.1) | copy-start | bytes 2654212
  72.5 3.9 %collective-permute-start.3 = (bf16[2304,128]{1,0:T(8,128)(2,1)S(1)}, bf16[2304,128]{1,0:T(8,128)(2,1)S(1)}, u32[]{:S(2)}, u32[]{:S(2)}) collective-permute-start(bf16[2304,128]{1,0:T(8,128)(2,1)S(1)} %get-tuple-element.16), channel_id=1, source_target_pairs={{0,16},{16,0},{1,17},{17,1},{2,18},{18,2},{3,19},{19,3},{4,20},{20... | collective-permute-start | bytes 1769480 | tf_op jit(solution)/shard_map/ppermute | solution.py:153
  76.6 31.7 %copy-start.5 = (bf16[2,64,36]{1,0,2:T(2,128)(2,1)S(1)}, bf16[2,64,36]{1,0,2:T(2,128)(2,1)}, u32[]{:S(2)}) copy-start(bf16[2,64,36]{1,0,2:T(2,128)(2,1)} %param.9) | copy-start | bytes 27652

commit v13 on v12

--- a/solution.py
+++ b/solution.py
@@ -102,8 +102,9 @@
     pair, own = lax.optimization_barrier((pair, hidden))
     pair = lax.ppermute(pair, "core", [(0, 1), (1, 0)])
     near = lax.ppermute(own, "gx", [(i, i ^ 1) for i in range(4)])
-    keys = jnp.concatenate([key_cache, pair[..., :HD]], 1)
-    values = jnp.concatenate([value_cache, pair[..., HD:]], 1)
+    fresh = jnp.pad(new_kv.transpose(1, 0, 2), ((0, 0), (0, 14), (0, 0)))
+    keys = jnp.concatenate([key_cache, pair[..., :HD], fresh[..., :HD]], 1)
+    values = jnp.concatenate([value_cache, pair[..., HD:], fresh[..., HD:]], 1)
     keys, near = lax.optimization_barrier((keys, near))
     near = jnp.where(gx % 2 == 0, jnp.stack([hidden, near]), jnp.stack([near, hidden]))
     far = lax.ppermute(near, "gx", [(i, i ^ 2) for i in range(4)])
@@ -111,23 +112,17 @@
     q = exchange(q.reshape(16, 4, 768), "gz")
     qf = q.reshape(16, 4, 3, HD).transpose(1, 0, 2, 3).reshape(4, HEADS, HD)
 
-    at = jnp.arange(256, dtype=jnp.int32)
+    at = jnp.arange(272, dtype=jnp.int32)
     owner = gx * 8 + gyx * 2 + jnp.where(at < 128, core, 1 - core)
     positions = owner * 128 + at % 128
-    present = (positions[None] < lengths[:, None])[:, None]
-    scale = HD**-0.5
-    s = jnp.einsum("bqd,bpd->bqp", qf, keys, preferred_element_type=F32) * scale
+    allowed = (at - 256 <= core) & (gx + gyx == 0)
+    present = jnp.where(at < 256, positions[None] < lengths[:, None], allowed[None])[:, None]
+    s = jnp.einsum("bqd,bpd->bqp", qf, keys, preferred_element_type=F32) * HD**-0.5
     s = jnp.where(present, s, NEG)
-    allowed = ((jnp.arange(2) <= core) & (gx + gyx == 0))[None, None]
-    sn = jnp.einsum("bqd,ubd->bqu", qf, new_kv[..., :HD], preferred_element_type=F32) * scale
-    sn = jnp.where(allowed, sn, NEG)
-    peak = jnp.maximum(jnp.max(s, -1), jnp.max(sn, -1)).astype(BF16)
-    pf = peak.astype(F32)[..., None]
-    w = jnp.where(present, jnp.exp(s - pf), 0.0).astype(BF16)
-    wn = jnp.where(allowed, jnp.exp(sn - pf), 0.0).astype(BF16)
-    total = jnp.sum(w.astype(F32), -1) + jnp.sum(wn.astype(F32), -1)
+    peak = jnp.max(s, -1).astype(BF16)
+    w = jnp.where(present, jnp.exp(s - peak.astype(F32)[..., None]), 0.0).astype(BF16)
+    total = jnp.sum(w.astype(F32), -1)
     acc = jnp.einsum("bqp,bpd->bqd", w, values, preferred_element_type=F32)
-    acc = acc + jnp.einsum("bqu,ubd->bqd", wn, new_kv[..., HD:], preferred_element_type=F32)
     total_hi = total.astype(BF16)
     total_lo = (total - total_hi.astype(F32)).astype(BF16)
     stats = jnp.stack([peak, total_hi, total_lo, jnp.zeros_like(peak)], 1)

time: 109 us -> 109 us (level)
  no operation moved by 1% of the time
where the time goes in v13:
time: 109 us
  starting transfers between devices  44.1 us (40%)
  blocking collectives  31.4 us (29%)
  waiting for transfers between devices  21.9 us (20%)
  Pallas kernels  3.88 us (4%)
  other arithmetic  3.43 us (3%)
  local copies, waits for them, and re-layouts  2.97 us (3%)
    all_to_all x2, blocking collectives, exchange(): return lax.all_to_all(x, axes, split_axis=0, concat_axis=0, tiled=True)  31.4 us
    all_to_all x3, starting transfers between devices, exchange(): return lax.all_to_all(x, axes, split_axis=0, concat_axis=0, tiled=True)  31.1 us
    all_to_all x3, waiting for transfers between devices, exchange(): return lax.all_to_all(x, axes, split_axis=0, concat_axis=0, tiled=True)  20.2 us
    ppermute x1, starting transfers between devices, per_device(): far = lax.ppermute(near, 'gx', [(i, i ^ 2) for i in range(4)])  5.34 us
    ppermute x1, starting transfers between devices, per_device(): near = lax.ppermute(own, 'gx', [(i, i ^ 1) for i in range(4)])  3.62 us
    pallas_call x1, Pallas kernels, turned_product(): pl.pallas_call(kernel, in_specs=[in_vmem, pl.BlockSpec(memory_space=pltpu...  2.92 us
  transfers between devices with their start and end apart: 7, of which 4 were waited for; matrix products, arithmetic and copies ran while one was open for 2% of the time, Pallas kernels for 3%

profile of v13, /device:TPU:32, one launch (start us, length us, event | category | flops | bytes accessed | tf_op | source)
XLA Modules:
  0.0 108.7 jit_solution(13036405137645880036)
XLA Ops:
  0.0 0.9 copy-done
  0.9 0.7 reshape.198
  1.6 15.2 %all-to-all-start = ((bf16[16,4,768]{2,1,0:T(4,128)(2,1)}), bf16[16,4,768]{2,1,0:T(4,128)(2,1)S(1)}, u32[]{:S(2)}, u32[]{:S(2)}) async-start(bf16[16,4,768]{2,1,0:T(4,128)(2,1)} %reshape.198), calls=%async_computation | async-start | bytes 196608 | tf_op jit(solution)/shard_map/all_to_all | solution.py:93
  16.8 1.1 pad_maximum_fusion.1
  17.9 3.6 %collective-permute-start.1 = (bf16[2,16,288]{2,1,0:T(8,128)(2,1)S(1)}, bf16[2,16,288]{2,1,0:T(8,128)(2,1)S(1)}, u32[]{:S(2)}, u32[]{:S(2)}) collective-permute-start(bf16[2,16,288]{2,1,0:T(8,128)(2,1)S(1)} %copy-done.4), channel_id=1, source_target_pairs={{0,128},{128,0},{256,384},{384,256},{1,129},{129,1},{257,385},{385... | collective-permute-start | bytes 55304 | tf_op jit(solution)/shard_map/ppermute | solution.py:104
  21.5 1.9 %collective-permute-start = (bf16[4,128,512]{2,1,0:T(8,128)(2,1)S(1)}, bf16[4,128,512]{2,1,0:T(8,128)(2,1)S(1)}, u32[]{:S(2)}, u32[]{:S(2)}) collective-permute-start(bf16[4,128,512]{2,1,0:T(8,128)(2,1)S(1)} %pad_maximum_fusion.1), channel_id=1, source_target_pairs={{0,16},{16,0},{1,17},{17,1},{2,18},{18,2},{3,19},{19,3},{4,20},{20... | collective-permute-start | bytes 1572872 | tf_op jit(solution)/shard_map/ppermute | solution.py:103
  23.7 6.1 %all-to-all-done = bf16[16,4,768]{2,1,0:T(4,128)(2,1)S(1)} async-done(((bf16[16,4,768]{2,1,0:T(4,128)(2,1)}), bf16[16,4,768]{2,1,0:T(4,128)(2,1)S(1)}, u32[]{:S(2)}, u32[]{:S(2)}) %all-to-all-start) | async-done | bytes 98336 | tf_op jit(solution)/shard_map/all_to_all | solution.py:93
  29.9 0.1 copy.67
  30.1 0.4 fusion.26
  30.5 0.2 convert_reduce_fusion.1
  30.7 0.1 maximum_maximum_fusion
  30.8 0.1 fusion.25
  31.0 0.3 convolution_convert_fusion
  31.3 0.7 fusion.7
  32.0 7.0 %all-to-all-start.1 = ((bf16[16,16,256]{2,1,0:T(8,128)(2,1)}), bf16[16,16,256]{2,1,0:T(8,128)(2,1)S(1)}, u32[]{:S(2)}, u32[]{:S(2)}) async-start(bf16[16,16,256]{2,1,0:T(8,128)(2,1)} %fusion.7), calls=%async_computation.1 | async-start | bytes 262144 | tf_op jit(solution)/shard_map/all_to_all | solution.py:93
  39.1 5.3 %collective-permute-start.2 = (bf16[2,2,16,288]{3,2,1,0:T(8,128)(2,1)S(1)}, bf16[2,2,16,288]{3,2,1,0:T(8,128)(2,1)S(1)}, u32[]{:S(2)}, u32[]{:S(2)}) collective-permute-start(bf16[2,2,16,288]{3,2,1,0:T(8,128)(2,1)S(1)} %maximum_select_fusion.2), channel_id=1, source_target_pairs={{0,256},{128,384},{256,0},{384,128},{1,257},{129,385},{257,1},{385... | collective-permute-start | bytes 110600 | tf_op jit(solution)/shard_map/ppermute | solution.py:110
  44.5 2.6 %all-to-all-done.1 = bf16[16,16,256]{2,1,0:T(8,128)(2,1)S(1)} async-done(((bf16[16,16,256]{2,1,0:T(8,128)(2,1)}), bf16[16,16,256]{2,1,0:T(8,128)(2,1)S(1)}, u32[]{:S(2)}, u32[]{:S(2)}) %all-to-all-start.1) | async-done | bytes 131104 | tf_op jit(solution)/shard_map/all_to_all | solution.py:93
  47.1 0.1 multiply_reduce_fusion
  47.3 0.1 convert_element_type.135
  47.4 0.7 copy.72
  48.0 8.8 %all-to-all-start.2 = ((bf16[128,1,96]{2,1,0:T(2,128)(2,1)}), bf16[128,1,96]{2,1,0:T(2,128)(2,1)S(1)}, u32[]{:S(2)}, u32[]{:S(2)}) async-start(bf16[128,1,96]{2,1,0:T(2,128)(2,1)} %copy.72), calls=%async_computation.2 | async-start | bytes 131072 | tf_op jit(solution)/shard_map/all_to_all | solution.py:93
  56.9 2.9 %shard_map.91.more_ref = f32[4608,128]{1,0:T(8,128)S(1)} custom-call(bf16[4,32,288]{2,1,0:T(8,128)(2,1)S(1)} %maximum_select_fusion.h_ref, bf16[288,4608]{1,0:T(8,128)(2,1)} %w_hbm.1), custom_call_target="tpu_custom_call" | custom-call | flops 339738624 | bytes 5013504 | tf_op jit(solution)/shard_map/pallas_call | solution.py:39
  59.9 11.5 %all-to-all-done.2 = bf16[128,1,96]{2,1,0:T(2,128)(2,1)S(1)} async-done(((bf16[128,1,96]{2,1,0:T(2,128)(2,1)}), bf16[128,1,96]{2,1,0:T(2,128)(2,1)S(1)}, u32[]{:S(2)}, u32[]{:S(2)}) %all-to-all-start.2) | async-done | bytes 24608 | tf_op jit(solution)/shard_map/all_to_all | solution.py:93
  71.4 1.0 shard_map.92
  72.4 2.1 %collective-permute-start.3 = (bf16[2304,128]{1,0:T(8,128)(2,1)S(1)}, bf16[2304,128]{1,0:T(8,128)(2,1)S(1)}, u32[]{:S(2)}, u32[]{:S(2)}) collective-permute-start(bf16[2304,128]{1,0:T(8,128)(2,1)S(1)} %get-tuple-element.16), channel_id=1, source_target_pairs={{0,16},{16,0},{1,17},{17,1},{2,18},{18,2},{3,19},{19,3},{4,20},{20... | collective-permute-start | bytes 1769480 | tf_op jit(solution)/shard_map/ppermute | solution.py:148
  74.5 1.8 %collective-permute-done.3 = bf16[2304,128]{1,0:T(8,128)(2,1)S(1)} collective-permute-done((bf16[2304,128]{1,0:T(8,128)(2,1)S(1)}, bf16[2304,128]{1,0:T(8,128)(2,1)S(1)}, u32[]{:S(2)}, u32[]{:S(2)}) %collective-permute-start.3) | collective-permute-done | bytes 589856 | tf_op jit(solution)/shard_map/ppermute | solution.py:148
  76.3 0.2 add_convert_fusion
  76.5 13.2 %all_to_all.25 = bf16[4,576,128]{2,1,0:T(8,128)(2,1)S(1)} all-to-all(bf16[4,576,128]{2,1,0:T(8,128)(2,1)S(1)} %bitcast.45), channel_id=1, replica_groups=mesh['gx'=4,'gyx'=4,'core'=2,'gz'=16] {'gyx'}, dimensions={0} | all-to-all | bytes 1179648 | tf_op jit(solution)/shard_map/all_to_all | solution.py:93
  89.7 0.1 reduce_sum.54
  89.8 18.1 %all_to_all.26 = bf16[16,9,4,128]{3,2,1,0:T(4,128)(2,1)S(1)} all-to-all(bf16[16,9,4,128]{3,2,1,0:T(4,128)(2,1)S(1)} %bitcast.46), channel_id=1, replica_groups=mesh['gx'=4,'gyx'=4,'core'=2,'gz'=16] {'gz'}, dimensions={0} | all-to-all | bytes 294912 | tf_op jit(solution)/shard_map/all_to_all | solution.py:93
  108.0 0.1 reshape.208
  108.1 0.6 fusion.9
  (47 shorter events, 0.8 us)
Async XLA Ops:
  0.0 0.9 copy-start
  0.0 17.9 %copy-start.4 = (bf16[2,16,288]{2,1,0:T(8,128)(2,1)S(1)}, bf16[2,16,288]{2,1,0:T(8,128)(2,1)}, u32[]{:S(2)}) copy-start(bf16[2,16,288]{2,1,0:T(8,128)(2,1)} %param.16) | copy-start | bytes 55300
  0.0 23.5 %copy-start.6 = (bf16[2,4,512]{2,1,0:T(4,128)(2,1)S(1)}, bf16[2,4,512]{2,1,0:T(4,128)(2,1)}, u32[]{:S(2)}) copy-start(bf16[2,4,512]{2,1,0:T(4,128)(2,1)} %param.11) | copy-start | bytes 24580
  0.0 23.6 %copy-start.7 = (s32[4]{0:T(128)S(1)}, s32[4]{0:T(128)}, u32[]{:S(2)}) copy-start(s32[4]{0:T(128)} %param.14) | copy-start | bytes 52
  1.6 28.2 %all-to-all-start = ((bf16[16,4,768]{2,1,0:T(4,128)(2,1)}), bf16[16,4,768]{2,1,0:T(4,128)(2,1)S(1)}, u32[]{:S(2)}, u32[]{:S(2)}) async-start(bf16[16,4,768]{2,1,0:T(4,128)(2,1)} %reshape.198), calls=%async_computation | async-start | bytes 196608 | tf_op jit(solution)/shard_map/all_to_all | solution.py:93
  17.9 12.1 %copy-start.2 = (bf16[4,128,256]{2,1,0:T(8,128)(2,1)S(1)}, bf16[4,128,256]{2,1,0:T(8,128)(2,1)}, u32[]{:S(2)}) copy-start(bf16[4,128,256]{2,1,0:T(8,128)(2,1)} %param.12) | copy-start | bytes 786436
  17.9 12.2 %collective-permute-start.1 = (bf16[2,16,288]{2,1,0:T(8,128)(2,1)S(1)}, bf16[2,16,288]{2,1,0:T(8,128)(2,1)S(1)}, u32[]{:S(2)}, u32[]{:S(2)}) collective-permute-start(bf16[2,16,288]{2,1,0:T(8,128)(2,1)S(1)} %copy-done.4), channel_id=1, source_target_pairs={{0,128},{128,0},{256,384},{384,256},{1,129},{129,1},{257,385},{385... | collective-permute-start | bytes 55304 | tf_op jit(solution)/shard_map/ppermute | solution.py:104
  21.5 8.5 %collective-permute-start = (bf16[4,128,512]{2,1,0:T(8,128)(2,1)S(1)}, bf16[4,128,512]{2,1,0:T(8,128)(2,1)S(1)}, u32[]{:S(2)}, u32[]{:S(2)}) collective-permute-start(bf16[4,128,512]{2,1,0:T(8,128)(2,1)S(1)} %pad_maximum_fusion.1), channel_id=1, source_target_pairs={{0,16},{16,0},{1,17},{17,1},{2,18},{18,2},{3,19},{19,3},{4,20},{20... | collective-permute-start | bytes 1572872 | tf_op jit(solution)/shard_map/ppermute | solution.py:103
  30.0 1.0 copy-start.3
  32.0 15.0 %all-to-all-start.1 = ((bf16[16,16,256]{2,1,0:T(8,128)(2,1)}), bf16[16,16,256]{2,1,0:T(8,128)(2,1)S(1)}, u32[]{:S(2)}, u32[]{:S(2)}) async-start(bf16[16,16,256]{2,1,0:T(8,128)(2,1)} %fusion.7), calls=%async_computation.1 | async-start | bytes 262144 | tf_op jit(solution)/shard_map/all_to_all | solution.py:93
  39.1 17.8 %collective-permute-start.2 = (bf16[2,2,16,288]{3,2,1,0:T(8,128)(2,1)S(1)}, bf16[2,2,16,288]{3,2,1,0:T(8,128)(2,1)S(1)}, u32[]{:S(2)}, u32[]{:S(2)}) collective-permute-start(bf16[2,2,16,288]{3,2,1,0:T(8,128)(2,1)S(1)} %maximum_select_fusion.2), channel_id=1, source_target_pairs={{0,256},{128,384},{256,0},{384,128},{1,257},{129,385},{257,1},{385... | collective-permute-start | bytes 110600 | tf_op jit(solution)/shard_map/ppermute | solution.py:110
  48.0 23.4 %all-to-all-start.2 = ((bf16[128,1,96]{2,1,0:T(2,128)(2,1)}), bf16[128,1,96]{2,1,0:T(2,128)(2,1)S(1)}, u32[]{:S(2)}, u32[]{:S(2)}) async-start(bf16[128,1,96]{2,1,0:T(2,128)(2,1)} %copy.72), calls=%async_computation.2 | async-start | bytes 131072 | tf_op jit(solution)/shard_map/all_to_all | solution.py:93
  56.9 14.5 %copy-start.1 = (bf16[96,4608]{1,0:T(8,128)(2,1)S(1)}, bf16[96,4608]{1,0:T(8,128)(2,1)}, u32[]{:S(2)}) copy-start(bf16[96,4608]{1,0:T(8,128)(2,1)} %w_ref.1) | copy-start | bytes 2654212
  72.4 3.9 %collective-permute-start.3 = (bf16[2304,128]{1,0:T(8,128)(2,1)S(1)}, bf16[2304,128]{1,0:T(8,128)(2,1)S(1)}, u32[]{:S(2)}, u32[]{:S(2)}) collective-permute-start(bf16[2304,128]{1,0:T(8,128)(2,1)S(1)} %get-tuple-element.16), channel_id=1, source_target_pairs={{0,16},{16,0},{1,17},{17,1},{2,18},{18,2},{3,19},{19,3},{4,20},{20... | collective-permute-start | bytes 1769480 | tf_op jit(solution)/shard_map/ppermute | solution.py:148
  76.5 31.6 %copy-start.5 = (bf16[2,64,36]{1,0,2:T(2,128)(2,1)S(1)}, bf16[2,64,36]{1,0,2:T(2,128)(2,1)}, u32[]{:S(2)}) copy-start(bf16[2,64,36]{1,0,2:T(2,128)(2,1)} %param.9) | copy-start | bytes 27652

commit v14 on v12

--- a/solution.py
+++ b/solution.py
@@ -54,39 +54,33 @@
     )(gathered, w)
 
 
-def split_product(core, x, w, more):
+def half_product(which, x, w, more, dtype):
     rows, depth = x.shape
     columns = w.shape[1]
     half = TILE // 2
 
-    def kernel(core_ref, x_ref, w_ref, more_ref, ours_ref, theirs_ref, full):
-        mine = core_ref[0]
+    def kernel(which_ref, x_ref, w_ref, more_ref, o_ref, full):
+        at = pl.multiple_of(which_ref[0] * half, half)
         for i in range(columns // TILE):
-            place = pl.ds(i * TILE, TILE)
-            y = jnp.dot(x_ref[...], w_ref[:, place], preferred_element_type=F32)
-            full[...] = y.T + more_ref[place, :]
-            rows_i = pl.ds(i * half, half)
-            ours_ref[rows_i, :] = full[pl.ds(pl.multiple_of(mine * half, half), half), :]
-            theirs = full[pl.ds(pl.multiple_of((1 - mine) * half, half), half), :]
-            theirs_ref[rows_i, :] = theirs.astype(BF16)
+            y = jnp.dot(x_ref[...], w_ref[:, pl.ds(i * TILE, TILE)], preferred_element_type=F32)
+            full[...] = y.T
+            y = full[pl.ds(at, half), :] + more_ref[pl.ds(i * TILE + at, half), :]
+            o_ref[pl.ds(i * half, half), :] = y.astype(dtype)
 
     in_vmem = pl.BlockSpec(memory_space=pltpu.VMEM)
     return pl.pallas_call(
         kernel,
         in_specs=[pl.BlockSpec(memory_space=pltpu.SMEM), in_vmem, in_vmem, in_vmem],
-        out_specs=[in_vmem, in_vmem],
-        out_shape=[
-            jax.ShapeDtypeStruct((columns // 2, rows), F32),
-            jax.ShapeDtypeStruct((columns // 2, rows), BF16),
-        ],
+        out_specs=in_vmem,
+        out_shape=jax.ShapeDtypeStruct((columns // 2, rows), dtype),
         scratch_shapes=[pltpu.VMEM((TILE, rows), F32)],
         compiler_params=pltpu.CompilerParams(vmem_limit_bytes=16 * 2**20),
         cost_estimate=pl.CostEstimate(
             flops=2 * rows * depth * columns,
-            bytes_accessed=2 * depth * columns + 7 * rows * columns,
+            bytes_accessed=2 * depth * columns + 4 * rows * columns,
             transcendentals=0,
         ),
-    )(core.reshape(1), x, w, more)
+    )(which.reshape(1), x, w, more)
 
 
 def exchange(x, axes):
@@ -148,7 +142,8 @@
 
     mine = exchange(attn, ("gx", "core", "gz"))
     mine = mine.reshape(4, 2, 16, 96).transpose(1, 2, 0, 3).reshape(128, 96)
-    ours, theirs = split_product(core, mine, out_weight, feed)
+    theirs = half_product(1 - core, mine, out_weight, feed, BF16)
+    ours = half_product(core, mine, out_weight, feed, F32)
 
     theirs = lax.ppermute(theirs, "core", [(0, 1), (1, 0)])
     row = (ours + theirs.astype(F32)).astype(BF16).reshape(4, 576, 128)

time: 109 us -> 109 us (level)
  transfers between devices with their start and end apart: 7 -> 7, of which waited for: 4 -> 4; matrix products, arithmetic and copies ran while one was open for 2% -> 2% of each run, Pallas kernels for 3% -> 4%
where the time goes in v14:
time: 109 us
  starting transfers between devices  44 us (40%)
  blocking collectives  31.3 us (29%)
  waiting for transfers between devices  21.1 us (19%)
  Pallas kernels  4.78 us (4%)
  other arithmetic  3.43 us (3%)
  local copies, waits for them, and re-layouts  2.87 us (3%)
    all_to_all x2, blocking collectives, exchange(): return lax.all_to_all(x, axes, split_axis=0, concat_axis=0, tiled=True)  31.3 us
    all_to_all x3, starting transfers between devices, exchange(): return lax.all_to_all(x, axes, split_axis=0, concat_axis=0, tiled=True)  30.9 us
    all_to_all x3, waiting for transfers between devices, exchange(): return lax.all_to_all(x, axes, split_axis=0, concat_axis=0, tiled=True)  20.3 us
    ppermute x1, starting transfers between devices, per_device(): far = lax.ppermute(near, 'gx', [(i, i ^ 2) for i in range(4)])  5.34 us
    ppermute x1, starting transfers between devices, per_device(): near = lax.ppermute(own, 'gx', [(i, i ^ 1) for i in range(4)])  3.62 us
    pallas_call x1, Pallas kernels, turned_product(): pl.pallas_call(kernel, in_specs=[in_vmem, pl.BlockSpec(memory_space=pltpu...  2.93 us
  transfers between devices with their start and end apart: 7, of which 4 were waited for; matrix products, arithmetic and copies ran while one was open for 2% of the time, Pallas kernels for 4%

profile of v14, /device:TPU:32, one launch (start us, length us, event | category | flops | bytes accessed | tf_op | source)
XLA Modules:
  0.0 108.8 jit_solution(7347556886810858285)
XLA Ops:
  0.0 0.9 copy-done
  0.9 0.7 reshape.202
  1.6 15.2 %all-to-all-start = ((bf16[16,4,768]{2,1,0:T(4,128)(2,1)}), bf16[16,4,768]{2,1,0:T(4,128)(2,1)S(1)}, u32[]{:S(2)}, u32[]{:S(2)}) async-start(bf16[16,4,768]{2,1,0:T(4,128)(2,1)} %reshape.202), calls=%async_computation | async-start | bytes 196608 | tf_op jit(solution)/shard_map/all_to_all | solution.py:87
  16.8 1.1 pad_maximum_fusion
  17.9 3.6 %collective-permute-start.1 = (bf16[2,16,288]{2,1,0:T(8,128)(2,1)S(1)}, bf16[2,16,288]{2,1,0:T(8,128)(2,1)S(1)}, u32[]{:S(2)}, u32[]{:S(2)}) collective-permute-start(bf16[2,16,288]{2,1,0:T(8,128)(2,1)S(1)} %copy-done.4), channel_id=1, source_target_pairs={{0,128},{128,0},{256,384},{384,256},{1,129},{129,1},{257,385},{385... | collective-permute-start | bytes 55304 | tf_op jit(solution)/shard_map/ppermute | solution.py:98
  21.5 1.9 %collective-permute-start = (bf16[4,128,512]{2,1,0:T(8,128)(2,1)S(1)}, bf16[4,128,512]{2,1,0:T(8,128)(2,1)S(1)}, u32[]{:S(2)}, u32[]{:S(2)}) collective-permute-start(bf16[4,128,512]{2,1,0:T(8,128)(2,1)S(1)} %pad_maximum_fusion), channel_id=1, source_target_pairs={{0,16},{16,0},{1,17},{17,1},{2,18},{18,2},{3,19},{19,3},{4,20},{20... | collective-permute-start | bytes 1572872 | tf_op jit(solution)/shard_map/ppermute | solution.py:97
  23.6 6.1 %all-to-all-done = bf16[16,4,768]{2,1,0:T(4,128)(2,1)S(1)} async-done(((bf16[16,4,768]{2,1,0:T(4,128)(2,1)}), bf16[16,4,768]{2,1,0:T(4,128)(2,1)S(1)}, u32[]{:S(2)}, u32[]{:S(2)}) %all-to-all-start) | async-done | bytes 98336 | tf_op jit(solution)/shard_map/all_to_all | solution.py:87
  29.9 0.1 copy.82
  30.0 0.2 fusion.31
  30.3 0.4 fusion.30
  30.7 0.2 convert_reduce_fusion.1
  31.1 0.2 fusion.16
  31.3 0.3 fusion.1
  31.6 0.7 fusion.7
  32.3 7.0 %all-to-all-start.1 = ((bf16[16,16,256]{2,1,0:T(8,128)(2,1)}), bf16[16,16,256]{2,1,0:T(8,128)(2,1)S(1)}, u32[]{:S(2)}, u32[]{:S(2)}) async-start(bf16[16,16,256]{2,1,0:T(8,128)(2,1)} %fusion.7), calls=%async_computation.1 | async-start | bytes 262144 | tf_op jit(solution)/shard_map/all_to_all | solution.py:87
  39.4 5.3 %collective-permute-start.2 = (bf16[2,2,16,288]{3,2,1,0:T(8,128)(2,1)S(1)}, bf16[2,2,16,288]{3,2,1,0:T(8,128)(2,1)S(1)}, u32[]{:S(2)}, u32[]{:S(2)}) collective-permute-start(bf16[2,2,16,288]{3,2,1,0:T(8,128)(2,1)S(1)} %maximum_select_fusion.2), channel_id=1, source_target_pairs={{0,256},{128,384},{256,0},{384,128},{1,257},{129,385},{257,1},{385... | collective-permute-start | bytes 110600 | tf_op jit(solution)/shard_map/ppermute | solution.py:103
  44.8 2.6 %all-to-all-done.1 = bf16[16,16,256]{2,1,0:T(8,128)(2,1)S(1)} async-done(((bf16[16,16,256]{2,1,0:T(8,128)(2,1)}), bf16[16,16,256]{2,1,0:T(8,128)(2,1)S(1)}, u32[]{:S(2)}, u32[]{:S(2)}) %all-to-all-start.1) | async-done | bytes 131104 | tf_op jit(solution)/shard_map/all_to_all | solution.py:87
  47.4 0.1 multiply_reduce_fusion
  47.7 0.7 copy.89
  48.3 8.7 %all-to-all-start.2 = ((bf16[128,1,96]{2,1,0:T(2,128)(2,1)}), bf16[128,1,96]{2,1,0:T(2,128)(2,1)S(1)}, u32[]{:S(2)}, u32[]{:S(2)}) async-start(bf16[128,1,96]{2,1,0:T(2,128)(2,1)} %copy.89), calls=%async_computation.2 | async-start | bytes 131072 | tf_op jit(solution)/shard_map/all_to_all | solution.py:87
  57.1 2.9 %shard_map.91.more_ref = f32[4608,128]{1,0:T(8,128)S(1)} custom-call(bf16[4,32,288]{2,1,0:T(8,128)(2,1)S(1)} %maximum_select_fusion.h_ref, bf16[288,4608]{1,0:T(8,128)(2,1)} %w_hbm.1), custom_call_target="tpu_custom_call" | custom-call | flops 339738624 | bytes 5013504 | tf_op jit(solution)/shard_map/pallas_call | solution.py:39
  60.0 11.6 %all-to-all-done.2 = bf16[128,1,96]{2,1,0:T(2,128)(2,1)S(1)} async-done(((bf16[128,1,96]{2,1,0:T(2,128)(2,1)}), bf16[128,1,96]{2,1,0:T(2,128)(2,1)S(1)}, u32[]{:S(2)}, u32[]{:S(2)}) %all-to-all-start.2) | async-done | bytes 24608 | tf_op jit(solution)/shard_map/all_to_all | solution.py:87
  71.7 0.9 shard_map.93
  72.6 2.2 %collective-permute-start.3 = (bf16[2304,128]{1,0:T(8,128)(2,1)S(1)}, bf16[2304,128]{1,0:T(8,128)(2,1)S(1)}, u32[]{:S(2)}, u32[]{:S(2)}) collective-permute-start(bf16[2304,128]{1,0:T(8,128)(2,1)S(1)} %shard_map.93), channel_id=1, source_target_pairs={{0,16},{16,0},{1,17},{17,1},{2,18},{18,2},{3,19},{19,3},{4,20},{20... | collective-permute-start | bytes 1769480 | tf_op jit(solution)/shard_map/ppermute | solution.py:148
  74.8 0.9 shard_map.92
  75.7 0.8 collective-permute-done.3
  76.5 0.1 add_convert_fusion
  76.6 13.3 %all_to_all.25 = bf16[4,576,128]{2,1,0:T(8,128)(2,1)S(1)} all-to-all(bf16[4,576,128]{2,1,0:T(8,128)(2,1)S(1)} %bitcast.44), channel_id=1, replica_groups=mesh['gx'=4,'gyx'=4,'core'=2,'gz'=16] {'gyx'}, dimensions={0} | all-to-all | bytes 1179648 | tf_op jit(solution)/shard_map/all_to_all | solution.py:87
  89.9 0.1 reduce_sum.61
  90.0 18.0 %all_to_all.26 = bf16[16,9,4,128]{3,2,1,0:T(4,128)(2,1)S(1)} all-to-all(bf16[16,9,4,128]{3,2,1,0:T(4,128)(2,1)S(1)} %bitcast.45), channel_id=1, replica_groups=mesh['gx'=4,'gyx'=4,'core'=2,'gz'=16] {'gz'}, dimensions={0} | all-to-all | bytes 294912 | tf_op jit(solution)/shard_map/all_to_all | solution.py:87
  108.1 0.1 reshape.213
  108.2 0.6 fusion.10
  (50 shorter events, 1.0 us)
Async XLA Ops:
  0.0 0.9 copy-start
  0.0 17.9 %copy-start.4 = (bf16[2,16,288]{2,1,0:T(8,128)(2,1)S(1)}, bf16[2,16,288]{2,1,0:T(8,128)(2,1)}, u32[]{:S(2)}) copy-start(bf16[2,16,288]{2,1,0:T(8,128)(2,1)} %param.16) | copy-start | bytes 55300
  0.0 23.5 %copy-start.7 = (s32[4]{0:T(128)S(1)}, s32[4]{0:T(128)}, u32[]{:S(2)}) copy-start(s32[4]{0:T(128)} %param.14) | copy-start | bytes 52
  0.0 23.6 %copy-start.6 = (bf16[2,4,512]{2,1,0:T(4,128)(2,1)S(1)}, bf16[2,4,512]{2,1,0:T(4,128)(2,1)}, u32[]{:S(2)}) copy-start(bf16[2,4,512]{2,1,0:T(4,128)(2,1)} %param.11) | copy-start | bytes 24580
  1.6 28.2 %all-to-all-start = ((bf16[16,4,768]{2,1,0:T(4,128)(2,1)}), bf16[16,4,768]{2,1,0:T(4,128)(2,1)S(1)}, u32[]{:S(2)}, u32[]{:S(2)}) async-start(bf16[16,4,768]{2,1,0:T(4,128)(2,1)} %reshape.202), calls=%async_computation | async-start | bytes 196608 | tf_op jit(solution)/shard_map/all_to_all | solution.py:87
  17.9 12.3 %copy-start.2 = (bf16[4,128,256]{2,1,0:T(8,128)(2,1)S(1)}, bf16[4,128,256]{2,1,0:T(8,128)(2,1)}, u32[]{:S(2)}) copy-start(bf16[4,128,256]{2,1,0:T(8,128)(2,1)} %param.12) | copy-start | bytes 786436
  17.9 12.4 %collective-permute-start.1 = (bf16[2,16,288]{2,1,0:T(8,128)(2,1)S(1)}, bf16[2,16,288]{2,1,0:T(8,128)(2,1)S(1)}, u32[]{:S(2)}, u32[]{:S(2)}) collective-permute-start(bf16[2,16,288]{2,1,0:T(8,128)(2,1)S(1)} %copy-done.4), channel_id=1, source_target_pairs={{0,128},{128,0},{256,384},{384,256},{1,129},{129,1},{257,385},{385... | collective-permute-start | bytes 55304 | tf_op jit(solution)/shard_map/ppermute | solution.py:98
  21.5 8.6 %collective-permute-start = (bf16[4,128,512]{2,1,0:T(8,128)(2,1)S(1)}, bf16[4,128,512]{2,1,0:T(8,128)(2,1)S(1)}, u32[]{:S(2)}, u32[]{:S(2)}) collective-permute-start(bf16[4,128,512]{2,1,0:T(8,128)(2,1)S(1)} %pad_maximum_fusion), channel_id=1, source_target_pairs={{0,16},{16,0},{1,17},{17,1},{2,18},{18,2},{3,19},{19,3},{4,20},{20... | collective-permute-start | bytes 1572872 | tf_op jit(solution)/shard_map/ppermute | solution.py:97
  30.2 1.2 %copy-start.3 = (bf16[4,128,256]{2,1,0:T(8,128)(2,1)S(1)}, bf16[4,128,256]{2,1,0:T(8,128)(2,1)}, u32[]{:S(2)}) copy-start(bf16[4,128,256]{2,1,0:T(8,128)(2,1)} %param.13) | copy-start | bytes 786436
  32.3 15.0 %all-to-all-start.1 = ((bf16[16,16,256]{2,1,0:T(8,128)(2,1)}), bf16[16,16,256]{2,1,0:T(8,128)(2,1)S(1)}, u32[]{:S(2)}, u32[]{:S(2)}) async-start(bf16[16,16,256]{2,1,0:T(8,128)(2,1)} %fusion.7), calls=%async_computation.1 | async-start | bytes 262144 | tf_op jit(solution)/shard_map/all_to_all | solution.py:87
  39.4 17.7 %collective-permute-start.2 = (bf16[2,2,16,288]{3,2,1,0:T(8,128)(2,1)S(1)}, bf16[2,2,16,288]{3,2,1,0:T(8,128)(2,1)S(1)}, u32[]{:S(2)}, u32[]{:S(2)}) collective-permute-start(bf16[2,2,16,288]{3,2,1,0:T(8,128)(2,1)S(1)} %maximum_select_fusion.2), channel_id=1, source_target_pairs={{0,256},{128,384},{256,0},{384,128},{1,257},{129,385},{257,1},{385... | collective-permute-start | bytes 110600 | tf_op jit(solution)/shard_map/ppermute | solution.py:103
  48.3 23.3 %all-to-all-start.2 = ((bf16[128,1,96]{2,1,0:T(2,128)(2,1)}), bf16[128,1,96]{2,1,0:T(2,128)(2,1)S(1)}, u32[]{:S(2)}, u32[]{:S(2)}) async-start(bf16[128,1,96]{2,1,0:T(2,128)(2,1)} %copy.89), calls=%async_computation.2 | async-start | bytes 131072 | tf_op jit(solution)/shard_map/all_to_all | solution.py:87
  57.1 14.6 %copy-start.1 = (bf16[96,4608]{1,0:T(8,128)(2,1)S(1)}, bf16[96,4608]{1,0:T(8,128)(2,1)}, u32[]{:S(2)}) copy-start(bf16[96,4608]{1,0:T(8,128)(2,1)} %w_ref.3) | copy-start | bytes 2654212
  72.6 3.9 %collective-permute-start.3 = (bf16[2304,128]{1,0:T(8,128)(2,1)S(1)}, bf16[2304,128]{1,0:T(8,128)(2,1)S(1)}, u32[]{:S(2)}, u32[]{:S(2)}) collective-permute-start(bf16[2304,128]{1,0:T(8,128)(2,1)S(1)} %shard_map.93), channel_id=1, source_target_pairs={{0,16},{16,0},{1,17},{17,1},{2,18},{18,2},{3,19},{19,3},{4,20},{20... | collective-permute-start | bytes 1769480 | tf_op jit(solution)/shard_map/ppermute | solution.py:148
  76.6 31.5 %copy-start.5 = (bf16[2,64,36]{1,0,2:T(2,128)(2,1)S(1)}, bf16[2,64,36]{1,0,2:T(2,128)(2,1)}, u32[]{:S(2)}) copy-start(bf16[2,64,36]{1,0,2:T(2,128)(2,1)} %param.9) | copy-start | bytes 27652
